TPU v7x, 32 devices: a whole 2x2x4 slice. The times are simulated.
32 devices in a mesh: nodes: 8 (over y, x, core), cols: 4 (over z).
Axes of the slice: x: 2, y: 2, z: 4, core: 2. Of those that a mesh axis runs over, the one named last changes fastest.
Arguments:
- features: float32 [4, 2048, 100], P('cols', 'nodes'), may hold values from -6 to 6
- adjacency: int32 [4, 2048, 2048], P('cols', 'nodes'), may hold values from 0 to 1, as said below
- node_mask: int32 [4, 2048], P('cols', 'nodes'), may hold values from 0 to 1
- labels: int32 [4, 2048], P('cols', 'nodes'), may hold values from 0 to 46
- label_mask: int32 [4, 2048], P('cols', 'nodes'), may hold values 0 or 1
- weight_first: float32 [200, 256], P(None, 'cols'), may hold values from -0.4375 to 0.4375
- weight_rest: float32 [2, 512, 256], P(None, None, 'cols'), may hold values from -0.25 to 0.25
- norm_params: float32 [2, 3, 256], replicated, may hold values from -3 to 4
- weight_head: float32 [256, 47], replicated, may hold values from -0.375 to 0.375
- bias_head: float32 [47], replicated, may hold values from -3 to 3
- moment_first: float32 [200, 256], P(None, 'cols'), may hold values from -1.5258789e-05 to 1.5258789e-05
- moment_rest: float32 [2, 512, 256], P(None, None, 'cols'), may hold values from -1.5258789e-05 to 1.5258789e-05
- moment_norm: float32 [2, 3, 256], replicated, may hold values from -5.340576e-05 to 5.340576e-05
- moment_head: float32 [256, 47], replicated, may hold values from -1.5258789e-05 to 1.5258789e-05
- moment_bias: float32 [47], replicated, may hold values from -5.340576e-05 to 5.340576e-05
- square_first: float32 [200, 256], P(None, 'cols'), may hold values from 6.789984e-13 to 2.7159937e-12
- square_rest: float32 [2, 512, 256], P(None, None, 'cols'), may hold values from 6.789984e-13 to 2.7159937e-12
- square_norm: float32 [2, 3, 256], replicated, may hold values from 6.789984e-12 to 2.7159936e-11
- square_head: float32 [256, 47], replicated, may hold values from 6.789984e-13 to 2.7159937e-12
- square_bias: float32 [47], replicated, may hold values from 6.789984e-12 to 2.7159936e-11
- average_first: float32 [200, 256], P(None, 'cols'), may hold values from -0.4375 to 0.4375
- average_rest: float32 [2, 512, 256], P(None, None, 'cols'), may hold values from -0.25 to 0.25
- average_norm: float32 [2, 3, 256], replicated, may hold values from -0.5 to 1.5
- average_head: float32 [256, 47], replicated, may hold values from -0.375 to 0.375
- average_bias: float32 [47], replicated, may hold values from -3 to 3
Outputs:
- loss_total: float32 [], replicated
- label_count: float32 [], replicated
- gradient_norm: float32 [], replicated
- momentum_first: float32 [200, 256], P(None, 'cols')
- variance_first: float32 [200, 256], P(None, 'cols')
- trained_first: float32 [200, 256], P(None, 'cols')
- averaged_first: float32 [200, 256], P(None, 'cols')
- momentum_rest: float32 [2, 512, 256], P(None, None, 'cols')
- variance_rest: float32 [2, 512, 256], P(None, None, 'cols')
- trained_rest: float32 [2, 512, 256], P(None, None, 'cols')
- averaged_rest: float32 [2, 512, 256], P(None, None, 'cols')
- momentum_norm: float32 [2, 3, 256], replicated
- variance_norm: float32 [2, 3, 256], replicated
- trained_norm: float32 [2, 3, 256], replicated
- averaged_norm: float32 [2, 3, 256], replicated
- momentum_head: float32 [256, 47], replicated
- variance_head: float32 [256, 47], replicated
- trained_head: float32 [256, 47], replicated
- averaged_head: float32 [256, 47], replicated
- momentum_bias: float32 [47], replicated
- variance_bias: float32 [47], replicated
- trained_bias: float32 [47], replicated
- averaged_bias: float32 [47], replicated
Inputs may be any that keep to these rules, and one draw needn't show every extreme that they name: adjacency[s, i, j] is 1 only where both nodes are real (node_mask 1).
All inputs are finite; a program needn't handle non-finite values. No bound on the sum of `label_mask` on one device may be relied on, other than what follows from the above.
Results may differ from a plain program's by a relative error of at most 0.0003.
Values sent between devices are 32-bit elements; how exact they have to be, the bound alone decides.
A program may use at most 128 MiB of HBM per device.

v0:
```python
import jax
import jax.numpy as jnp
from jax import lax
from jax.sharding import PartitionSpec as P

LAYERS = 3
ADAM_STEP = 10


HIGH = lax.Precision.HIGHEST
CLIP = 0.02
RATE_MATRIX = 0.03
RATE_SMALL = 0.3
BETA_ONE = 0.9
BETA_TWO = 0.999
ADAM_EPS = 1e-08
DECAY = 0.01
AVERAGE = 0.9
NORM_EPS = 1e-05


def matmul(left, right):
    return jnp.dot(left, right, precision=HIGH)


def aggregate(hidden, adj_rows, degree):
    total = matmul(adj_rows, lax.all_gather(hidden, "nodes", axis=0, tiled=True))
    return total / degree


def layer_forward(hidden, adj_rows, degree, weight, gain, shift, valid):
    inputs = jnp.concatenate([hidden, aggregate(hidden, adj_rows, degree)], axis=1)
    stored = lax.all_gather(inputs, "cols", axis=0, tiled=True)
    linear = lax.all_to_all(matmul(stored, weight), "cols", split_axis=0, concat_axis=1, tiled=True)
    active = jax.nn.gelu(linear)
    first, second, total = lax.psum(
        (jnp.sum(valid * active, 0), jnp.sum(valid * active * active, 0), jnp.sum(valid)),
        ("nodes", "cols"),
    )
    mean = first / total
    var = second / total - mean * mean
    inverse = lax.rsqrt(var + NORM_EPS)
    normed = (active - mean) * inverse
    return (gain * normed + shift, (stored, linear, normed, inverse, total))


def layer_backward(grad_out, kept, adj_rows, degree, weight, gain, valid, need_input):
    stored, linear, normed, inverse, total = kept
    grad_gain, grad_shift = lax.psum(
        (jnp.sum(grad_out * normed, 0), jnp.sum(grad_out, 0)), ("nodes", "cols")
    )
    grad_normed = grad_out * gain
    grad_active = inverse * (
        grad_normed - valid * (gain * grad_shift + normed * gain * grad_gain) / total
    )
    unused, active_back = jax.vjp(jax.nn.gelu, linear)
    grad_linear = active_back(grad_active)[0]
    grad_inputs = None
    grad_cols = lax.all_to_all(grad_linear, "cols", split_axis=1, concat_axis=0, tiled=True)
    grad_weight = matmul(stored.T, grad_cols)
    if need_input:
        grad_inputs = lax.psum_scatter(
            matmul(grad_cols, weight.T), "cols", scatter_dimension=0, tiled=True
        )
    grad_hidden = None
    if need_input:
        width = weight.shape[0] // 2
        spread = grad_inputs[:, width:] / degree
        grad_hidden = grad_inputs[:, :width] + lax.psum_scatter(
            matmul(adj_rows.T, spread), "nodes", scatter_dimension=0, tiled=True
        )
    return (grad_hidden, grad_weight, grad_gain, grad_shift)


def adamw(weight, first, second, average, grad, rate):
    first = BETA_ONE * first + (1.0 - BETA_ONE) * grad
    second = BETA_TWO * second + (1.0 - BETA_TWO) * grad * grad
    fix_one = 1.0 - BETA_ONE**ADAM_STEP
    fix_two = 1.0 - BETA_TWO**ADAM_STEP
    update = first / fix_one / (jnp.sqrt(second / fix_two) + ADAM_EPS)
    weight = weight - rate * (update + DECAY * weight)
    average = AVERAGE * average + (1.0 - AVERAGE) * weight
    return (first, second, weight, average)


def local(
    features,
    adjacency,
    node_mask,
    labels,
    label_mask,
    weight_first,
    weight_rest,
    norm_params,
    weight_head,
    bias_head,
    moment_first,
    moment_rest,
    moment_norm,
    moment_head,
    moment_bias,
    square_first,
    square_rest,
    square_norm,
    square_head,
    square_bias,
    average_first,
    average_rest,
    average_norm,
    average_head,
    average_bias,
):
    adj_rows = adjacency[0].astype(jnp.float32)
    degree = jnp.maximum(jnp.sum(adjacency[0], axis=1), 1).astype(jnp.float32)[:, None]
    valid = node_mask[0].astype(jnp.float32)[:, None]
    counted = (label_mask[0] * node_mask[0]).astype(jnp.float32)[:, None]
    first_used, rest_used = (weight_first, weight_rest)
    layer_weights = [first_used] + [rest_used[index] for index in range(LAYERS - 1)]
    hidden = features[0]
    kept_all = []
    for layer in range(LAYERS):
        hidden, kept = layer_forward(
            hidden,
            adj_rows,
            degree,
            layer_weights[layer],
            norm_params[0, layer],
            norm_params[1, layer],
            valid,
        )
        kept_all.append(kept)
    logits = matmul(hidden, weight_head) + bias_head
    logp = jax.nn.log_softmax(logits, axis=-1)
    onehot = (
        labels[0][:, None] == jnp.arange(weight_head.shape[1], dtype=jnp.int32)[None, :]
    ).astype(jnp.float32)
    loss_part = -jnp.sum(counted * jnp.sum(onehot * logp, axis=-1, keepdims=True))
    loss_total, label_count = lax.psum((loss_part, jnp.sum(counted)), ("nodes", "cols"))
    grad_logits = counted * (jnp.exp(logp) - onehot) / label_count
    grad_hidden = matmul(grad_logits, weight_head.T)
    grad_weights = [None] * LAYERS
    grad_gains = [None] * LAYERS
    grad_shifts = [None] * LAYERS
    for layer in reversed(range(LAYERS)):
        grad_hidden, grad_weights[layer], grad_gains[layer], grad_shifts[layer] = layer_backward(
            grad_hidden,
            kept_all[layer],
            adj_rows,
            degree,
            layer_weights[layer],
            norm_params[0, layer],
            valid,
            layer > 0,
        )
    grad_first = grad_weights[0]
    grad_rest = jnp.stack(grad_weights[1:])
    grad_first, grad_rest = lax.psum((grad_first, grad_rest), "nodes")
    grad_head, grad_bias = lax.psum(
        (matmul(hidden.T, grad_logits), jnp.sum(grad_logits, 0)), ("nodes", "cols")
    )
    grad_norm_params = jnp.stack([jnp.stack(grad_gains), jnp.stack(grad_shifts)])
    shard_squares = lax.psum(
        jnp.sum(grad_first * grad_first) + jnp.sum(grad_rest * grad_rest), "cols"
    )
    local_squares = (
        jnp.sum(grad_norm_params * grad_norm_params)
        + jnp.sum(grad_head * grad_head)
        + jnp.sum(grad_bias * grad_bias)
    )
    gradient_norm = jnp.sqrt(shard_squares + local_squares)
    scale = CLIP / jnp.maximum(gradient_norm, CLIP)
    first_out = adamw(
        weight_first, moment_first, square_first, average_first, grad_first * scale, RATE_MATRIX
    )
    rest_out = adamw(
        weight_rest, moment_rest, square_rest, average_rest, grad_rest * scale, RATE_MATRIX
    )
    norm_out = adamw(
        norm_params, moment_norm, square_norm, average_norm, grad_norm_params * scale, RATE_SMALL
    )
    head_out = adamw(
        weight_head, moment_head, square_head, average_head, grad_head * scale, RATE_MATRIX
    )
    bias_out = adamw(
        bias_head, moment_bias, square_bias, average_bias, grad_bias * scale, RATE_SMALL
    )
    return (
        loss_total,
        label_count,
        gradient_norm,
        first_out[0],
        first_out[1],
        first_out[2],
        first_out[3],
        rest_out[0],
        rest_out[1],
        rest_out[2],
        rest_out[3],
        norm_out[0],
        norm_out[1],
        norm_out[2],
        norm_out[3],
        head_out[0],
        head_out[1],
        head_out[2],
        head_out[3],
        bias_out[0],
        bias_out[1],
        bias_out[2],
        bias_out[3],
    )


def solution(mesh):
    placed = (
        P("cols", "nodes", None),
        P("cols", "nodes", None),
        P("cols", "nodes"),
        P("cols", "nodes"),
        P("cols", "nodes"),
        P(None, "cols"),
        P(None, None, "cols"),
        P(),
        P(),
        P(),
        P(None, "cols"),
        P(None, None, "cols"),
        P(),
        P(),
        P(),
        P(None, "cols"),
        P(None, None, "cols"),
        P(),
        P(),
        P(),
        P(None, "cols"),
        P(None, None, "cols"),
        P(),
        P(),
        P(),
    )
    return jax.shard_map(
        local,
        mesh=mesh,
        in_specs=placed,
        out_specs=(
            P(),
            P(),
            P(),
            P(None, "cols"),
            P(None, "cols"),
            P(None, "cols"),
            P(None, "cols"),
            P(None, None, "cols"),
            P(None, None, "cols"),
            P(None, None, "cols"),
            P(None, None, "cols"),
            P(),
            P(),
            P(),
            P(),
            P(),
            P(),
            P(),
            P(),
            P(),
            P(),
            P(),
            P(),
        ),
        check_vma=False,
    )
```

profile of v0, /device:TPU:0, one launch (start us, length us, event | category | flops | bytes accessed | tf_op | source)
XLA Modules:
  0.0 791.8 jit_solution(10530752797901459968)
XLA Ops:
  7.2 1.1 copy.124
  8.3 15.1 %all-gather = f32[1,2048,100]{1,0,2:T(1,128)S(1)} all-gather(f32[1,256,100]{1,0,2:T(1,128)} %param.25), channel_id=2, replica_groups=mesh['nodes'=8,'cols'=4] {'nodes'}, dimensions={1}, use_global_device_ids=true | all-gather | bytes 921600 | tf_op jit(solution)/shard_map/all_gather | solution.py:27
  23.4 1.8 reduce_sum.237
  25.2 2.1 fusion.25
  27.4 20.2 %all_gather.19 = f32[1024,200]{0,1:T(8,128)S(1)} all-gather(f32[256,200]{0,1:T(8,128)S(1)} %pad_maximum_fusion.3), channel_id=1, replica_groups=mesh['nodes'=8,'cols'=4] {'cols'}, dimensions={0}, use_global_device_ids=true | all-gather | bytes 1024000 | tf_op jit(solution)/shard_map/all_gather | solution.py:33
  48.3 0.7 copy.123
  49.0 3.4 all-to-all-start
  52.5 1.2 fusion.127
  54.2 6.6 all-to-all-done
  61.2 38.1 %all-reduce.5 = (f32[256]{0:T(256)S(1)}, f32[]{:T(128)}, f32[256]{0:T(256)S(1)}) all-reduce(f32[256]{0:T(256)S(1)} %reduce_sum.239, f32[]{:T(128)} %get-tuple-element.134, f32[256]{0:T(256)S(1)} %reduce_sum.242), channel_id=1, replica_groups=mesh['nodes'=8,'cols'=4] {'nodes','cols'}, use_global_device_ids=true, to_apply=%region_2.0 | all-reduce | flops 513 | bytes 4104 | tf_op jit(solution)/shard_map/psum | solution.py:36
  100.0 0.9 multiply_add_fusion.3
  101.0 27.9 %all-gather.6.cloned.1.call-done = f32[2048,256]{0,1:T(8,128)} async-done(((f32[256,256]{0,1:T(8,128)}), f32[2048,256]{0,1:T(8,128)}) %all-gather.6.cloned.1.call-update) | async-done | bytes 2097168 | tf_op jit(solution)/shard_map/all_gather | solution.py:27
  128.8 3.5 fusion.16
  132.4 0.8 pad_maximum_fusion
  133.3 46.0 %all-gather.8.cloned.1.call-done = f32[1024,512]{0,1:T(8,128)} async-done(((f32[256,512]{0,1:T(8,128)}), f32[1024,512]{0,1:T(8,128)}) %all-gather.8.cloned.1.call-update) | async-done | bytes 2097168 | tf_op jit(solution)/shard_map/all_gather | solution.py:33
  179.3 2.9 copy.89
  182.2 3.7 fusion.94
  185.9 11.5 %all_to_all.108 = f32[4,256,64]{1,2,0:T(8,128)S(1)} all-to-all(f32[4,256,64]{1,2,0:T(8,128)S(1)} %fusion.94), channel_id=1, replica_groups=mesh['nodes'=8,'cols'=4] {'cols'}, dimensions={0} | all-to-all | bytes 524288 | tf_op jit(solution)/shard_map/all_to_all | solution.py:34
  197.8 38.8 %all-reduce.4 = (f32[256]{0:T(256)S(1)}, f32[256]{0:T(256)S(1)}) all-reduce(f32[256]{0:T(256)S(1)} %reduce_sum.244, f32[256]{0:T(256)S(1)} %reduce_sum.246), channel_id=1, replica_groups=mesh['nodes'=8,'cols'=4] {'nodes','cols'}, use_global_device_ids=true, to_apply=%region_8.0 | all-reduce | flops 512 | bytes 4096 | tf_op jit(solution)/shard_map/psum | solution.py:36
  237.3 0.9 multiply_add_fusion.2
  238.3 27.7 %all-gather.10.cloned.1.call-done = f32[2048,256]{0,1:T(8,128)} async-done(((f32[256,256]{0,1:T(8,128)}), f32[2048,256]{0,1:T(8,128)}) %all-gather.10.cloned.1.call-update) | async-done | bytes 2097168 | tf_op jit(solution)/shard_map/all_gather | solution.py:27
  265.9 3.5 fusion.22
  269.5 0.8 pad_maximum_fusion.1
  270.6 45.8 %all-gather.12.cloned.1.call-done = f32[1024,512]{0,1:T(8,128)} async-done(((f32[256,512]{0,1:T(8,128)}), f32[1024,512]{0,1:T(8,128)}) %all-gather.12.cloned.1.call-update) | async-done | bytes 2097168 | tf_op jit(solution)/shard_map/all_gather | solution.py:33
  316.4 2.9 copy.90
  319.3 3.7 fusion.90
  323.1 11.5 %all_to_all.109 = f32[4,256,64]{1,2,0:T(8,128)S(1)} all-to-all(f32[4,256,64]{1,2,0:T(8,128)S(1)} %fusion.90), channel_id=1, replica_groups=mesh['nodes'=8,'cols'=4] {'cols'}, dimensions={0} | all-to-all | bytes 524288 | tf_op jit(solution)/shard_map/all_to_all | solution.py:34
  335.6 39.1 %all-reduce.3 = (f32[]{:T(128)}, f32[256]{0:T(256)S(1)}, f32[256]{0:T(256)S(1)}) all-reduce(f32[]{:T(128)} %get-tuple-element.126, f32[256]{0:T(256)S(1)} %reduce_sum.248, f32[256]{0:T(256)S(1)} %reduce_sum.250), channel_id=1, replica_groups=mesh['nodes'=8,'cols'=4] {'nodes','cols'}, use_global_device_ids=true, to_apply=%region_21.22 | all-reduce | flops 513 | bytes 4104 | tf_op jit(solution)/shard_map/psum | solution.py:138
  375.4 1.1 fusion.76
  377.2 1.2 fusion.129
  379.0 3.3 fusion.120
  382.3 40.8 %all-reduce.2 = (f32[256]{0:T(256)}, f32[256]{0:T(256)}) all-reduce(f32[256]{0:T(256)} %get-tuple-element.80, f32[256]{0:T(256)} %get-tuple-element.79), channel_id=1, replica_groups=mesh['nodes'=8,'cols'=4] {'nodes','cols'}, use_global_device_ids=true, to_apply=%region_25.26 | all-reduce | flops 512 | bytes 4096 | tf_op jit(solution)/shard_map/psum | solution.py:49
  423.8 2.0 fusion.49
  425.8 11.0 %all_to_all.110 = f32[256,4,64]{0,2,1:T(8,128)S(1)} all-to-all(f32[256,4,64]{0,2,1:T(8,128)S(1)} %bitcast.208), channel_id=1, replica_groups=mesh['nodes'=8,'cols'=4] {'cols'}, dimensions={1} | all-to-all | bytes 524288 | tf_op jit(solution)/shard_map/all_to_all | solution.py:59
  437.5 4.1 fusion.92
  441.7 43.0 %reduce-scatter.5.cloned.1.call-done = f32[256,512]{0,1:T(8,128)} async-done(((f32[1024,512]{0,1:T(8,128)}), f32[256,512]{0,1:T(8,128)}) %reduce-scatter.5.cloned.1.call-update) | async-done | bytes 524304 | tf_op jit(solution)/shard_map/reduce_scatter | solution.py:62
  484.6 4.1 convolution_bitcast_fusion.1
  488.9 40.7 %reduce-scatter.7.cloned.1.call-done = f32[256,256]{0,1:T(8,128)} async-done(((f32[2048,256]{0,1:T(8,128)}), f32[256,256]{0,1:T(8,128)}) %reduce-scatter.7.cloned.1.call-update) | async-done | bytes 262160 | tf_op jit(solution)/shard_map/reduce_scatter | solution.py:69
  529.5 1.8 fusion.118
  531.3 39.6 %all-reduce.1 = (f32[256]{0:T(256)}, f32[256]{0:T(256)}) all-reduce(f32[256]{0:T(256)} %get-tuple-element.72, f32[256]{0:T(256)} %get-tuple-element.71), channel_id=1, replica_groups=mesh['nodes'=8,'cols'=4] {'nodes','cols'}, use_global_device_ids=true, to_apply=%region_31.32 | all-reduce | flops 512 | bytes 4096 | tf_op jit(solution)/shard_map/psum | solution.py:49
  571.0 0.7 mul.744
  571.7 2.0 fusion.42
  573.7 11.6 %all_to_all.111 = f32[256,4,64]{0,2,1:T(8,128)S(1)} all-to-all(f32[256,4,64]{0,2,1:T(8,128)S(1)} %bitcast.207), channel_id=1, replica_groups=mesh['nodes'=8,'cols'=4] {'cols'}, dimensions={1} | all-to-all | bytes 524288 | tf_op jit(solution)/shard_map/all_to_all | solution.py:59
  586.1 3.2 fusion.96
  589.3 43.1 %reduce-scatter.9.cloned.1.call-done = f32[256,512]{0,1:T(8,128)} async-done(((f32[1024,512]{0,1:T(8,128)}), f32[256,512]{0,1:T(8,128)}) %reduce-scatter.9.cloned.1.call-update) | async-done | bytes 524304 | tf_op jit(solution)/shard_map/reduce_scatter | solution.py:62
  632.4 4.1 convolution_bitcast_fusion
  636.6 2.2 fusion.116
  638.8 1.3 multiply_reduce_fusion.10
  640.8 2.7 fusion.85
  643.5 3.8 convolution_bitcast_fusion.2
  647.4 2.2 convolution_bitcast_fusion.3
  649.6 0.7 pad_maximum_fusion.2
  650.4 26.9 %reduce-scatter.11.cloned.1.call-done = f32[256,256]{0,1:T(8,128)} async-done(((f32[2048,256]{0,1:T(8,128)}), f32[256,256]{0,1:T(8,128)}) %reduce-scatter.11.cloned.1.call-update) | async-done | bytes 262160 | tf_op jit(solution)/shard_map/reduce_scatter | solution.py:69
  677.3 1.3 fusion.119
  678.7 39.9 %all-reduce = (f32[]{:T(128)}, f32[256]{0:T(256)S(1)}, f32[256]{0:T(256)S(1)}, f32[256,47]{0,1:T(8,128)S(1)}, f32[47]{0:T(128)S(1)}) all-reduce(f32[]{:T(128)S(6)} %neg.3, f32[256]{0:T(256)S(1)} %get-tuple-element.70, f32[256]{0:T(256)S(1)} %get-tuple-element.69, ...), channel_id=1, replica_groups=mesh['nodes'=8,'cols'=4] {'nodes','cols'}, use_global_device_ids=true, to_apply=%region_19.0 | all-reduce | flops 12592 | bytes 100736 | tf_op jit(solution)/shard_map/psum | solution.py:138
  718.7 2.8 fusion.35
  721.5 3.8 all-to-all-start.5
  725.2 9.3 %all-reduce.8.cloned.1.call-done = f32[2,512,64]{1,2,0:T(8,128)} async-done(((f32[2,512,64]{1,2,0:T(8,128)}), f32[2,512,64]{1,2,0:T(8,128)}) %all-reduce.8.cloned.1.call-update) | async-done | bytes 262160 | tf_op jit(solution)/shard_map/psum | solution.py:157
  734.5 1.7 multiply_reduce_fusion.3
  739.4 0.9 fusion.131
  740.3 22.7 %psum.161 = f32[200,64]{0,1:T(8,128)S(1)} all-reduce(f32[200,64]{0,1:T(8,128)S(1)} %fusion.131), channel_id=1, replica_groups=mesh['nodes'=8,'cols'=4] {'nodes'}, use_global_device_ids=true, to_apply=%region_38.39 | all-reduce | flops 12800 | bytes 102400 | tf_op jit(solution)/shard_map/psum | solution.py:157
  765.5 12.2 %psum.163 = f32[]{:T(128)} all-reduce(f32[]{:T(128)S(6)} %add.314), channel_id=1, replica_groups=mesh['nodes'=8,'cols'=4] {'cols'}, use_global_device_ids=true, to_apply=%region_42.43 | all-reduce | flops 1 | bytes 8 | tf_op jit(solution)/shard_map/psum | solution.py:162
  782.2 0.7 multiply_add_fusion.4
  783.0 1.1 multiply_add_fusion
  (173 shorter events, 15.5 us)
Async XLA Ops:
  7.2 18.0 %copy-start = (s32[1,256,2048]{2,1,0:T(8,128)S(1)}, s32[1,256,2048]{2,1,0:T(8,128)}, u32[]{:S(2)}) copy-start(s32[1,256,2048]{2,1,0:T(8,128)} %param.26) | copy-start | bytes 6291460
  25.2 240.8 %copy-start.28 = (f32[256]{0:T(256)}, f32[256]{0:T(256)S(1)}, u32[]{:S(2)}) copy-start(f32[256]{0:T(256)S(1)} %maximum_convert_fusion) | copy-start | bytes 3076
  25.2 22.4 %copy-start.17 = (f32[200,64]{0,1:T(8,128)S(1)}, f32[200,64]{0,1:T(8,128)}, u32[]{:S(2)}) copy-start(f32[200,64]{0,1:T(8,128)} %param.30) | copy-start | bytes 153604
  27.3 25.1 %copy-start.51 = (s32[1,256]{1,0:T(1,128)S(1)}, s32[1,256]{1,0:T(1,128)}, u32[]{:S(2)}) copy-start(s32[1,256]{1,0:T(1,128)} %param.27) | copy-start | bytes 3076
  27.3 25.1 %copy-start.55 = (s32[1,256]{1,0:T(1,128)S(1)}, s32[1,256]{1,0:T(1,128)}, u32[]{:S(2)}) copy-start(s32[1,256]{1,0:T(1,128)} %param.29) | copy-start | bytes 3076
  27.3 26.3 %copy-start.30 = (f32[2,3,256]{2,0,1:T(2,128)S(1)}, f32[2,3,256]{2,0,1:T(2,128)}, u32[]{:S(2)}) copy-start(f32[2,3,256]{2,0,1:T(2,128)} %param.32) | copy-start | bytes 18436
  49.0 11.8 %all-to-all-start = ((f32[4,256,64]{1,2,0:T(8,128)}), f32[4,256,64]{1,2,0:T(8,128)S(1)}, u32[]{:S(2)}, u32[]{:S(2)}) async-start(f32[4,256,64]{1,2,0:T(8,128)} %bitcast.196), calls=%async_computation | async-start | bytes 524288 | tf_op jit(solution)/shard_map/all_to_all | solution.py:34
  52.4 76.4 %all-gather.6.cloned.1.call-start = ((), (), s32[]{:S(2)}) async-start(), calls=%async_computation.10 | async-start | bytes 2359296 | tf_op jit(solution)/shard_map/all_gather | solution.py:27
  52.5 282.1 %copy-start.22 = (f32[1,256]{1,0:T(1,128)}, f32[1,256]{1,0:T(1,128)S(1)}, u32[]{:S(2)}) copy-start(f32[1,256]{1,0:T(1,128)S(1)} %convert_element_type.53) | copy-start | bytes 3076
  54.2 78.1 %copy-start.38 = (f32[1,1,256]{2,0,1:T(1,128)}, f32[1,1,256]{2,0,1:T(1,128)S(1)}, u32[]{:S(2)}) copy-start(f32[1,1,256]{2,0,1:T(1,128)S(1)} %get-tuple-element.131) | copy-start | bytes 3076
  54.2 183.0 %copy-start.40 = (f32[1,1,256]{2,0,1:T(1,128)}, f32[1,1,256]{2,0,1:T(1,128)S(1)}, u32[]{:S(2)}) copy-start(f32[1,1,256]{2,0,1:T(1,128)S(1)} %get-tuple-element.132) | copy-start | bytes 3076
  100.0 32.4 %copy-start.32 = (f32[256]{0:T(256)}, f32[256]{0:T(256)S(1)}, u32[]{:S(2)}) copy-start(f32[256]{0:T(256)S(1)} %get-tuple-element.124) | copy-start | bytes 3076
  100.0 32.4 %copy-start.34 = (f32[256]{0:T(256)}, f32[256]{0:T(256)S(1)}, u32[]{:S(2)}) copy-start(f32[256]{0:T(256)S(1)} %get-tuple-element.125) | copy-start | bytes 3076
  100.9 31.4 %copy-start.10 = (f32[256,256]{0,1:T(8,128)S(1)}, f32[256,256]{0,1:T(8,128)}, u32[]{:S(2)}) copy-start(f32[256,256]{0,1:T(8,128)} %multiply_add_fusion.3) | copy-start | bytes 786436
  100.9 78.4 %all-gather.8.cloned.1.call-start = ((), (), s32[]{:S(2)}) async-start(), calls=%async_computation.11 | async-start | bytes 2621440 | tf_op jit(solution)/shard_map/all_gather | solution.py:33
  133.2 49.0 %copy-start.3 = (f32[2,512,64]{1,2,0:T(8,128)S(1)}, f32[2,512,64]{1,2,0:T(8,128)}, u32[]{:S(2)}) copy-start(f32[2,512,64]{1,2,0:T(8,128)} %param.31) | copy-start | bytes 786436
  133.2 132.7 %all-gather.10.cloned.1.call-start = ((), (), s32[]{:S(2)}) async-start(), calls=%async_computation.12 | async-start | bytes 2359296 | tf_op jit(solution)/shard_map/all_gather | solution.py:27
  237.2 32.2 %copy-start.36 = (f32[256]{0:T(256)}, f32[256]{0:T(256)S(1)}, u32[]{:S(2)}) copy-start(f32[256]{0:T(256)S(1)} %get-tuple-element.122) | copy-start | bytes 3076
  237.3 32.2 %copy-start.37 = (f32[256]{0:T(256)}, f32[256]{0:T(256)S(1)}, u32[]{:S(2)}) copy-start(f32[256]{0:T(256)S(1)} %get-tuple-element.123) | copy-start | bytes 3076
  238.2 78.2 %all-gather.12.cloned.1.call-start = ((), (), s32[]{:S(2)}) async-start(), calls=%async_computation.13 | async-start | bytes 2621440 | tf_op jit(solution)/shard_map/all_gather | solution.py:33
  270.4 214.3 %reduce-scatter.5.cloned.1.call-start = ((), (), s32[]{:S(2)}) async-start(), calls=%async_computation.14 | async-start | bytes 2621440 | tf_op jit(solution)/shard_map/reduce_scatter | solution.py:62
  375.4 7.0 copy-start.42
  375.4 6.9 copy-start.43
  378.5 3.9 copy-start.48
  441.6 87.9 %reduce-scatter.7.cloned.1.call-start = ((), (), s32[]{:S(2)}) async-start(), calls=%async_computation.15 | async-start | bytes 2359296 | tf_op jit(solution)/shard_map/reduce_scatter | solution.py:69
  488.8 143.6 %reduce-scatter.9.cloned.1.call-start = ((), (), s32[]{:S(2)}) async-start(), calls=%async_computation.16 | async-start | bytes 2621440 | tf_op jit(solution)/shard_map/reduce_scatter | solution.py:62
  571.0 15.2 %copy-start.4 = (f32[2,512,64]{1,2,0:T(8,128)S(1)}, f32[2,512,64]{1,2,0:T(8,128)}, u32[]{:S(2)}) copy-start(f32[2,512,64]{1,2,0:T(8,128)} %param.31) | copy-start | bytes 786436
  586.1 46.3 %copy-start.29 = (f32[256]{0:T(256)S(1)}, f32[256]{0:T(256)}, u32[]{:S(2)}) copy-start(f32[256]{0:T(256)} %copy-done.28) | copy-start | bytes 3076
  589.3 88.0 %reduce-scatter.11.cloned.1.call-start = ((), (), s32[]{:S(2)}) async-start(), calls=%async_computation.17 | async-start | bytes 2359296 | tf_op jit(solution)/shard_map/reduce_scatter | solution.py:69
  636.6 7.0 copy-start.7
  636.6 10.8 %copy-start.1 = (f32[1024,512]{0,1:T(8,128)S(1)}, f32[1024,512]{0,1:T(8,128)}, u32[]{:S(2)}) copy-start(f32[1024,512]{0,1:T(8,128)} %all-gather.8.cloned.1.call-done) | copy-start | bytes 6291460
  636.6 97.9 %all-reduce.8.cloned.1.call-start = ((), (), s32[]{:S(2)}) async-start(), calls=%async_computation.18 | async-start | bytes 524288 | tf_op jit(solution)/shard_map/psum | solution.py:157
  640.7 6.6 copy-start.9
  647.4 29.9 %copy-start.33 = (f32[256]{0:T(256)S(1)}, f32[256]{0:T(256)}, u32[]{:S(2)}) copy-start(f32[256]{0:T(256)} %copy-done.32) | copy-start | bytes 3076
  647.4 29.9 %copy-start.35 = (f32[256]{0:T(256)S(1)}, f32[256]{0:T(256)}, u32[]{:S(2)}) copy-start(f32[256]{0:T(256)} %copy-done.34) | copy-start | bytes 3076
  647.4 31.3 %copy-start.24 = (f32[256,47]{0,1:T(8,128)S(1)}, f32[256,47]{0,1:T(8,128)}, u32[]{:S(2)}) copy-start(f32[256,47]{0,1:T(8,128)} %fusion.85) | copy-start | bytes 144388
  647.4 31.3 %copy-start.53 = (f32[47]{0:T(128)S(1)}, f32[47]{0:T(128)}, u32[]{:S(2)}) copy-start(f32[47]{0:T(128)} %get-tuple-element.81) | copy-start | bytes 568
  647.4 71.2 %copy-start.39 = (f32[1,1,256]{2,0,1:T(1,128)S(1)}, f32[1,1,256]{2,0,1:T(1,128)}, u32[]{:S(2)}) copy-start(f32[1,1,256]{2,0,1:T(1,128)} %copy-done.38) | copy-start | bytes 3076
  647.4 71.2 %copy-start.23 = (f32[1,256]{1,0:T(1,128)S(1)}, f32[1,256]{1,0:T(1,128)}, u32[]{:S(2)}) copy-start(f32[1,256]{1,0:T(1,128)} %copy-done.22) | copy-start | bytes 3076
  649.6 86.6 %copy-start.47 = (f32[256]{0:T(256)S(1)}, f32[256]{0:T(256)}, u32[]{:S(2)}) copy-start(f32[256]{0:T(256)} %get-tuple-element.90) | copy-start | bytes 3076
  649.6 86.6 %copy-start.49 = (f32[256]{0:T(256)S(1)}, f32[256]{0:T(256)}, u32[]{:S(2)}) copy-start(f32[256]{0:T(256)} %get-tuple-element.91) | copy-start | bytes 3076
  649.6 86.6 %copy-start.50 = (f32[256]{0:T(256)S(1)}, f32[256]{0:T(256)}, u32[]{:S(2)}) copy-start(f32[256]{0:T(256)} %get-tuple-element.89) | copy-start | bytes 3076
  649.6 86.6 %copy-start.52 = (f32[256]{0:T(256)S(1)}, f32[256]{0:T(256)}, u32[]{:S(2)}) copy-start(f32[256]{0:T(256)} %get-tuple-element.88) | copy-start | bytes 3076
  678.6 99.9 %copy-start.31 = (f32[2,3,256]{2,0,1:T(2,128)S(1)}, f32[2,3,256]{2,0,1:T(2,128)}, u32[]{:S(2)}) copy-start(f32[2,3,256]{2,0,1:T(2,128)} %param.32) | copy-start | bytes 18436
  678.6 99.9 %copy-start.44 = (f32[2,3,256]{2,0,1:T(2,128)S(1)}, f32[2,3,256]{2,0,1:T(2,128)}, u32[]{:S(2)}) copy-start(f32[2,3,256]{2,0,1:T(2,128)} %param.47) | copy-start | bytes 18436
  678.6 99.9 %copy-start.45 = (f32[2,3,256]{2,0,1:T(2,128)S(1)}, f32[2,3,256]{2,0,1:T(2,128)}, u32[]{:S(2)}) copy-start(f32[2,3,256]{2,0,1:T(2,128)} %param.42) | copy-start | bytes 18436
  678.6 99.9 %copy-start.46 = (f32[2,3,256]{2,0,1:T(2,128)S(1)}, f32[2,3,256]{2,0,1:T(2,128)}, u32[]{:S(2)}) copy-start(f32[2,3,256]{2,0,1:T(2,128)} %param.37) | copy-start | bytes 18436
  678.6 102.3 %copy-start.54 = (f32[47]{0:T(128)S(1)}, f32[47]{0:T(128)}, u32[]{:S(2)}) copy-start(f32[47]{0:T(128)} %param.34) | copy-start | bytes 568
  678.6 102.3 %copy-start.56 = (f32[47]{0:T(128)S(1)}, f32[47]{0:T(128)}, u32[]{:S(2)}) copy-start(f32[47]{0:T(128)} %param.49) | copy-start | bytes 568
  678.6 102.3 %copy-start.57 = (f32[47]{0:T(128)S(1)}, f32[47]{0:T(128)}, u32[]{:S(2)}) copy-start(f32[47]{0:T(128)} %param.44) | copy-start | bytes 568
  678.6 102.3 %copy-start.58 = (f32[47]{0:T(128)S(1)}, f32[47]{0:T(128)}, u32[]{:S(2)}) copy-start(f32[47]{0:T(128)} %param.39) | copy-start | bytes 568
  678.7 102.8 %copy-start.18 = (f32[256,47]{0,1:T(8,128)S(1)}, f32[256,47]{0,1:T(8,128)}, u32[]{:S(2)}) copy-start(f32[256,47]{0,1:T(8,128)} %param.33) | copy-start | bytes 144388
  678.7 102.8 %copy-start.25 = (f32[256,47]{0,1:T(8,128)S(1)}, f32[256,47]{0,1:T(8,128)}, u32[]{:S(2)}) copy-start(f32[256,47]{0,1:T(8,128)} %param.48) | copy-start | bytes 144388
  678.7 102.8 %copy-start.26 = (f32[256,47]{0,1:T(8,128)S(1)}, f32[256,47]{0,1:T(8,128)}, u32[]{:S(2)}) copy-start(f32[256,47]{0,1:T(8,128)} %param.43) | copy-start | bytes 144388
  678.7 102.8 %copy-start.27 = (f32[256,47]{0,1:T(8,128)S(1)}, f32[256,47]{0,1:T(8,128)}, u32[]{:S(2)}) copy-start(f32[256,47]{0,1:T(8,128)} %param.38) | copy-start | bytes 144388
  718.7 63.6 %copy-start.19 = (f32[200,64]{0,1:T(8,128)S(1)}, f32[200,64]{0,1:T(8,128)}, u32[]{:S(2)}) copy-start(f32[200,64]{0,1:T(8,128)} %param.45) | copy-start | bytes 153604
  718.7 63.6 %copy-start.20 = (f32[200,64]{0,1:T(8,128)S(1)}, f32[200,64]{0,1:T(8,128)}, u32[]{:S(2)}) copy-start(f32[200,64]{0,1:T(8,128)} %param.40) | copy-start | bytes 153604
  718.7 63.5 %copy-start.21 = (f32[200,64]{0,1:T(8,128)S(1)}, f32[200,64]{0,1:T(8,128)}, u32[]{:S(2)}) copy-start(f32[200,64]{0,1:T(8,128)} %param.35) | copy-start | bytes 153604
  721.5 61.5 %copy-start.5 = (f32[2,512,64]{1,2,0:T(8,128)S(1)}, f32[2,512,64]{1,2,0:T(8,128)}, u32[]{:S(2)}) copy-start(f32[2,512,64]{1,2,0:T(8,128)} %param.31) | copy-start | bytes 786436
  721.5 61.5 %copy-start.14 = (f32[2,512,64]{1,2,0:T(8,128)S(1)}, f32[2,512,64]{1,2,0:T(8,128)}, u32[]{:S(2)}) copy-start(f32[2,512,64]{1,2,0:T(8,128)} %param.46) | copy-start | bytes 786436
  721.5 61.5 %copy-start.15 = (f32[2,512,64]{1,2,0:T(8,128)S(1)}, f32[2,512,64]{1,2,0:T(8,128)}, u32[]{:S(2)}) copy-start(f32[2,512,64]{1,2,0:T(8,128)} %param.41) | copy-start | bytes 786436
  721.5 61.5 %copy-start.16 = (f32[2,512,64]{1,2,0:T(8,128)S(1)}, f32[2,512,64]{1,2,0:T(8,128)}, u32[]{:S(2)}) copy-start(f32[2,512,64]{1,2,0:T(8,128)} %param.36) | copy-start | bytes 786436
  721.5 17.9 %all-to-all-start.5 = ((f32[256,4,64]{0,2,1:T(8,128)}), f32[256,4,64]{0,2,1:T(8,128)S(1)}, u32[]{:S(2)}, u32[]{:S(2)}) async-start(f32[256,4,64]{0,2,1:T(8,128)} %bitcast.33), calls=%async_computation.9 | async-start | bytes 524288 | tf_op jit(solution)/shard_map/all_to_all | solution.py:59
  734.5 48.5 %copy-start.12 = (f32[2,512,64]{1,2,0:T(8,128)S(1)}, f32[2,512,64]{1,2,0:T(8,128)}, u32[]{:S(2)}) copy-start(f32[2,512,64]{1,2,0:T(8,128)} %all-reduce.8.cloned.1.call-done) | copy-start | bytes 786436
  (6 other events, 6.9 us)
Sparse Core Ops, SparseCore 0:
  101.0 27.7 all-gather.5
  133.3 45.9 all-gather.7
  238.3 27.5 all-gather.9
  270.5 45.9 all-gather.11
  441.7 42.8 reduce-scatter.4
  488.9 40.5 reduce-scatter.6
  589.4 42.9 reduce-scatter.8
  636.7 40.5 reduce-scatter.10
  680.9 53.5 all-reduce.7
where the time goes:
time: 794 us; the launch traced here: 792 us
  blocking collectives  352 us (44%)
  waiting for transfers between devices  317 us (40%)
  matrix products  46.9 us (6%)
  other arithmetic  32.9 us (4%)
  between operations  20.4 us (3%)
  local copies, waits for them, and re-layouts  14.7 us (2%)
    all_gather x2, waiting for transfers between devices, layer_forward(): stored = lax.all_gather(inputs, 'cols', axis=0, tiled=True)  91.9 us
    reduce_scatter x2, waiting for transfers between devices, layer_backward(): lax.psum_scatter(matmul(grad_cols, weight.T), 'cols', scatter_dimension=0...  86 us
    psum x2, blocking collectives, layer_backward(): lax.psum((jnp.sum(grad_out * normed, 0), jnp.sum(grad_out, 0)), ('nodes',...  80.4 us
    psum x2, blocking collectives, local(): lax.psum((loss_part, jnp.sum(counted)), ('nodes', 'cols'))  79 us
    psum x2, blocking collectives, layer_forward(): lax.psum((jnp.sum(valid * active, 0), jnp.sum(valid * active * active, 0)...  76.9 us
    reduce_scatter x2, waiting for transfers between devices, layer_backward(): lax.psum_scatter(matmul(adj_rows.T, spread), 'nodes', scatter_dimension=0...  67.6 us
    all_gather x2, waiting for transfers between devices, aggregate(): lax.all_gather(hidden, 'nodes', axis=0, tiled=True)  55.5 us
    dot_general x16, matrix products, matmul(): return jnp.dot(left, right, precision=HIGH)  46.9 us
  transfers between devices with their start and end apart: 11, of which 10 were waited for; matrix products, arithmetic and copies ran while one was open for 3% of the time, Pallas kernels for 0%

commit v1 on v0

v1 whole, which is shorter than its diff:
```python
import functools
import types

import jax
import jax.numpy as jnp
from jax import lax
from jax.experimental import pallas as pl
from jax.experimental.pallas import tpu as pltpu
from jax.sharding import PartitionSpec as P

LAYERS = 3
ADAM_STEP = 10
CLIP = 0.02
RATE_MATRIX = 0.03
RATE_SMALL = 0.3
BETA_ONE = 0.9
BETA_TWO = 0.999
ADAM_EPS = 1e-08
DECAY = 0.01
AVERAGE = 0.9
NORM_EPS = 1e-05

MESH = pl.DeviceIdType.MESH
F32 = jnp.float32
BF16 = jnp.bfloat16
LANES = 128
GELU_OUT = 0.7978845608028654
GELU_CUBE = 0.044715


def split(value):
    high = value.astype(BF16)
    return high, (value - high.astype(F32)).astype(BF16)


def dot(left, right):
    return lax.dot_general(left, right, (((1,), (0,)), ((), ())), preferred_element_type=F32)


def dot_t(left, right):
    return lax.dot_general(left, right, (((1,), (1,)), ((), ())), preferred_element_type=F32)


def dot3(left, right):
    (lh, ll), (rh, rl) = left, right
    return dot(lh, rh) + (dot(lh, rl) + dot(ll, rh))


def dot3_t(left, right):
    (lh, ll), (rh, rl) = left, right
    return dot_t(lh, rh) + (dot_t(lh, rl) + dot_t(ll, rh))


def remote(src, dst, send, recv, device):
    return pltpu.make_async_remote_copy(
        src_ref=src, dst_ref=dst, send_sem=send, recv_sem=recv, device_id=device, device_id_type=MESH
    )


def wait_bytes(ref, sem):
    pltpu.make_async_copy(ref, ref, sem).wait()


def flip(index, distance):
    bit = 1
    while bit <= distance:
        if distance & bit:
            index = index + (1 - 2 * lax.rem(lax.div(index, bit), 2)) * bit
        bit *= 2
    return index


def step_kernel(d, *refs):
    v = types.SimpleNamespace(**dict(zip(d.names, refs, strict=True)))
    NN, NC, R, H, FP, HC, CH, L = d.NN, d.NC, d.R, d.H, d.FP, d.HC, d.CH, LAYERS
    NDEV, RPP, PPC, HV = d.NDEV, d.RPP, d.PPC, d.HV
    n, c = lax.axis_index("nodes"), lax.axis_index("cols")
    me = n * NC + c
    ch, k = lax.div(n, 2), lax.rem(n, 2)
    sib = (ch * 2 + 1 - k, c)

    def device(index):
        return lax.div(index, NC), lax.rem(index, NC)

    def rows(i, size):
        return pl.ds(pl.multiple_of(i * size, size), size)

    barrier = pltpu.get_barrier_semaphore()

    def greet(i, carry):
        pl.semaphore_signal(
            barrier, inc=1, device_id=device(lax.rem(me + i, NDEV)), device_id_type=MESH
        )
        return carry

    lax.fori_loop(1, NDEV, greet, 0)

    def adj_load(j):
        return pltpu.make_async_copy(
            v.adj.at[:, rows(j, R)], v.adjb.at[lax.rem(j, d.NS)], v.ld.at[lax.rem(j, d.NS)]
        )

    for j in range(min(NN, d.NS)):
        adj_load(j).start()
    v.xg[n] = jnp.zeros((R, FP), F32)
    v.xg[n, :, : d.F] = v.feat[...]

    v.wpad[...] = jnp.zeros(v.wpad.shape, F32)
    v.wpad[: d.F, :HC] = v.w0[: d.F, :]
    v.wpad[FP : FP + d.F, :HC] = v.w0[d.F :, :]
    v.wt0[rows(c, HC), :] = v.wpad[: 2 * FP, :].T[:HC]
    for i in range(L - 1):
        v.wpad[:, :HC] = v.wr[i]
        v.wtr[i, rows(c, HC), :] = v.wpad[...].T[:HC]
    pl.semaphore_wait(barrier, NDEV - 1)

    def ag_send(g, src, buf):
        for dd in reversed(range(1, CH)):
            remote(
                src, buf.at[n], v.s_xy.at[g, dd], v.r_xy.at[g, dd], (flip(ch, dd) * 2 + k, c)
            ).start()
        remote(src, buf.at[n], v.s_sb.at[g, 0], v.r_sb.at[g, 0], sib).start()

    def ag_forward(g, buf, dd):
        j = flip(ch, dd) * 2 + k
        wait_bytes(buf.at[j], v.r_xy.at[g, dd])
        remote(buf.at[j], buf.at[j], v.s_sb.at[g, dd], v.r_sb.at[g, dd], sib).start()
        return j

    def ag_sibling(g, buf, dd):
        j = flip(ch, dd) * 2 + 1 - k
        wait_bytes(buf.at[j], v.r_sb.at[g, dd])
        return j

    def ag_drain(g, src):
        for dd in range(CH):
            if dd:
                wait_bytes(src, v.s_xy.at[g, dd])
            wait_bytes(src, v.s_sb.at[g, dd])

    def ar_send(a):
        def one(i, carry):
            remote(
                v.arb.at[a, me],
                v.arb.at[a, me],
                v.s_ar.at[a],
                v.r_ar.at[a],
                device(lax.rem(me + i, NDEV)),
            ).start()
            return carry

        lax.fori_loop(1, NDEV, one, 0)

    def ar_put(a, vectors):
        at = 0
        for vec in vectors:
            for i in range(vec.shape[1] // LANES):
                v.arb[a, me, at : at + 1, :] = vec[:, i * LANES : (i + 1) * LANES]
                at += 1
        if at < 8:
            v.arb[a, me, at:, :] = jnp.zeros((8 - at, LANES), F32)

    def ar_wait(a):
        wait_bytes(v.arb.at[a, pl.ds(0, NDEV - 1)], v.r_ar.at[a])
        return jnp.sum(v.arb[a], axis=0)

    def vec(total, i):
        return jnp.concatenate([total[i * HV + j : i * HV + j + 1] for j in range(HV)], axis=1)

    ag_send(0, v.xg.at[n], v.xg)
    for l in range(L):
        ref = v.wt0 if l == 0 else v.wtr.at[l - 1]
        for dd in range(1, NC):
            block = ref.at[rows(c, HC), :]
            remote(block, block, v.s_w.at[l], v.r_w.at[l], (n, lax.rem(c + dd, NC))).start()

    eye = lax.broadcasted_iota(jnp.int32, (R, R), 0) == lax.broadcasted_iota(jnp.int32, (R, R), 1)
    ones = jnp.ones((R, LANES), BF16)

    def column(row):
        return dot(jnp.where(eye, row.astype(F32), 0.0).astype(BF16), ones)

    v.valid[...] = column(v.nm[...])
    v.counted[...] = column(v.lm[...] * v.nm[...])
    v.label[...] = column(v.lb[...])

    v.invdeg[...] = jnp.zeros((R, LANES), F32)

    def adj_block(j, carry):
        adj_load(j).wait()
        block = v.adjb[lax.rem(j, d.NS)].astype(F32)
        if NN > d.NS:

            @pl.when(j + d.NS < NN)
            def _():
                adj_load(j + d.NS).start()

        half = block.astype(BF16)
        v.abf[j] = half
        v.at[j] = block.T.astype(BF16)
        v.invdeg[...] += dot(half, ones)
        return carry

    lax.fori_loop(0, NN, adj_block, 0)
    degree = v.invdeg[...]
    v.linked[...] = jnp.minimum(degree, 1.0)
    v.invdeg[...] = 1.0 / jnp.maximum(degree, 1.0)

    def wide(value):
        return jnp.concatenate([value] * HV, axis=1) if HV > 1 else value

    def gather_dot(g, buf, own, width):
        def add(j, block, first=False):
            high, low = split(block)
            a = v.abf[j]
            part = dot(jnp.concatenate([a, a], axis=1), jnp.concatenate([high, low], axis=0))
            if first:
                v.agg[:, :width] = part
            else:
                v.agg[:, :width] += part

        add(n, own[...], True)
        j = ag_sibling(g, buf, 0)
        add(j, buf[j])
        for dd in range(1, CH):
            j = ag_forward(g, buf, dd)
            add(j, buf[j])
        for dd in range(1, CH):
            j = ag_sibling(g, buf, dd)
            add(j, buf[j])

    RC = min(R, 64)

    def activate(l):
        def chunk(i, carry):
            r = rows(i, RC)
            x = v.lin[r, :]
            square = x * x
            t = jnp.tanh(GELU_OUT * x * (1.0 + GELU_CUBE * square))
            half = 0.5 * (1.0 + t)
            act = x * half
            v.acts[l, r, :] = act
            v.gp[l, r, :] = half + (0.5 * GELU_OUT) * x * (1.0 - t * t) * (
                1.0 + (3.0 * GELU_CUBE) * square
            )
            masked = wide(v.valid[r, :]) * act
            return (
                carry[0] + jnp.sum(masked.reshape(RC // 8, 8, H), axis=0),
                carry[1] + jnp.sum((masked * act).reshape(RC // 8, 8, H), axis=0),
            )

        zero = jnp.zeros((8, H), F32)
        one, two = lax.fori_loop(0, R // RC, chunk, (zero, zero))
        return jnp.sum(one, axis=0, keepdims=True), jnp.sum(two, axis=0, keepdims=True)

    def keep_stats(l, total):
        count = jnp.max(v.count[0:1, :], axis=1, keepdims=True)
        mean = vec(total, 0) / count
        var = vec(total, 1) / count - mean * mean
        inverse = lax.rsqrt(var + NORM_EPS)
        gain, shift = v.npar[0, l : l + 1, :], v.npar[1, l : l + 1, :]
        v.vecs[l, 0:1, :] = mean
        v.vecs[l, 1:2, :] = inverse
        v.vecs[l, 2:3, :] = gain * inverse
        v.vecs[l, 3:4, :] = shift - mean * (gain * inverse)
        v.vecs[l, 4:5, :] = gain

    gather_dot(0, v.xg, v.xg.at[n], FP)
    v.inh[0, :, :FP], v.inl[0, :, :FP] = split(v.xg[n])
    v.inh[0, :, FP : 2 * FP], v.inl[0, :, FP : 2 * FP] = split(v.agg[:, :FP] * v.invdeg[...])
    wait_bytes(v.wt0.at[pl.ds(0, (NC - 1) * HC)], v.r_w.at[0])
    v.w0h[...], v.w0l[...] = split(v.wt0[...])
    v.lin[...] = dot3_t(
        (v.inh[0, :, : 2 * FP], v.inl[0, :, : 2 * FP]), (v.w0h[...], v.w0l[...])
    )
    one, two = activate(0)
    ag_send(1, v.acts.at[0], v.ag.at[0])
    ar_put(
        0,
        [
            one,
            two,
            jnp.sum(v.valid[...], axis=0, keepdims=True),
            jnp.sum(v.counted[...], axis=0, keepdims=True),
        ],
    )
    ar_send(0)

    for l in range(1, L):
        wait_bytes(v.wtr.at[l - 1, pl.ds(0, (NC - 1) * HC)], v.r_w.at[l])
        v.wh[l - 1], v.wl[l - 1] = split(v.wtr[l - 1])
        total = ar_wait(l - 1)
        if l == 1:
            v.count[...] = total[2 * HV : 2 * HV + 2]
        keep_stats(l - 1, total)
        scale, shift = v.vecs[l - 1, 2:3, :], v.vecs[l - 1, 3:4, :]
        v.inh[l, :, :H], v.inl[l, :, :H] = split(v.acts[l - 1] * scale + shift)
        v.lin[...] = dot3_t(
            (v.inh[l, :, :H], v.inl[l, :, :H]), (v.wh[l - 1, :, :H], v.wl[l - 1, :, :H])
        )
        gather_dot(l, v.ag.at[l - 1], v.acts.at[l - 1], H)
        v.inh[l, :, H:], v.inl[l, :, H:] = split(
            v.agg[...] * wide(v.invdeg[...]) * scale + wide(v.linked[...]) * shift
        )
        v.lin[...] += dot3_t(
            (v.inh[l, :, H:], v.inl[l, :, H:]), (v.wh[l - 1, :, H:], v.wl[l - 1, :, H:])
        )
        one, two = activate(l)
        if l < L - 1:
            ag_send(l + 1, v.acts.at[l], v.ag.at[l])
        ar_put(l, [one, two])
        ar_send(l)

    v.whp[...] = jnp.zeros(v.whp.shape, F32)
    v.whp[:, : d.C] = v.whd[...]
    head = split(v.whp[...])
    lane = lax.broadcasted_iota(jnp.int32, (R, LANES), 1)
    onehot = jnp.where(lane.astype(F32) == v.label[...], 1.0, 0.0)
    for g in (1, 2):
        ag_drain(g, v.acts.at[0])
    keep_stats(L - 1, ar_wait(L - 1))
    last = split(v.acts[L - 1] * v.vecs[L - 1, 2:3, :] + v.vecs[L - 1, 3:4, :])
    logits = dot3(last, head) + v.bias[...]
    real = lane < d.C
    top = jnp.max(jnp.where(real, logits, -3.0e38), axis=1, keepdims=True)
    moved = logits - top
    power = jnp.where(real, jnp.exp(moved), 0.0)
    total = jnp.sum(power, axis=1, keepdims=True)
    logp = moved - jnp.log(total)
    counted = v.counted[...]
    label_count = jnp.max(v.count[1:2, :], axis=1, keepdims=True)
    g_logits = counted * (power / total - onehot) / label_count
    gl_split = split(g_logits)
    v.gout[...] = dot3_t(gl_split, head)

    def norm_sums(l):
        mean, inverse = v.vecs[l, 0:1, :], v.vecs[l, 1:2, :]

        def chunk(i, carry):
            r = rows(i, RC)
            g = v.gout[r, :]
            normed = (v.acts[l, r, :] - mean) * inverse
            return (
                carry[0] + jnp.sum((g * normed).reshape(RC // 8, 8, H), axis=0),
                carry[1] + jnp.sum(g.reshape(RC // 8, 8, H), axis=0),
            )

        zero = jnp.zeros((8, H), F32)
        one, two = lax.fori_loop(0, R // RC, chunk, (zero, zero))
        return jnp.sum(one, axis=0, keepdims=True), jnp.sum(two, axis=0, keepdims=True)

    ar_put(3, norm_sums(L - 1))
    ar_send(3)
    rows_loss = jnp.sum(jnp.where(real, onehot * logp, 0.0), axis=1, keepdims=True) * counted
    ar_put(
        6,
        [
            -jnp.sum(rows_loss, axis=0, keepdims=True),
            jnp.sum(g_logits, axis=0, keepdims=True),
        ],
    )
    ar_send(6)
    last_t = split((v.acts[L - 1] * v.vecs[L - 1, 2:3, :] + v.vecs[L - 1, 3:4, :]).T)
    v.hg[...] = dot3(last_t, gl_split)

    HP, HPC = d.HP, d.HPC

    def head_scatter(i, carry):
        t = lax.rem(me + i, NDEV)

        def go():
            remote(
                v.hg.at[rows(t, HP), :], v.hrecv.at[me], v.s_h.at[0], v.r_h.at[0], device(t)
            ).start()

        if HPC == NDEV:
            go()
        else:
            pl.when(t < HPC)(go)
        return carry

    lax.fori_loop(1, NDEV, head_scatter, 0)

    def others(index, size, ref_of, init):
        return lax.fori_loop(1, size, lambda i, s: s + ref_of(lax.rem(index + i, size)), init)

    def head_gather():
        def go():
            wait_bytes(v.hrecv.at[pl.ds(0, NDEV - 1)], v.r_h.at[0])
            piece = others(me, NDEV, lambda s: v.hrecv[s], v.hg[rows(me, HP), :])
            v.hfin[rows(me, HP), :] = piece

            def one(i, carry):
                block = v.hfin.at[rows(me, HP), :]
                remote(
                    block, block, v.s_h.at[1], v.r_h.at[1], device(lax.rem(me + i, NDEV))
                ).start()
                return carry

            lax.fori_loop(1, NDEV, one, 0)

        if HPC == NDEV:
            go()
        else:
            pl.when(me < HPC)(go)

    def cols_send(i):
        for dd in range(1, NC):
            t = lax.rem(c + dd, NC)
            remote(v.dwb.at[i, t], v.zrecv.at[i, c], v.s_z.at[i], v.r_z.at[i], (n, t)).start()

    def nodes_send(i):
        wait_bytes(v.zrecv.at[i, pl.ds(0, NC - 1)], v.r_z.at[i])
        v.zs[i] = others(c, NC, lambda s: v.zrecv[i, s], v.dwb[i, c])

        def one(j, carry):
            t = lax.rem(n + j, NN)

            def go():
                remote(
                    v.zs.at[i, rows(t, RPP), :], v.nrecv.at[i, n], v.s_n.at[i], v.r_n.at[i], (t, c)
                ).start()

            if PPC == NN:
                go()
            else:
                pl.when(t < PPC)(go)
            return carry

        lax.fori_loop(1, NN, one, 0)

    def reducer(fn):
        if PPC == NN:
            fn()
        else:
            pl.when(n < PPC)(fn)

    def pieces_out(i, fin, piece):
        fin[rows(n, RPP), :] = piece
        square = piece * piece
        for j in range(square.shape[1] // LANES):
            v.sq[...] += jnp.sum(
                square[:, j * LANES : (j + 1) * LANES].reshape(RPP // 8, 8, LANES), axis=0
            )

        def one(j, carry):
            block = fin.at[rows(n, RPP), :]
            remote(
                block, block, v.s_f.at[i], v.r_f.at[i], (lax.rem(n + j, NN), c)
            ).start()
            return carry

        lax.fori_loop(1, NN, one, 0)

    def nodes_gather(i):
        def go():
            wait_bytes(v.nrecv.at[i, pl.ds(0, NN - 1)], v.r_n.at[i])
            piece = others(n, NN, lambda s: v.nrecv[i, s], v.zs[i, rows(n, RPP), :])
            pieces_out(i, v.fin.at[i], piece)

        reducer(go)

    v.sq[...] = jnp.zeros((8, LANES), F32)

    def linear_grad(l, a):
        total = ar_wait(a)
        g_gain, g_shift = vec(total, 0), vec(total, 1)
        v.gn[0, l : l + 1, :] = g_gain
        v.gn[1, l : l + 1, :] = g_shift
        mean, inverse, scale = v.vecs[l, 0:1, :], v.vecs[l, 1:2, :], v.vecs[l, 2:3, :]
        count = jnp.max(v.count[0:1, :], axis=1, keepdims=True)
        by_one = scale * g_shift / count
        by_normed = scale * g_gain / count

        def chunk(i, carry):
            r = rows(i, RC)
            normed = (v.acts[l, r, :] - mean) * inverse
            g_active = scale * v.gout[r, :] - wide(v.valid[r, :]) * (by_one + normed * by_normed)
            g_linear = v.gp[l, r, :] * g_active
            v.lin[r, :] = g_linear
            v.glh[r, :], v.gll[r, :] = split(g_linear)
            return carry

        lax.fori_loop(0, R // RC, chunk, 0)

    def weight_grad(l, width):
        return dot3(split(v.lin[...].T), (v.inh[l, :, :width], v.inl[l, :, :width]))

    order = list(reversed(range(1, CH))) + [0]

    def scatter_drain(g):
        for dd in range(CH):
            wait_bytes(v.ag.at[0, dd], v.s_rs.at[g, 0, dd])
            if dd:
                wait_bytes(v.ag.at[0, dd], v.s_rs.at[g, 1, dd])

    for l in (2, 1):
        a = 5 - l
        g = l - 1
        linear_grad(l, a)
        gl = (v.glh[...], v.gll[...])
        spread = dot3(gl, (v.wh[l - 1, :, H:], v.wl[l - 1, :, H:])) * wide(v.invdeg[...])
        high, low = split(spread)
        v.spread[:R, :] = high
        v.spread[R:, :] = low
        out, srecv, crecv = v.ag.at[1], v.ag.at[0, :CH], v.ag.at[0, CH:]
        if l < L - 1:
            scatter_drain(g + 1)

        def partial(j):
            t = v.at[j]
            return dot(jnp.concatenate([t, t], axis=1), v.spread[...])

        for dd in order:
            out[dd] = partial(flip(ch, dd) * 2 + 1 - k)
            remote(out.at[dd], srecv.at[dd], v.s_rs.at[g, 0, dd], v.r_rs.at[g, 0, dd], sib).start()
        for dd in order:
            part = partial(flip(ch, dd) * 2 + k)
            wait_bytes(srecv.at[dd], v.r_rs.at[g, 0, dd])
            out[CH + dd] = part + srecv[dd]
            if dd:
                remote(
                    out.at[CH + dd],
                    crecv.at[dd],
                    v.s_rs.at[g, 1, dd],
                    v.r_rs.at[g, 1, dd],
                    (flip(ch, dd) * 2 + k, c),
                ).start()
        v.gout[...] = out[CH] + dot3(
            gl, (v.wh[l - 1, :, :H], v.wl[l - 1, :, :H])
        )
        grad = weight_grad(l, 2 * H)
        for t in range(NC):
            v.dwb[l - 1, t] = grad[t * HC : (t + 1) * HC, :]
        cols_send(l - 1)
        if l == 2:
            head_gather()
        else:
            nodes_gather(1)
        for dd in range(1, CH):
            wait_bytes(crecv.at[dd], v.r_rs.at[g, 1, dd])
            v.gout[...] += crecv[dd]
        ar_put(a + 1, norm_sums(l - 1))
        ar_send(a + 1)
        nodes_send(l - 1)

    linear_grad(0, 5)
    grad = weight_grad(0, 2 * FP)
    for t in range(NC):
        v.d0[t] = grad[t * HC : (t + 1) * HC, :]

    def first_scatter(i, carry):
        t = lax.rem(me + i, NDEV)
        tn, tc = device(t)

        def go():
            remote(
                v.d0.at[tc, rows(tn, RPP), :], v.recv0.at[me], v.s_0.at[0], v.r_0.at[0], (tn, tc)
            ).start()

        if PPC == NN:
            go()
        else:
            pl.when(tn < PPC)(go)
        return carry

    lax.fori_loop(1, NDEV, first_scatter, 0)
    nodes_gather(0)

    def first_gather():
        wait_bytes(v.recv0.at[pl.ds(0, NDEV - 1)], v.r_0.at[0])
        piece = others(me, NDEV, lambda s: v.recv0[s], v.d0[c, rows(n, RPP), :])
        pieces_out(2, v.fin0, piece)

    reducer(first_gather)
    ar_put(7, [jnp.sum(v.sq[...], axis=0, keepdims=True)])
    ar_send(7)

    total = ar_wait(6)
    bias_grad = total[1:2]
    v.misc[...] = jnp.zeros((8, LANES), F32)
    v.misc[0:1, :] = total[0:1]
    v.misc[1:2, :] = v.count[1:2, :]
    v.misc[3:4, :] = bias_grad

    def fin_wait(i, fin):
        if PPC == NN:
            wait_bytes(fin.at[pl.ds(0, (NN - 1) * RPP), :], v.r_f.at[i])
        else:

            @pl.when(n < PPC)
            def _():
                wait_bytes(fin.at[pl.ds(0, (PPC - 1) * RPP), :], v.r_f.at[i])

            @pl.when(n >= PPC)
            def _():
                wait_bytes(fin.at[pl.ds(0, PPC * RPP), :], v.r_f.at[i])

    if HPC == NDEV:
        wait_bytes(v.hfin.at[pl.ds(0, (NDEV - 1) * HP), :], v.r_h.at[1])
    else:

        @pl.when(me < HPC)
        def _():
            wait_bytes(v.hfin.at[pl.ds(0, (HPC - 1) * HP), :], v.r_h.at[1])

        @pl.when(me >= HPC)
        def _():
            wait_bytes(v.hfin.at[pl.ds(0, HPC * HP), :], v.r_h.at[1])

    head_grad = v.hfin[...]
    v.gh[...] = head_grad[:, : d.C]
    replicated = jnp.sum(head_grad * head_grad, axis=0, keepdims=True) + bias_grad * bias_grad
    small = jnp.zeros((1, H), F32)
    for i in range(2):
        small += jnp.sum(v.gn[i] * v.gn[i], axis=0, keepdims=True)
    for j in range(HV):
        replicated += small[:, j * LANES : (j + 1) * LANES]

    for i in range(L - 1):
        fin_wait(i, v.fin.at[i])
        v.wpad[...] = jnp.zeros(v.wpad.shape, F32)
        v.wpadt[:HC, :] = v.fin[i]
        v.gr[i] = v.wpadt[...].T[:, :HC]
    total = ar_wait(7)
    squares = jnp.sum(total[0:1] + replicated, axis=1, keepdims=True)
    norm = jnp.sqrt(squares)
    v.misc[2:3, :] = jnp.broadcast_to(norm, (1, LANES))
    v.misc[4:5, :] = jnp.broadcast_to(CLIP / jnp.maximum(norm, CLIP), (1, LANES))
    fin_wait(2, v.fin0)
    v.wpadt[:HC, : 2 * FP] = v.fin0[...]
    first_grad = v.wpadt[:, : 2 * FP].T
    v.g0[: d.F, :] = first_grad[: d.F, :HC]
    v.g0[d.F :, :] = first_grad[FP : FP + d.F, :HC]

    ag_drain(0, v.xg.at[0])
    for l in range(L):
        ref = v.wt0 if l == 0 else v.wtr.at[l - 1]
        wait_bytes(ref.at[pl.ds(0, (NC - 1) * HC)], v.s_w.at[l])
    for a in range(8):
        wait_bytes(v.arb.at[a, pl.ds(0, NDEV - 1)], v.s_ar.at[a])
    for i in range(L - 1):
        wait_bytes(v.zrecv.at[i, pl.ds(0, NC - 1)], v.s_z.at[i])

    scatter_drain(0)

    if PPC == NN:
        for i in range(L - 1):
            wait_bytes(v.nrecv.at[i, pl.ds(0, NN - 1)], v.s_n.at[i])
        wait_bytes(v.recv0.at[pl.ds(0, NDEV - 1)], v.s_0.at[0])
    else:

        @pl.when(n < PPC)
        def _():
            for i in range(L - 1):
                wait_bytes(v.nrecv.at[i, pl.ds(0, PPC - 1)], v.s_n.at[i])
            wait_bytes(v.recv0.at[pl.ds(0, PPC * NC - 1)], v.s_0.at[0])

        @pl.when(n >= PPC)
        def _():
            for i in range(L - 1):
                wait_bytes(v.nrecv.at[i, pl.ds(0, PPC)], v.s_n.at[i])
            wait_bytes(v.recv0.at[pl.ds(0, PPC * NC)], v.s_0.at[0])

    def drain_fin():
        for i in range(L - 1):
            wait_bytes(v.nrecv.at[i, pl.ds(0, NN - 1)], v.s_f.at[i])
        wait_bytes(v.recv0.at[pl.ds(0, NN - 1)], v.s_f.at[2])

    reducer(drain_fin)

    def drain_head():
        wait_bytes(v.hrecv.at[pl.ds(0, NDEV - 1)], v.s_h.at[1])

    if HPC == NDEV:
        wait_bytes(v.hrecv.at[pl.ds(0, NDEV - 1)], v.s_h.at[0])
        drain_head()
    else:

        @pl.when(me < HPC)
        def _():
            wait_bytes(v.hrecv.at[pl.ds(0, HPC - 1)], v.s_h.at[0])
            drain_head()

        @pl.when(me >= HPC)
        def _():
            wait_bytes(v.hrecv.at[pl.ds(0, HPC)], v.s_h.at[0])


def gradients(NN, NC, feat, adj, nm, lb, lm, w0, wr, npar, whd, bias):
    R, F = feat.shape
    H, C = whd.shape
    HC = w0.shape[1]
    CH, NDEV = NN // 2, NN * NC
    FP = -(-F // LANES) * LANES
    RPP = max(8, HC // NN)
    HP = max(8, H // NDEV)
    NS = min(NN, 8)
    d = types.SimpleNamespace(
        NN=NN, NC=NC, R=R, F=F, H=H, C=C, HC=HC, CH=CH, NDEV=NDEV, FP=FP, RPP=RPP, NS=NS,
        PPC=HC // RPP, HP=HP, HPC=H // HP, HV=H // LANES,
    )
    dma = pltpu.SemaphoreType.DMA
    L = LAYERS
    scratch = {
        "xg": pltpu.VMEM((NN, R, FP), F32),
        "ag": pltpu.VMEM((L - 1, NN, R, H), F32),
        "acts": pltpu.VMEM((L, R, H), F32),
        "gp": pltpu.VMEM((L, R, H), F32),
        "adjb": pltpu.VMEM((NS, R, R), jnp.int32),
        "abf": pltpu.VMEM((NN, R, R), BF16),
        "at": pltpu.VMEM((NN, R, R), BF16),
        "wpad": pltpu.VMEM((2 * H, LANES), F32),
        "wpadt": pltpu.VMEM((LANES, 2 * H), F32),
        "wt0": pltpu.VMEM((H, 2 * FP), F32),
        "wtr": pltpu.VMEM((L - 1, H, 2 * H), F32),
        "w0h": pltpu.VMEM((H, 2 * FP), BF16),
        "w0l": pltpu.VMEM((H, 2 * FP), BF16),
        "wh": pltpu.VMEM((L - 1, H, 2 * H), BF16),
        "wl": pltpu.VMEM((L - 1, H, 2 * H), BF16),
        "whp": pltpu.VMEM((H, LANES), F32),
        "inh": pltpu.VMEM((L, R, 2 * H), BF16),
        "inl": pltpu.VMEM((L, R, 2 * H), BF16),
        "agg": pltpu.VMEM((R, max(H, FP)), F32),
        "lin": pltpu.VMEM((R, H), F32),
        "gout": pltpu.VMEM((R, H), F32),
        "glh": pltpu.VMEM((R, H), BF16),
        "gll": pltpu.VMEM((R, H), BF16),
        "spread": pltpu.VMEM((2 * R, H), BF16),
        "valid": pltpu.VMEM((R, LANES), F32),
        "counted": pltpu.VMEM((R, LANES), F32),
        "label": pltpu.VMEM((R, LANES), F32),
        "invdeg": pltpu.VMEM((R, LANES), F32),
        "linked": pltpu.VMEM((R, LANES), F32),
        "count": pltpu.VMEM((2, LANES), F32),
        "vecs": pltpu.VMEM((L, 8, H), F32),
        "sq": pltpu.VMEM((8, LANES), F32),
        "arb": pltpu.VMEM((8, NDEV, 8, LANES), F32),
        "dwb": pltpu.VMEM((L - 1, NC, HC, 2 * H), F32),
        "zrecv": pltpu.VMEM((L - 1, NC, HC, 2 * H), F32),
        "zs": pltpu.VMEM((L - 1, HC, 2 * H), F32),
        "nrecv": pltpu.VMEM((L - 1, NN, RPP, 2 * H), F32),
        "fin": pltpu.VMEM((L - 1, HC, 2 * H), F32),
        "d0": pltpu.VMEM((NC, HC, 2 * FP), F32),
        "recv0": pltpu.VMEM((NDEV, RPP, 2 * FP), F32),
        "fin0": pltpu.VMEM((HC, 2 * FP), F32),
        "hg": pltpu.VMEM((H, LANES), F32),
        "hrecv": pltpu.VMEM((NDEV, HP, LANES), F32),
        "hfin": pltpu.VMEM((H, LANES), F32),
        "ld": dma((NS,)),
        "s_xy": dma((L, CH)),
        "r_xy": dma((L, CH)),
        "s_sb": dma((L, CH)),
        "r_sb": dma((L, CH)),
        "s_w": dma((L,)),
        "r_w": dma((L,)),
        "s_ar": dma((8,)),
        "r_ar": dma((8,)),
        "s_rs": dma((L - 1, 2, CH)),
        "r_rs": dma((L - 1, 2, CH)),
        "s_z": dma((L - 1,)),
        "r_z": dma((L - 1,)),
        "s_n": dma((L - 1,)),
        "r_n": dma((L - 1,)),
        "s_f": dma((L,)),
        "r_f": dma((L,)),
        "s_0": dma((1,)),
        "r_0": dma((1,)),
        "s_h": dma((2,)),
        "r_h": dma((2,)),
    }
    ins = ["feat", "adj", "nm", "lb", "lm", "w0", "wr", "npar", "whd", "bias"]
    outs = ["g0", "gr", "gn", "gh", "misc"]
    d.names = ins + outs + list(scratch)
    vmem = pl.BlockSpec(memory_space=pltpu.VMEM)
    specs = [vmem] * len(ins)
    specs[1] = pl.BlockSpec(memory_space=pl.ANY)
    return pl.pallas_call(
        functools.partial(step_kernel, d),
        out_shape=[
            jax.ShapeDtypeStruct(w0.shape, F32),
            jax.ShapeDtypeStruct(wr.shape, F32),
            jax.ShapeDtypeStruct(npar.shape, F32),
            jax.ShapeDtypeStruct(whd.shape, F32),
            jax.ShapeDtypeStruct((8, LANES), F32),
        ],
        in_specs=specs,
        out_specs=[vmem] * len(outs),
        scratch_shapes=list(scratch.values()),
        compiler_params=pltpu.CompilerParams(
            collective_id=0, has_side_effects=True, vmem_limit_bytes=60 * 2**20
        ),
    )(feat, adj, nm, lb, lm, w0, wr, npar, whd, bias)


def adamw(weight, first, second, average, grad, rate):
    first = BETA_ONE * first + (1.0 - BETA_ONE) * grad
    second = BETA_TWO * second + (1.0 - BETA_TWO) * grad * grad
    fix_one = 1.0 - BETA_ONE**ADAM_STEP
    fix_two = 1.0 - BETA_TWO**ADAM_STEP
    update = first / fix_one / (jnp.sqrt(second / fix_two) + ADAM_EPS)
    weight = weight - rate * (update + DECAY * weight)
    average = AVERAGE * average + (1.0 - AVERAGE) * weight
    return (first, second, weight, average)


def local(
    nodes, cols, features, adjacency, node_mask, labels, label_mask,
    weight_first, weight_rest, norm_params, weight_head, bias_head,
    moment_first, moment_rest, moment_norm, moment_head, moment_bias,
    square_first, square_rest, square_norm, square_head, square_bias,
    average_first, average_rest, average_norm, average_head, average_bias,
):
    classes = weight_head.shape[1]
    bias = jnp.pad(bias_head[None, :], ((0, 0), (0, LANES - classes)))
    grad_first, grad_rest, grad_norm_params, grad_head, misc = gradients(
        nodes, cols, features[0], adjacency[0], node_mask, labels, label_mask,
        weight_first, weight_rest, norm_params, weight_head, bias,
    )
    loss_total, label_count, gradient_norm, scale = (misc[i, 0] for i in (0, 1, 2, 4))
    grad_bias = misc[3, :classes]
    first_out = adamw(
        weight_first, moment_first, square_first, average_first, grad_first * scale, RATE_MATRIX
    )
    rest_out = adamw(
        weight_rest, moment_rest, square_rest, average_rest, grad_rest * scale, RATE_MATRIX
    )
    norm_out = adamw(
        norm_params, moment_norm, square_norm, average_norm, grad_norm_params * scale, RATE_SMALL
    )
    head_out = adamw(
        weight_head, moment_head, square_head, average_head, grad_head * scale, RATE_MATRIX
    )
    bias_out = adamw(
        bias_head, moment_bias, square_bias, average_bias, grad_bias * scale, RATE_SMALL
    )
    return (
        loss_total, label_count, gradient_norm,
        *first_out, *rest_out, *norm_out, *head_out, *bias_out,
    )


def solution(mesh):
    rows, first, rest, all_of = P("cols", "nodes", None), P(None, "cols"), P(None, None, "cols"), P()
    state = [first, rest, all_of, all_of, all_of]
    return jax.shard_map(
        functools.partial(local, mesh.shape["nodes"], mesh.shape["cols"]),
        mesh=mesh,
        in_specs=(rows, rows) + (P("cols", "nodes"),) * 3 + tuple(state * 4),
        out_specs=(all_of,) * 3 + tuple(spec for spec in state for _ in range(4)),
        check_vma=False,
    )
```

time: 794 us -> 171 us (0.22)
  blocking collectives: 352 us -> 0 us
  waiting for transfers between devices: 317 us -> 0 us
  Pallas kernels: 0 us -> 137 us
  matrix products: 46.9 us -> 0 us
  other arithmetic: 32.9 us -> 6.57 us
  between operations: 20.4 us -> 0.93 us
  local copies, waits for them, and re-layouts: 14.7 us -> 25.2 us
    psum x8 -> x0, blocking collectives: 271 us -> none  [the longest x2 80.4 us: layer_backward(): lax.psum((jnp.sum(grad_out * normed, 0), jnp.sum(grad_out, 0)), ('nodes',...]
    reduce_scatter x4 -> x0, waiting for transfers between devices: 154 us -> none  [the longest x2 86 us: layer_backward(): lax.psum_scatter(matmul(grad_cols, weight.T), 'cols', scatter_dimension=0...]
    all_gather x4 -> x0, waiting for transfers between devices: 147 us -> none  [the longest x2 91.9 us: layer_forward(): stored = lax.all_gather(inputs, 'cols', axis=0, tiled=True)]
    pallas_call x0 -> x1, Pallas kernels: none -> 137 us  [gradients(): pl.pallas_call(functools.partial(step_kernel, d), out_shape=[jax.ShapeDty...]
    dot_general x16 -> x0, matrix products: 46.9 us -> none  [matmul(): return jnp.dot(left, right, precision=HIGH)]
    all_to_all x4 -> x0, blocking collectives: 45.6 us -> none  [the longest x2 23 us: layer_forward(): lax.all_to_all(matmul(stored, weight), 'cols', split_axis=0, concat_axis=...]
    all_gather x2 -> x0, blocking collectives: 35.3 us -> none  [the longest x1 20.2 us: layer_forward(): stored = lax.all_gather(inputs, 'cols', axis=0, tiled=True)]
    unnamed x123 -> x76, local copies, waits for them, and re-layouts: 7.03 us -> 22.6 us
  transfers between devices with their start and end apart: 11 -> 0, of which waited for: 10 -> 0; matrix products, arithmetic and copies ran while one was open for 3% -> 0% of each run, Pallas kernels for 0% -> 0%
where the time goes in v1:
time: 171 us; the launch traced here: 170 us
  Pallas kernels  137 us (80%)
  local copies, waits for them, and re-layouts  25.2 us (15%)
  other arithmetic  6.57 us (4%)
    pallas_call x1, Pallas kernels, gradients(): pl.pallas_call(functools.partial(step_kernel, d), out_shape=[jax.ShapeDty...  137 us
    unnamed x76, local copies, waits for them, and re-layouts  22.6 us
    add x5, other arithmetic, adamw(): average = AVERAGE * average + (1.0 - AVERAGE) * weight  6.57 us

profile of v1, /device:TPU:0, one launch (start us, length us, event | category | flops | bytes accessed | tf_op | source)
XLA Modules:
  0.0 170.1 jit_solution(2028604472815848686)
XLA Ops:
  0.7 0.0 copy-start.3
  0.7 2.0 %copy.91.refs_6_ = f32[2,512,64]{2,1,0:T(8,128)} copy(f32[2,512,64]{1,2,0:T(8,128)} %param.31) | data formatting | bytes 524288 | tf_op args[6]
  2.7 1.5 copy.93.refs_8_
  4.2 1.6 copy.90.refs_5_
  5.8 1.6 copy.89
  7.5 1.3 copy.92.refs_7_
  8.8 1.2 pad.4.refs_9_
  9.9 137.5 %shard_map.416 = (f32[200,64]{1,0:T(8,128)}, f32[2,512,64]{2,1,0:T(8,128)}, f32[2,3,256]{2,1,0:T(4,128)}, f32[256,47]{1,0:T(8,128)}, f32[8,128]{1,0:T(8,128)}) custom-call(f32[256,100]{1,0:T(8,128)} %bitcast.15, s32[256,2048]{1,0:T(8,128)} %bitcast.14, s32[1,256]{1,0:T(1,128)} %refs_2_.1, s32[1,256]{1,0:T(1,128)} %refs_3_.1, s32[1,256]{1,0:T(1,128)} %refs_4_.1, ...), custom_call_target="tpu_custom_call" | custom-call | tf_op jit(solution)/shard_map/pallas_call | solution.py:778
  147.4 1.4 fusion.15
  148.8 0.0 copy-done.3
  148.8 0.2 copy.101
  149.0 0.0 copy-done.4
  149.0 1.0 copy.104
  150.0 0.0 copy-done.5
  150.0 1.0 copy.99
  151.0 0.0 copy-done
  151.0 2.5 %multiply_add_fusion = (f32[2,512,64]{2,1,0:T(8,128)S(1)}, f32[2,512,64]{2,1,0:T(8,128)S(1)}, f32[2,512,64]{2,1,0:T(8,128)S(1)}, f32[2,512,64]{2,1,0:T(8,128)S(1)}) fusion(f32[2,512,64]{2,1,0:T(8,128)} %copy.104, f32[2,512,64]{2,1,0:T(8,128)S(1)} %copy-done, f32[2,512,64]{2,1,0:T(8,128)} %get-tuple-element.30, f32[]{:T(128)} %bitcast.6, ...), kind=kLoop, calls=%fused_computation.2 | loop fusion | flops 1245184 | bytes 2359300 | tf_op jit(solution)/shard_map/add | solution.py:803
  153.5 0.0 copy-start.11
  153.5 0.0 copy-start.12
  153.5 0.0 copy-start.13
  153.5 0.0 copy-start.1
  153.5 0.0 copy-start.6
  153.5 0.9 copy.122
  154.4 0.9 copy.123
  155.3 0.0 copy-start.8
  155.3 0.0 copy-start.9
  155.3 0.0 copy-start.10
  155.4 0.0 copy-start.2
  155.4 0.0 copy-start.7
  155.4 0.9 copy.124
  156.3 0.9 copy.125
  157.2 0.0 copy-done.11
  157.2 0.1 copy.111
  157.3 0.0 copy-done.12
  157.3 0.1 copy.113
  157.4 0.0 copy-done.13
  157.4 0.0 copy-start.14
  157.4 0.0 copy-start.15
  157.4 0.0 copy-start.16
  157.4 0.0 copy-start.17
  157.4 0.0 copy-start.18
  157.5 0.1 copy.116
  157.6 0.0 copy-done.1
  157.6 0.8 multiply_add_fusion.2
  158.4 0.7 copy.130
  159.1 0.7 copy.131
  159.8 0.7 copy.132
  160.5 0.7 copy.133
  161.2 0.0 copy-done.20
  161.2 1.9 %multiply_add_fusion.6 = (f32[47]{0:T(128)}, f32[47]{0:T(128)}, f32[47]{0:T(128)}, f32[47]{0:T(128)}) fusion(f32[47]{0:T(128)S(1)} %copy-done.20, f32[47]{0:T(128)S(1)} %copy-done.19, f32[]{:T(128)} %bitcast.6, f32[8,128]{1,0:T(8,128)} %get-tuple-element.28, f32[47]{0:T(128)S(1)} %copy-done.21, f32[47]{0:T(128)S(1)} %copy-done.22), kind=kLoop, calls=%fused_computation.27 | loop fusion | flops 893 | bytes 1696 | tf_op jit(solution)/shard_map/add | solution.py:803
  163.1 0.1 copy.94
  163.2 0.1 copy.95
  163.3 0.1 copy.98
  163.4 0.8 multiply_add_fusion.4
  164.2 0.7 copy.118
  164.9 0.7 copy.119
  165.6 0.7 copy.120
  166.3 0.7 copy.121
  167.0 0.0 copy-done.15
  167.0 0.7 fusion.4
  167.7 0.6 copy.126
  168.3 0.6 copy.127
  168.9 0.6 copy.128
  169.5 0.6 copy.129
  (20 shorter events, 0.0 us)
Async XLA Ops:
  0.7 148.1 %copy-start.3 = (f32[2,512,64]{1,2,0:T(8,128)S(1)}, f32[2,512,64]{1,2,0:T(8,128)}, u32[]{:S(2)}) copy-start(f32[2,512,64]{1,2,0:T(8,128)} %param.41) | copy-start | bytes 786436
  4.2 144.8 %copy-start.4 = (f32[2,512,64]{1,2,0:T(8,128)S(1)}, f32[2,512,64]{1,2,0:T(8,128)}, u32[]{:S(2)}) copy-start(f32[2,512,64]{1,2,0:T(8,128)} %param.46) | copy-start | bytes 786436
  9.9 140.1 %copy-start.5 = (f32[2,512,64]{1,2,0:T(8,128)S(1)}, f32[2,512,64]{1,2,0:T(8,128)}, u32[]{:S(2)}) copy-start(f32[2,512,64]{1,2,0:T(8,128)} %param.36) | copy-start | bytes 786436
  9.9 141.1 %copy-start = (f32[2,512,64]{2,1,0:T(8,128)S(1)}, f32[2,512,64]{2,1,0:T(8,128)}, u32[]{:S(2)}) copy-start(f32[2,512,64]{2,1,0:T(8,128)} %copy.91.refs_6_) | copy-start | bytes 786436
  153.5 3.7 %copy-start.11 = (f32[256,47]{0,1:T(8,128)S(1)}, f32[256,47]{0,1:T(8,128)}, u32[]{:S(2)}) copy-start(f32[256,47]{0,1:T(8,128)} %param.38) | copy-start | bytes 144388
  153.5 3.8 %copy-start.12 = (f32[256,47]{0,1:T(8,128)S(1)}, f32[256,47]{0,1:T(8,128)}, u32[]{:S(2)}) copy-start(f32[256,47]{0,1:T(8,128)} %param.43) | copy-start | bytes 144388
  153.5 3.9 %copy-start.13 = (f32[256,47]{0,1:T(8,128)S(1)}, f32[256,47]{0,1:T(8,128)}, u32[]{:S(2)}) copy-start(f32[256,47]{0,1:T(8,128)} %param.48) | copy-start | bytes 144388
  153.5 4.1 %copy-start.1 = (f32[256,47]{1,0:T(8,128)S(1)}, f32[256,47]{1,0:T(8,128)}, u32[]{:S(2)}) copy-start(f32[256,47]{1,0:T(8,128)} %copy.93.refs_8_) | copy-start | bytes 144388
  153.5 4.0 %copy-start.6 = (f32[256,47]{1,0:T(8,128)S(1)}, f32[256,47]{1,0:T(8,128)}, u32[]{:S(2)}) copy-start(f32[256,47]{1,0:T(8,128)} %get-tuple-element.32) | copy-start | bytes 144388
  155.3 5.9 %copy-start.19 = (f32[47]{0:T(128)S(1)}, f32[47]{0:T(128)}, u32[]{:S(2)}) copy-start(f32[47]{0:T(128)} %param.34) | copy-start | bytes 568
  155.3 5.9 %copy-start.20 = (f32[47]{0:T(128)S(1)}, f32[47]{0:T(128)}, u32[]{:S(2)}) copy-start(f32[47]{0:T(128)} %param.49) | copy-start | bytes 568
  155.3 5.9 %copy-start.21 = (f32[47]{0:T(128)S(1)}, f32[47]{0:T(128)}, u32[]{:S(2)}) copy-start(f32[47]{0:T(128)} %param.44) | copy-start | bytes 568
  155.3 5.9 %copy-start.22 = (f32[47]{0:T(128)S(1)}, f32[47]{0:T(128)}, u32[]{:S(2)}) copy-start(f32[47]{0:T(128)} %param.39) | copy-start | bytes 568
  155.3 7.8 %copy-start.8 = (f32[200,64]{0,1:T(8,128)S(1)}, f32[200,64]{0,1:T(8,128)}, u32[]{:S(2)}) copy-start(f32[200,64]{0,1:T(8,128)} %param.35) | copy-start | bytes 153604
  155.3 7.9 %copy-start.9 = (f32[200,64]{0,1:T(8,128)S(1)}, f32[200,64]{0,1:T(8,128)}, u32[]{:S(2)}) copy-start(f32[200,64]{0,1:T(8,128)} %param.40) | copy-start | bytes 153604
  155.3 7.9 %copy-start.10 = (f32[200,64]{0,1:T(8,128)S(1)}, f32[200,64]{0,1:T(8,128)}, u32[]{:S(2)}) copy-start(f32[200,64]{0,1:T(8,128)} %param.45) | copy-start | bytes 153604
  155.4 8.0 %copy-start.2 = (f32[200,64]{1,0:T(8,128)S(1)}, f32[200,64]{1,0:T(8,128)}, u32[]{:S(2)}) copy-start(f32[200,64]{1,0:T(8,128)} %copy.90.refs_5_) | copy-start | bytes 153604
  155.4 8.0 %copy-start.7 = (f32[200,64]{1,0:T(8,128)S(1)}, f32[200,64]{1,0:T(8,128)}, u32[]{:S(2)}) copy-start(f32[200,64]{1,0:T(8,128)} %get-tuple-element.29) | copy-start | bytes 153604
  157.4 9.6 %copy-start.14 = (f32[2,3,256]{2,0,1:T(2,128)S(1)}, f32[2,3,256]{2,0,1:T(2,128)}, u32[]{:S(2)}) copy-start(f32[2,3,256]{2,0,1:T(2,128)} %param.32) | copy-start | bytes 18436
  157.4 9.6 %copy-start.15 = (f32[2,3,256]{2,1,0:T(4,128)S(1)}, f32[2,3,256]{2,1,0:T(4,128)}, u32[]{:S(2)}) copy-start(f32[2,3,256]{2,1,0:T(4,128)} %get-tuple-element.31) | copy-start | bytes 18436
  157.4 9.6 %copy-start.16 = (f32[2,3,256]{2,0,1:T(2,128)S(1)}, f32[2,3,256]{2,0,1:T(2,128)}, u32[]{:S(2)}) copy-start(f32[2,3,256]{2,0,1:T(2,128)} %param.47) | copy-start | bytes 18436
  157.4 9.6 %copy-start.17 = (f32[2,3,256]{2,0,1:T(2,128)S(1)}, f32[2,3,256]{2,0,1:T(2,128)}, u32[]{:S(2)}) copy-start(f32[2,3,256]{2,0,1:T(2,128)} %param.42) | copy-start | bytes 18436
  157.4 9.6 %copy-start.18 = (f32[2,3,256]{2,0,1:T(2,128)S(1)}, f32[2,3,256]{2,0,1:T(2,128)}, u32[]{:S(2)}) copy-start(f32[2,3,256]{2,0,1:T(2,128)} %param.37) | copy-start | bytes 18436

commit v2 on v1

v2 whole, which is shorter than its diff:
```python
import functools
import types

import jax
import jax.numpy as jnp
from jax import lax
from jax.experimental import pallas as pl
from jax.experimental.pallas import tpu as pltpu
from jax.sharding import PartitionSpec as P

LAYERS = 3
ADAM_STEP = 10
CLIP = 0.02
RATE_MATRIX = 0.03
RATE_SMALL = 0.3
BETA_ONE = 0.9
BETA_TWO = 0.999
ADAM_EPS = 1e-08
DECAY = 0.01
AVERAGE = 0.9
NORM_EPS = 1e-05

MESH = pl.DeviceIdType.MESH
F32 = jnp.float32
BF16 = jnp.bfloat16
LANES = 128
GELU_OUT = 0.7978845608028654
GELU_CUBE = 0.044715


def cat(values, axis):
    return values[0] if len(values) == 1 else jnp.concatenate(values, axis=axis)


def split(value):
    high = value.astype(BF16)
    return high, (value - high.astype(F32)).astype(BF16)


def dot(left, right):
    return lax.dot_general(left, right, (((1,), (0,)), ((), ())), preferred_element_type=F32)


def dot_t(left, right):
    return lax.dot_general(left, right, (((1,), (1,)), ((), ())), preferred_element_type=F32)


def dot3(left, right):
    (lh, ll), (rh, rl) = left, right
    return dot(cat([lh, lh, ll], 1), cat([rh, rl, rh], 0))


def dot3_t(left, right):
    (lh, ll), (rh, rl) = left, right
    return dot_t(cat([lh, lh, ll], 1), cat([rh, rl, rh], 1))


def remote(src, dst, send, recv, device):
    return pltpu.make_async_remote_copy(
        src_ref=src, dst_ref=dst, send_sem=send, recv_sem=recv, device_id=device, device_id_type=MESH
    )


def wait_bytes(ref, sem):
    pltpu.make_async_copy(ref, ref, sem).wait()


def flip(index, distance):
    bit = 1
    while bit <= distance:
        if distance & bit:
            index = index + (1 - 2 * lax.rem(lax.div(index, bit), 2)) * bit
        bit *= 2
    return index


def step_kernel(d, *refs):
    v = types.SimpleNamespace(**dict(zip(d.names, refs, strict=True)))
    NN, NC, R, H, HC, CH, L = d.NN, d.NC, d.R, d.H, d.HC, d.CH, LAYERS
    NDEV, RPP, PPC, HV, F, FR, CR = d.NDEV, d.RPP, d.PPC, d.HV, d.F, d.FR, d.CR
    n, c = lax.axis_index("nodes"), lax.axis_index("cols")
    me = n * NC + c
    ch, k = lax.div(n, 2), lax.rem(n, 2)
    sib = (ch * 2 + 1 - k, c)
    drains = []

    def device(index):
        return lax.div(index, NC), lax.rem(index, NC)

    def peer(dd):
        return flip(ch, dd) * 2 + k, c

    def rows(i, size):
        return pl.ds(pl.multiple_of(i * size, size), size)

    def send(src, dst, ssem, rsem, dev):
        remote(src, dst, ssem, rsem, dev).start()
        drains.append(lambda: wait_bytes(src, ssem))

    def either(always, condition, fn, other=None):
        if always:
            fn()
        else:
            pl.when(condition)(fn)
            if other is not None:
                pl.when(jnp.logical_not(condition))(other)

    barrier = pltpu.get_barrier_semaphore()

    def greet(i, carry):
        pl.semaphore_signal(
            barrier, inc=1, device_id=device(lax.rem(me + i, NDEV)), device_id_type=MESH
        )
        return carry

    lax.fori_loop(1, NDEV, greet, 0)

    def adj_cols(j, core):
        return v.adj.at[:, rows(j * 2 + core, R)]

    loads = [pltpu.make_async_copy(v.wr.at[i], v.wtr.at[i, rows(c, HC), :], v.ld.at[i]) for i in range(L - 1)]
    for copy in loads:
        copy.start()
    for j in range(CH):
        pltpu.make_async_copy(adj_cols(j, k), v.adjb.at[0, j], v.ld.at[L + j]).start()
    v.xown[:F, :] = v.feat[...]
    v.xown[F:, :] = jnp.ones((FR - F, R), F32)
    v.wt0[rows(c, HC), :] = jnp.zeros((HC, 2 * FR), F32)
    v.wt0[rows(c, HC), :F] = v.w0[:, :F]
    v.wt0[rows(c, HC), FR : FR + F] = v.w0[:, F:]
    pl.semaphore_wait(barrier, NDEV - 1)

    def halves(ref):
        size = ref.shape[0]
        first = -(-size // 16) * 8
        return ref.at[:first], ref.at[first:]

    def ag_send(g, src, buf, part):
        s, r = v.s_ag.at[g], v.r_ag.at[g]
        mine = halves(src)
        slot = halves(buf.at[ch])
        if CH == 4:
            send(mine[part], slot[part], s.at[part], r.at[part], peer(1))
            if part == 1:
                send(mine[1], slot[1], s.at[3], r.at[3], peer(2))
                send(mine[0], slot[0], s.at[2], r.at[2], peer(2))
        elif part == 1:
            for dd in reversed(range(1, CH)):
                send(src, buf.at[ch], s.at[dd], r.at[dd], peer(dd))

    def ag_blocks(g, src, buf, add):
        s, r = v.s_ag.at[g], v.r_ag.at[g]
        for part in range(2):
            add(ch, part, halves(src)[part])
        if CH == 4:
            x, y, z = (halves(buf.at[flip(ch, dd)]) for dd in (1, 2, 3))
            wait_bytes(x[0], r.at[0])
            send(x[0], x[0], s.at[4], r.at[4], peer(2))
            wait_bytes(y[1], r.at[3])
            send(y[1], y[1], s.at[5], r.at[5], peer(1))
            add(flip(ch, 1), 0, x[0])
            add(flip(ch, 2), 1, y[1])
            wait_bytes(x[1], r.at[1])
            add(flip(ch, 1), 1, x[1])
            wait_bytes(y[0], r.at[2])
            add(flip(ch, 2), 0, y[0])
            wait_bytes(z[0], r.at[4])
            add(flip(ch, 3), 0, z[0])
            wait_bytes(z[1], r.at[5])
            add(flip(ch, 3), 1, z[1])
        else:
            for dd in range(1, CH):
                wait_bytes(buf.at[flip(ch, dd)], r.at[dd])
                for part in range(2):
                    add(flip(ch, dd), part, halves(buf.at[flip(ch, dd)])[part])

    def ar_send(a):
        def one(i, carry):
            remote(
                v.arb.at[a, me], v.arb.at[a, me], v.s_ar.at[a], v.r_ar.at[a],
                device(lax.rem(me + i, NDEV)),
            ).start()
            return carry

        lax.fori_loop(1, NDEV, one, 0)
        drains.append(lambda: wait_bytes(v.arb.at[a, pl.ds(0, NDEV - 1)], v.s_ar.at[a]))

    def ar_put(a, vectors):
        at = 0
        for vec in vectors:
            for i in range(vec.shape[1] // LANES):
                v.arb[a, me, at : at + 1, :] = vec[:, i * LANES : (i + 1) * LANES]
                at += 1
        if at < 8:
            v.arb[a, me, at:, :] = jnp.zeros((8 - at, LANES), F32)

    def ar_wait(a):
        wait_bytes(v.arb.at[a, pl.ds(0, NDEV - 1)], v.r_ar.at[a])
        return jnp.sum(v.arb[a], axis=0)

    def vec(total, i):
        return cat([total[i * HV + j : i * HV + j + 1] for j in range(HV)], 1)

    for part in range(2):
        ag_send(0, v.xown, v.xg, part)
    for j in range(CH):
        send(adj_cols(j, 1 - k), v.adjb.at[1, j], v.s_adj.at[j], v.r_adj.at[j], sib)
    for l in range(L):
        if l:
            loads[l - 1].wait()
        ref = v.wt0 if l == 0 else v.wtr.at[l - 1]
        for dd in range(1, NC):
            block = ref.at[rows(c, HC), :]
            remote(block, block, v.s_w.at[l], v.r_w.at[l], (n, lax.rem(c + dd, NC))).start()
        drains.append(lambda ref=ref, l=l: wait_bytes(ref.at[pl.ds(0, (NC - 1) * HC)], v.s_w.at[l]))

    def column(row):
        return jnp.broadcast_to(row.astype(F32), (LANES, R)).T

    v.valid[...] = column(v.nm[...])
    v.counted[...] = column(v.lm[...] * v.nm[...])
    v.label[...] = column(v.lb[...])
    v.whp[...] = jnp.zeros(v.whp.shape, F32)
    v.whp[: d.C, :] = v.whd[...]
    v.biasp[...] = jnp.zeros(v.biasp.shape, F32)
    v.biasp[:, : d.C] = v.bias[...]

    def adj_block(j, side):
        block = v.adjb[side, j].astype(F32)
        v.abf[j, side * R : (side + 1) * R, :] = block.astype(BF16)
        v.at[side, j] = block.T.astype(BF16)

    def adj_own(j, carry):
        pltpu.make_async_copy(adj_cols(j, k), v.adjb.at[0, j], v.ld.at[L + j]).wait()
        adj_block(j, 0)
        return carry

    def adj_sib(j, carry):
        wait_bytes(v.adjb.at[1, j], v.r_adj.at[j])
        adj_block(j, 1)
        return carry

    lax.fori_loop(0, CH, adj_own, 0)
    lax.fori_loop(0, CH, adj_sib, 0)

    def wide(value):
        return cat([value] * HV, 1)

    RC = min(R // 2, 64)
    HALF = R // 2

    def activate(l, part):
        def chunk(i, carry):
            r = rows(i, RC)
            x = v.lin[r, :]
            square = x * x
            t = jnp.tanh(GELU_OUT * x * (1.0 + GELU_CUBE * square))
            half = 0.5 * (1.0 + t)
            act = x * half
            v.acts[l, r, :] = act
            v.gp[l, r, :] = half + (0.5 * GELU_OUT) * x * (1.0 - t * t) * (
                1.0 + (3.0 * GELU_CUBE) * square
            )
            masked = wide(v.valid[r, :]) * act
            return (
                carry[0] + jnp.sum(masked.reshape(RC // 8, 8, H), axis=0),
                carry[1] + jnp.sum((masked * act).reshape(RC // 8, 8, H), axis=0),
            )

        zero = jnp.zeros((8, H), F32)
        per = HALF // RC
        return lax.fori_loop(part * per, (part + 1) * per, chunk, (zero, zero))

    def over_rows(value):
        return jnp.sum(value, axis=0, keepdims=True)

    def keep_stats(l, total):
        count = jnp.max(v.count[0:1, :], axis=1, keepdims=True)
        mean = vec(total, 0) / count
        var = vec(total, 1) / count - mean * mean
        inverse = lax.rsqrt(var + NORM_EPS)
        gain, shift = v.npar[l, 0:1, :], v.npar[l, 1:2, :]
        v.vecs[l, 0:1, :] = mean
        v.vecs[l, 1:2, :] = inverse
        v.vecs[l, 2:3, :] = gain * inverse
        v.vecs[l, 3:4, :] = shift - mean * (gain * inverse)

    def finish(l, part_lin):
        sums = []
        for part in range(2):
            part_lin(part)
            sums.append(activate(l, part))
            if l < L - 1:
                ag_send(l + 1, v.acts.at[l], v.ag.at[l], part)
        message = [over_rows(sums[0][i] + sums[1][i]) for i in range(2)]
        if l == 0:
            message += [over_rows(v.valid[...]), over_rows(v.counted[...])]
        ar_put(l, message)
        ar_send(l)

    first_rows = len(drains)
    def add_first(chip, part, ref):
        high, low = split(ref[...])
        a = v.abf[chip]
        got = dot_t(cat([high, low], 1), cat([a, a], 1))
        first = -(-FR // 16) * 8
        r = slice(0, first) if part == 0 else slice(first, FR)
        seen = v.aggt[r, :]
        v.aggt[r, :] = seen + got

    v.aggt[...] = jnp.zeros((FR, 2 * R), F32)
    ag_blocks(0, v.xown, v.xg, add_first)
    v.part0[...] = v.aggt[:, R:]
    send(v.part0, v.part0r, v.s_sib.at[0], v.r_sib.at[0], sib)
    wait_bytes(v.wt0.at[pl.ds(0, (NC - 1) * HC)], v.r_w.at[0])
    v.w0h[...], v.w0l[...] = split(v.wt0[...])
    feature = lax.broadcasted_iota(jnp.int32, (FR, R), 0) < F
    v.in0h[:FR, :], v.in0l[:FR, :] = split(jnp.where(feature, v.xown[...], 0.0))
    wait_bytes(v.part0r, v.r_sib.at[0])
    total = v.aggt[:, :R] + v.part0r[...]
    degree = total[F : F + 1, :]
    v.in0h[FR:, :], v.in0l[FR:, :] = split(
        jnp.where(feature, total * (1.0 / jnp.maximum(degree, 1.0)), 0.0)
    )
    v.lin[...] = dot3((v.w0h[...], v.w0l[...]), (v.in0h[...], v.in0l[...])).T
    finish(0, lambda part: None)
    degree = column(degree)
    v.degree[...] = degree
    v.linked[...] = jnp.minimum(degree, 1.0)
    v.invdeg[...] = 1.0 / jnp.maximum(degree, 1.0)

    for l in range(1, L):
        wait_bytes(v.wtr.at[l - 1, pl.ds(0, (NC - 1) * HC)], v.r_w.at[l])
        v.wh[l - 1], v.wl[l - 1] = split(v.wtr[l - 1])
        total = ar_wait(l - 1)
        if l == 1:
            v.count[...] = total[2 * HV : 2 * HV + 2]
        keep_stats(l - 1, total)
        scale, shift = v.vecs[l - 1, 2:3, :], v.vecs[l - 1, 3:4, :]
        v.inh[l - 1, :, :H], v.inl[l - 1, :, :H] = split(v.acts[l - 1] * scale + shift)
        v.lin[...] = dot3_t(
            (v.inh[l - 1, :, :H], v.inl[l - 1, :, :H]), (v.wh[l - 1, :, :H], v.wl[l - 1, :, :H])
        )
        v.agg[...] = jnp.zeros((2 * R, H), F32)

        def add(chip, part, ref):
            high, low = split(ref[...])
            a = v.abf[chip, :, part * HALF : (part + 1) * HALF]
            v.agg[...] += dot(cat([a, a], 1), cat([high, low], 0))

        ag_blocks(l, v.acts.at[l - 1], v.ag.at[l - 1], add)
        v.parts[l - 1] = v.agg[R:, :]
        send(v.parts.at[l - 1], v.partr.at[l - 1], v.s_sib.at[l], v.r_sib.at[l], sib)
        wait_bytes(v.partr.at[l - 1], v.r_sib.at[l])

        def part_lin(part):
            r = slice(part * HALF, (part + 1) * HALF)
            agg = v.agg[r, :] + v.partr[l - 1, r, :]
            v.kept[l - 1, r, :] = agg
            v.inh[l - 1, r, H:], v.inl[l - 1, r, H:] = split(
                agg * wide(v.invdeg[r, :]) * scale + wide(v.linked[r, :]) * shift
            )
            v.lin[r, :] += dot3_t(
                (v.inh[l - 1, r, H:], v.inl[l - 1, r, H:]), (v.wh[l - 1, :, H:], v.wl[l - 1, :, H:])
            )

        finish(l, part_lin)

    for drain in drains[first_rows:]:
        drain()
    del drains[first_rows:]

    head = split(v.whp[...])
    lane = lax.broadcasted_iota(jnp.int32, (R, LANES), 1)
    onehot = jnp.where(lane.astype(F32) == v.label[...], 1.0, 0.0)
    real = lane < d.C
    counted = v.counted[...]
    label_count = jnp.max(v.count[1:2, :], axis=1, keepdims=True)
    keep_stats(L - 1, ar_wait(L - 1))
    last = split(v.acts[L - 1] * v.vecs[L - 1, 2:3, :] + v.vecs[L - 1, 3:4, :])
    logits = dot3_t(last, head) + v.biasp[...]
    top = jnp.max(jnp.where(real, logits, -3.0e38), axis=1, keepdims=True)
    moved = logits - top
    power = jnp.where(real, jnp.exp(moved), 0.0)
    power_sum = jnp.sum(power, axis=1, keepdims=True)
    g_logits = counted * (power / power_sum - onehot) / label_count
    gl_split = split(g_logits)
    v.gout[...] = dot3(gl_split, head)

    def last_sums():
        mean, inverse = v.vecs[L - 1, 0:1, :], v.vecs[L - 1, 1:2, :]

        def chunk(i, carry):
            r = rows(i, RC)
            g = v.gout[r, :]
            normed = (v.acts[L - 1, r, :] - mean) * inverse
            return (
                carry[0] + jnp.sum((g * normed).reshape(RC // 8, 8, H), axis=0),
                carry[1] + jnp.sum(g.reshape(RC // 8, 8, H), axis=0),
            )

        zero = jnp.zeros((8, H), F32)
        return [over_rows(s) for s in lax.fori_loop(0, R // RC, chunk, (zero, zero))]

    ar_put(3, last_sums())
    ar_send(3)
    logp = moved - jnp.log(power_sum)
    rows_loss = jnp.sum(jnp.where(real, onehot * logp, 0.0), axis=1, keepdims=True) * counted
    ar_put(6, [-over_rows(rows_loss), over_rows(g_logits)])
    ar_send(6)
    head_grad = dot3(split(g_logits.T[:CR, :]), last)
    HT = d.HT
    for t in range(HT):
        i, j = t // HV, t % HV
        v.hg[t] = head_grad[8 * i : 8 * i + 8, j * LANES : (j + 1) * LANES]

    def others(index, size, ref_of, init):
        return lax.fori_loop(1, size, lambda i, s: s + ref_of(lax.rem(index + i, size)), init)

    def head_scatter(i, carry):
        t = lax.rem(me + i, NDEV)

        def go():
            remote(v.hg.at[t], v.hrecv.at[me], v.s_h.at[0], v.r_h.at[0], device(t)).start()

        either(HT == NDEV, t < HT, go)
        return carry

    lax.fori_loop(1, NDEV, head_scatter, 0)
    drains.append(
        lambda: either(
            HT == NDEV,
            me < HT,
            lambda: wait_bytes(v.hrecv.at[pl.ds(0, HT - 1)], v.s_h.at[0]),
            lambda: wait_bytes(v.hrecv.at[pl.ds(0, HT)], v.s_h.at[0]),
        )
    )

    def head_gather():
        def go():
            wait_bytes(v.hrecv.at[pl.ds(0, NDEV - 1)], v.r_h.at[0])
            v.hfin[me] = others(me, NDEV, lambda s: v.hrecv[s], v.hg[me])

            def one(i, carry):
                remote(
                    v.hfin.at[me], v.hfin.at[me], v.s_h.at[1], v.r_h.at[1],
                    device(lax.rem(me + i, NDEV)),
                ).start()
                return carry

            lax.fori_loop(1, NDEV, one, 0)

        either(HT == NDEV, me < HT, go)
        drains.append(
            lambda: either(
                HT == NDEV,
                me < HT,
                lambda: wait_bytes(v.hrecv.at[pl.ds(0, NDEV - 1)], v.s_h.at[1]),
            )
        )

    def cols_send(i):
        for dd in range(1, NC):
            t = lax.rem(c + dd, NC)
            remote(v.dwb.at[i, t], v.zrecv.at[i, c], v.s_z.at[i], v.r_z.at[i], (n, t)).start()
        drains.append(lambda: wait_bytes(v.zrecv.at[i, pl.ds(0, NC - 1)], v.s_z.at[i]))

    def nodes_send(i):
        wait_bytes(v.zrecv.at[i, pl.ds(0, NC - 1)], v.r_z.at[i])
        v.zs[i] = others(c, NC, lambda s: v.zrecv[i, s], v.dwb[i, c])

        def one(j, carry):
            t = lax.rem(n + j, NN)
            either(
                PPC == NN,
                t < PPC,
                lambda: remote(
                    v.zs.at[i, rows(t, RPP), :], v.nrecv.at[i, n], v.s_n.at[i], v.r_n.at[i], (t, c)
                ).start(),
            )
            return carry

        lax.fori_loop(1, NN, one, 0)
        drains.append(
            lambda: either(
                PPC == NN,
                n < PPC,
                lambda: wait_bytes(v.nrecv.at[i, pl.ds(0, PPC - 1)], v.s_n.at[i]),
                lambda: wait_bytes(v.nrecv.at[i, pl.ds(0, PPC)], v.s_n.at[i]),
            )
        )

    def pieces_out(i, fin, piece):
        fin[rows(n, RPP), :] = piece
        square = jnp.sum((piece * piece).reshape(RPP // 8, 8, piece.shape[1]), axis=0)
        v.sq[...] += jnp.sum(square, axis=1, keepdims=True)

        def one(j, carry):
            block = fin.at[rows(n, RPP), :]
            remote(block, block, v.s_f.at[i], v.r_f.at[i], (lax.rem(n + j, NN), c)).start()
            return carry

        lax.fori_loop(1, NN, one, 0)

    def pieces_drain(i, like):
        drains.append(
            lambda: either(
                PPC == NN, n < PPC, lambda: wait_bytes(like.at[pl.ds(0, NN - 1)], v.s_f.at[i])
            )
        )

    def nodes_gather(i):
        def go():
            wait_bytes(v.nrecv.at[i, pl.ds(0, NN - 1)], v.r_n.at[i])
            piece = others(n, NN, lambda s: v.nrecv[i, s], v.zs[i, rows(n, RPP), :])
            pieces_out(i, v.fin.at[i], piece)

        either(PPC == NN, n < PPC, go)
        pieces_drain(i, v.nrecv.at[i])

    v.sq[...] = jnp.zeros((8, LANES), F32)

    def linear_grad(l, a):
        total = ar_wait(a)
        g_gain, g_shift = vec(total, 0), vec(total, 1)
        v.gn[l, 0:1, :] = g_gain
        v.gn[l, 1:2, :] = g_shift
        mean, inverse, scale = v.vecs[l, 0:1, :], v.vecs[l, 1:2, :], v.vecs[l, 2:3, :]
        count = jnp.max(v.count[0:1, :], axis=1, keepdims=True)
        by_one = scale * g_shift / count
        by_normed = scale * g_gain / count

        def chunk(i, carry):
            r = rows(i, RC)
            normed = (v.acts[l, r, :] - mean) * inverse
            g_active = scale * v.gout[r, :] - wide(v.valid[r, :]) * (by_one + normed * by_normed)
            g_linear = v.gp[l, r, :] * g_active
            v.lin[r, :] = g_linear
            v.glh[r, :], v.gll[r, :] = split(g_linear)
            return carry

        lax.fori_loop(0, R // RC, chunk, 0)

    for l in (2, 1):
        g = l - 1
        linear_grad(l, 5 - l)
        gl = (v.glh[...], v.gll[...])
        back = v.ag.at[2 - l]
        v.spread[...] = dot3(gl, (v.wh[g, :, H:], v.wl[g, :, H:])) * wide(v.invdeg[...])
        v.spreads[g] = v.spread[...]
        send(v.spreads.at[g], v.spreadr.at[g], v.s_sib.at[L + g], v.r_sib.at[L + g], sib)
        if g == 0:
            for drain in scatter_drains:
                drain()
        own = cat(list(split(v.spread[...])), 0)
        for dd in reversed(range(CH)):
            t = v.at[0, flip(ch, dd)]
            v.out[dd] = dot(cat([t, t], 1), own)
        wait_bytes(v.spreadr.at[g], v.r_sib.at[L + g])
        other = cat(list(split(v.spreadr[g])), 0)

        def complete(dd):
            t = v.at[1, flip(ch, dd)]
            v.out[dd] += dot(cat([t, t], 1), other)

        s, r = v.s_rs.at[g], v.r_rs.at[g]
        kept_drains, drains = drains, []
        if CH == 4:
            x, y, z = (halves(v.out.at[dd]) for dd in (1, 2, 3))
            from_x, from_y, via = (halves(back.at[i]) for i in range(3))
            complete(3)
            send(z[0], via[0], s.at[0], r.at[0], peer(1))
            send(z[1], via[1], s.at[1], r.at[1], peer(2))
            complete(1)
            send(x[0], from_x[0], s.at[2], r.at[2], peer(1))
            complete(2)
            send(y[1], from_y[1], s.at[3], r.at[3], peer(2))
            complete(0)
            wait_bytes(via[0], r.at[0])
            y[0][...] += via[0][...]
            send(y[0], from_y[0], s.at[5], r.at[5], peer(2))
            wait_bytes(via[1], r.at[1])
            x[1][...] += via[1][...]
            send(x[1], from_x[1], s.at[4], r.at[4], peer(1))
        else:
            for dd in reversed(range(1, CH)):
                complete(dd)
                send(v.out.at[dd], back.at[dd], s.at[dd], r.at[dd], peer(dd))
            complete(0)
        scatter_drains, drains = drains, kept_drains

        v.gout[...] = dot3(gl, (v.wh[g, :, :H], v.wl[g, :, :H]))
        mean, inverse = v.vecs[g, 0:1, :], v.vecs[g, 1:2, :]

        def chunk(i, carry):
            r = rows(i, RC)
            self, spread, degree = v.gout[r, :], v.spread[r, :], wide(v.degree[r, :])
            normed = (v.acts[g, r, :] - mean) * inverse
            reached = (v.kept[g, r, :] - degree * mean) * inverse
            v.gout[r, :] = self + v.out[0, r, :]
            return (
                carry[0] + jnp.sum((self * normed + spread * reached).reshape(RC // 8, 8, H), axis=0),
                carry[1] + jnp.sum((self + spread * degree).reshape(RC // 8, 8, H), axis=0),
            )

        zero = jnp.zeros((8, H), F32)
        ar_put(6 - l, [over_rows(s) for s in lax.fori_loop(0, R // RC, chunk, (zero, zero))])
        ar_send(6 - l)
        if l == 1:
            nodes_send(1)
        grad = dot3(split(v.lin[...].T), (v.inh[g], v.inl[g]))
        for t in range(NC):
            v.dwb[g, t] = grad[t * HC : (t + 1) * HC, :]
        cols_send(g)
        if l == 1:
            head_gather()
        if CH == 4:
            for half, i in ((from_x[0], 2), (from_y[1], 3), (from_y[0], 5), (from_x[1], 4)):
                wait_bytes(half, r.at[i])
            v.gout[...] += back[0] + back[1]
        else:
            for dd in range(1, CH):
                wait_bytes(back.at[dd], r.at[dd])
                v.gout[...] += back[dd]
    drains += scatter_drains

    linear_grad(0, 5)
    grad = dot3_t(split(v.lin[...].T), (v.in0h[...], v.in0l[...]))
    for t in range(NC):
        v.d0[t] = grad[t * HC : (t + 1) * HC, :]

    def first_scatter(i, carry):
        tn, tc = device(lax.rem(me + i, NDEV))
        either(
            PPC == NN,
            tn < PPC,
            lambda: remote(
                v.d0.at[tc, rows(tn, RPP), :], v.recv0.at[me], v.s_0.at[0], v.r_0.at[0], (tn, tc)
            ).start(),
        )
        return carry

    lax.fori_loop(1, NDEV, first_scatter, 0)
    drains.append(
        lambda: either(
            PPC == NN,
            n < PPC,
            lambda: wait_bytes(v.recv0.at[pl.ds(0, PPC * NC - 1)], v.s_0.at[0]),
            lambda: wait_bytes(v.recv0.at[pl.ds(0, PPC * NC)], v.s_0.at[0]),
        )
    )
    nodes_send(0)
    nodes_gather(1)
    nodes_gather(0)

    def first_gather():
        wait_bytes(v.recv0.at[pl.ds(0, NDEV - 1)], v.r_0.at[0])
        piece = others(me, NDEV, lambda s: v.recv0[s], v.d0[c, rows(n, RPP), :])
        pieces_out(L - 1, v.fin0, piece)

    either(PPC == NN, n < PPC, first_gather)
    pieces_drain(L - 1, v.recv0)
    ar_put(7, [over_rows(v.sq[...])])
    ar_send(7)

    total = ar_wait(6)
    bias_grad = total[1:2]
    v.misc[...] = jnp.zeros((8, LANES), F32)
    v.misc[0:1, :] = total[0:1]
    v.misc[1:2, :] = v.count[1:2, :]
    v.misc[3:4, :] = bias_grad

    def fin_wait(i, fin):
        either(
            PPC == NN,
            n < PPC,
            lambda: wait_bytes(fin.at[pl.ds(0, (PPC - 1) * RPP), :], v.r_f.at[i]),
            lambda: wait_bytes(fin.at[pl.ds(0, PPC * RPP), :], v.r_f.at[i]),
        )

    either(
        HT == NDEV,
        me < HT,
        lambda: wait_bytes(v.hfin.at[pl.ds(0, HT - 1)], v.r_h.at[1]),
        lambda: wait_bytes(v.hfin.at[pl.ds(0, HT)], v.r_h.at[1]),
    )
    square = jnp.zeros((8, LANES), F32)
    for t in range(HT):
        i, j = t // HV, t % HV
        tile = v.hfin[t]
        v.gh[8 * i : 8 * i + 8, j * LANES : (j + 1) * LANES] = tile
        square += tile * tile
    replicated = over_rows(square) + bias_grad * bias_grad
    small = jnp.zeros((1, H), F32)
    for l in range(L):
        small += over_rows(v.gn[l] * v.gn[l])
    for j in range(HV):
        replicated += small[:, j * LANES : (j + 1) * LANES]

    for i in range(L - 1):
        fin_wait(i, v.fin.at[i])
        v.gr[i] = v.fin[i]
    total = ar_wait(7)
    squares = total[0:1, 0:1] + jnp.sum(replicated, axis=1, keepdims=True)
    norm = jnp.sqrt(squares)
    v.misc[2:3, :] = jnp.broadcast_to(norm, (1, LANES))
    v.misc[4:5, :] = jnp.broadcast_to(CLIP / jnp.maximum(norm, CLIP), (1, LANES))
    fin_wait(L - 1, v.fin0)
    v.g0[:, :F] = v.fin0[:, :F]
    v.g0[:, F:] = v.fin0[:, FR : FR + F]

    for drain in drains:
        drain()


def gradients(NN, NC, feat, adj, nm, lb, lm, w0, wr, npar, whd, bias):
    F, R = feat.shape
    C, H = whd.shape
    HC = w0.shape[0]
    CH, NDEV = NN // 2, NN * NC
    up = lambda size: -(-size // 8) * 8
    FR, CR = up(F + 1), up(C)
    RPP = max(8, HC // NN)
    HV = H // LANES
    d = types.SimpleNamespace(
        NN=NN, NC=NC, R=R, F=F, H=H, C=C, HC=HC, CH=CH, NDEV=NDEV, FR=FR, CR=CR, RPP=RPP,
        PPC=HC // RPP, HV=HV, HT=CR // 8 * HV,
    )
    dma = pltpu.SemaphoreType.DMA
    L = LAYERS
    scratch = {
        "xown": pltpu.VMEM((FR, R), F32),
        "xg": pltpu.VMEM((CH, FR, R), F32),
        "ag": pltpu.VMEM((L - 1, CH, R, H), F32),
        "acts": pltpu.VMEM((L, R, H), F32),
        "gp": pltpu.VMEM((L, R, H), F32),
        "adjb": pltpu.VMEM((2, CH, R, R), jnp.int32),
        "abf": pltpu.VMEM((CH, 2 * R, R), BF16),
        "at": pltpu.VMEM((2, CH, R, R), BF16),
        "wt0": pltpu.VMEM((H, 2 * FR), F32),
        "wtr": pltpu.VMEM((L - 1, H, 2 * H), F32),
        "w0h": pltpu.VMEM((H, 2 * FR), BF16),
        "w0l": pltpu.VMEM((H, 2 * FR), BF16),
        "wh": pltpu.VMEM((L - 1, H, 2 * H), BF16),
        "wl": pltpu.VMEM((L - 1, H, 2 * H), BF16),
        "whp": pltpu.VMEM((LANES, H), F32),
        "biasp": pltpu.VMEM((1, LANES), F32),
        "in0h": pltpu.VMEM((2 * FR, R), BF16),
        "in0l": pltpu.VMEM((2 * FR, R), BF16),
        "inh": pltpu.VMEM((L - 1, R, 2 * H), BF16),
        "inl": pltpu.VMEM((L - 1, R, 2 * H), BF16),
        "aggt": pltpu.VMEM((FR, 2 * R), F32),
        "part0": pltpu.VMEM((FR, R), F32),
        "part0r": pltpu.VMEM((FR, R), F32),
        "agg": pltpu.VMEM((2 * R, H), F32),
        "parts": pltpu.VMEM((L - 1, R, H), F32),
        "partr": pltpu.VMEM((L - 1, R, H), F32),
        "kept": pltpu.VMEM((L - 1, R, H), F32),
        "lin": pltpu.VMEM((R, H), F32),
        "gout": pltpu.VMEM((R, H), F32),
        "glh": pltpu.VMEM((R, H), BF16),
        "gll": pltpu.VMEM((R, H), BF16),
        "spread": pltpu.VMEM((R, H), F32),
        "spreads": pltpu.VMEM((L - 1, R, H), F32),
        "spreadr": pltpu.VMEM((L - 1, R, H), F32),
        "out": pltpu.VMEM((CH, R, H), F32),
        "valid": pltpu.VMEM((R, LANES), F32),
        "counted": pltpu.VMEM((R, LANES), F32),
        "label": pltpu.VMEM((R, LANES), F32),
        "degree": pltpu.VMEM((R, LANES), F32),
        "invdeg": pltpu.VMEM((R, LANES), F32),
        "linked": pltpu.VMEM((R, LANES), F32),
        "count": pltpu.VMEM((2, LANES), F32),
        "vecs": pltpu.VMEM((L, 8, H), F32),
        "sq": pltpu.VMEM((8, LANES), F32),
        "arb": pltpu.VMEM((8, NDEV, 8, LANES), F32),
        "dwb": pltpu.VMEM((L - 1, NC, HC, 2 * H), F32),
        "zrecv": pltpu.VMEM((L - 1, NC, HC, 2 * H), F32),
        "zs": pltpu.VMEM((L - 1, HC, 2 * H), F32),
        "nrecv": pltpu.VMEM((L - 1, NN, RPP, 2 * H), F32),
        "fin": pltpu.VMEM((L - 1, HC, 2 * H), F32),
        "d0": pltpu.VMEM((NC, HC, 2 * FR), F32),
        "recv0": pltpu.VMEM((NDEV, RPP, 2 * FR), F32),
        "fin0": pltpu.VMEM((HC, 2 * FR), F32),
        "hg": pltpu.VMEM((d.HT, 8, LANES), F32),
        "hrecv": pltpu.VMEM((NDEV, 8, LANES), F32),
        "hfin": pltpu.VMEM((d.HT, 8, LANES), F32),
        "ld": dma((L + CH,)),
        "s_adj": dma((CH,)),
        "r_adj": dma((CH,)),
        "s_ag": dma((L, max(CH, 6))),
        "r_ag": dma((L, max(CH, 6))),
        "s_sib": dma((2 * L - 1,)),
        "r_sib": dma((2 * L - 1,)),
        "s_w": dma((L,)),
        "r_w": dma((L,)),
        "s_ar": dma((8,)),
        "r_ar": dma((8,)),
        "s_rs": dma((L - 1, max(CH, 6))),
        "r_rs": dma((L - 1, max(CH, 6))),
        "s_z": dma((L - 1,)),
        "r_z": dma((L - 1,)),
        "s_n": dma((L - 1,)),
        "r_n": dma((L - 1,)),
        "s_f": dma((L,)),
        "r_f": dma((L,)),
        "s_0": dma((1,)),
        "r_0": dma((1,)),
        "s_h": dma((2,)),
        "r_h": dma((2,)),
    }
    ins = ["feat", "adj", "nm", "lb", "lm", "w0", "wr", "npar", "whd", "bias"]
    outs = ["g0", "gr", "gn", "gh", "misc"]
    d.names = ins + outs + list(scratch)
    vmem = pl.BlockSpec(memory_space=pltpu.VMEM)
    specs = [vmem] * len(ins)
    for name in ("adj", "wr"):
        specs[ins.index(name)] = pl.BlockSpec(memory_space=pl.ANY)
    return pl.pallas_call(
        functools.partial(step_kernel, d),
        out_shape=[
            jax.ShapeDtypeStruct(w0.shape, F32),
            jax.ShapeDtypeStruct(wr.shape, F32),
            jax.ShapeDtypeStruct(npar.shape, F32),
            jax.ShapeDtypeStruct((CR, H), F32),
            jax.ShapeDtypeStruct((8, LANES), F32),
        ],
        in_specs=specs,
        out_specs=[vmem] * len(outs),
        scratch_shapes=list(scratch.values()),
        compiler_params=pltpu.CompilerParams(
            collective_id=0, has_side_effects=True, vmem_limit_bytes=60 * 2**20
        ),
    )(feat, adj, nm, lb, lm, w0, wr, npar, whd, bias)


def adamw(weight, first, second, average, grad, rate):
    first = BETA_ONE * first + (1.0 - BETA_ONE) * grad
    second = BETA_TWO * second + (1.0 - BETA_TWO) * grad * grad
    fix_one = 1.0 - BETA_ONE**ADAM_STEP
    fix_two = 1.0 - BETA_TWO**ADAM_STEP
    update = first / fix_one / (jnp.sqrt(second / fix_two) + ADAM_EPS)
    weight = weight - rate * (update + DECAY * weight)
    average = AVERAGE * average + (1.0 - AVERAGE) * weight
    return (first, second, weight, average)


def update_kernel(*refs):
    grads, state, scalars, results = refs[:5], refs[5:25], refs[25:28], refs[28:]
    misc = grads[4]
    scale = misc[4:5, 0:1]
    for i in range(3):
        scalars[i][...] = misc[i : i + 1, 0:1]
    for group in range(5):
        weight, first, second, average = (state[group + 5 * i] for i in (0, 1, 2, 3))
        rate = RATE_SMALL if group in (2, 4) else RATE_MATRIX
        shape = weight.shape
        if group == 4:
            grad = misc[3:4, : shape[1]]
        elif group == 3:
            grad = grads[3][: shape[0], :]
        else:
            grad = grads[group][...]
        done = adamw(weight[...], first[...], second[...], average[...], grad * scale, rate)
        for ref, value in zip(results[4 * group : 4 * group + 4], done, strict=True):
            ref[...] = value


def local(
    nodes, cols, features, adjacency, node_mask, labels, label_mask, *state
):
    turn = (
        lambda a: a.T,
        lambda a: a.transpose(0, 2, 1),
        lambda a: a.transpose(1, 0, 2),
        lambda a: a.T,
        lambda a: a.reshape(1, -1),
    )
    back = turn[:4] + (lambda a: a.reshape(-1),)
    state = [turn[i % 5](a) for i, a in enumerate(state)]
    grads = gradients(
        nodes, cols, features[0].T, adjacency[0], node_mask, labels, label_mask, *state[:5]
    )
    outs = [jax.ShapeDtypeStruct((1, 1), F32)] * 3
    outs += [jax.ShapeDtypeStruct(a.shape, F32) for a in state[:5] for _ in range(4)]
    done = pl.pallas_call(update_kernel, out_shape=outs)(*grads, *state)
    return (
        *(a.reshape(()) for a in done[:3]),
        *(back[i // 4](a) for i, a in enumerate(done[3:])),
    )


def solution(mesh):
    rows, first, rest, all_of = P("cols", "nodes", None), P(None, "cols"), P(None, None, "cols"), P()
    state = [first, rest, all_of, all_of, all_of]
    return jax.shard_map(
        functools.partial(local, mesh.shape["nodes"], mesh.shape["cols"]),
        mesh=mesh,
        in_specs=(rows, rows) + (P("cols", "nodes"),) * 3 + tuple(state * 4),
        out_specs=(all_of,) * 3 + tuple(spec for spec in state for _ in range(4)),
        check_vma=False,
    )
```

time: 171 us -> 143 us (0.84)
  local copies, waits for them, and re-layouts: 25.2 us -> 1.55 us
  other arithmetic: 6.57 us -> 0 us
  Pallas kernels: 137 us -> 141 us
    unnamed x76 -> x1, local copies, waits for them, and re-layouts: 22.6 us -> 1.55 us
    add x5 -> x0, other arithmetic: 6.57 us -> none  [adamw(): average = AVERAGE * average + (1.0 - AVERAGE) * weight]
    pallas_call x0 -> x1, Pallas kernels: none -> 3.12 us  [local(): done = pl.pallas_call(update_kernel, out_shape=outs)(*grads, *state)]
where the time goes in v2:
time: 143 us
  Pallas kernels  141 us (99%)
  local copies, waits for them, and re-layouts  1.55 us (1%)
    pallas_call x1, Pallas kernels, gradients(): pl.pallas_call(functools.partial(step_kernel, d), out_shape=[jax.ShapeDty...  138 us
    pallas_call x1, Pallas kernels, local(): done = pl.pallas_call(update_kernel, out_shape=outs)(*grads, *state)  3.12 us

profile of v2, /device:TPU:0, one launch (start us, length us, event | category | flops | bytes accessed | tf_op | source)
XLA Modules:
  0.0 143.3 jit_solution(7087525053919554158)
XLA Ops:
  0.7 1.5 %copy.50 = f32[1,256,100]{1,2,0:T(8,128)} copy(f32[1,256,100]{1,0,2:T(1,128)} %param.25) | data formatting | bytes 204800
  2.2 137.9 %shard_map.416 = (f32[64,200]{1,0:T(8,128)}, f32[2,64,512]{2,1,0:T(8,128)}, f32[3,2,256]{2,1,0:T(2,128)}, f32[48,256]{1,0:T(8,128)}, f32[8,128]{1,0:T(8,128)}) custom-call(f32[100,256]{1,0:T(8,128)} %bitcast.52, s32[256,2048]{1,0:T(8,128)} %bitcast.49, s32[1,256]{1,0:T(1,128)} %refs_2_.1, s32[1,256]{1,0:T(1,128)} %refs_3_.1, s32[1,256]{1,0:T(1,128)} %refs_4_.1, ...), custom_call_target="tpu_custom_call" | custom-call | tf_op jit(solution)/shard_map/pallas_call | solution.py:819
  140.1 3.1 %shard_map.417 = (f32[1,1]{1,0:T(1,128)}, f32[1,1]{1,0:T(1,128)}, f32[1,1]{1,0:T(1,128)}, f32[64,200]{1,0:T(8,128)}, f32[64,200]{1,0:T(8,128)}, /*index=5*/f32[6...) custom-call(f32[64,200]{1,0:T(8,128)} %get-tuple-element.51.refs_0_,, ...), custom_call_target="tpu_custom_call" | custom-call | tf_op jit(solution)/shard_map/pallas_call | solution.py:886

commit v3 on v2

--- a/solution.py
+++ b/solution.py
@@ -77,7 +77,7 @@
 def step_kernel(d, *refs):
     v = types.SimpleNamespace(**dict(zip(d.names, refs, strict=True)))
     NN, NC, R, H, HC, CH, L = d.NN, d.NC, d.R, d.H, d.HC, d.CH, LAYERS
-    NDEV, RPP, PPC, HV, F, FR, CR = d.NDEV, d.RPP, d.PPC, d.HV, d.F, d.FR, d.CR
+    NDEV, RPP, PPC, PH, HV, F, FR, CR = d.NDEV, d.RPP, d.PPC, d.PH, d.HV, d.F, d.FR, d.CR
     n, c = lax.axis_index("nodes"), lax.axis_index("cols")
     me = n * NC + c
     ch, k = lax.div(n, 2), lax.rem(n, 2)
@@ -100,10 +100,17 @@
     def either(always, condition, fn, other=None):
         if always:
             fn()
-        else:
-            pl.when(condition)(fn)
-            if other is not None:
-                pl.when(jnp.logical_not(condition))(other)
+            return
+
+        @pl.when(condition)
+        def _():
+            fn()
+
+        if other is not None:
+
+            @pl.when(jnp.logical_not(condition))
+            def _():
+                other()
 
     barrier = pltpu.get_barrier_semaphore()
 
@@ -118,16 +125,26 @@
     def adj_cols(j, core):
         return v.adj.at[:, rows(j * 2 + core, R)]
 
-    loads = [pltpu.make_async_copy(v.wr.at[i], v.wtr.at[i, rows(c, HC), :], v.ld.at[i]) for i in range(L - 1)]
-    for copy in loads:
+    own_rows = rows(c, HC)
+    w_loads = [
+        pltpu.make_async_copy(v.wr.at[i], v.wtr.at[i, own_rows, :], v.ld.at[i]) for i in range(L - 1)
+    ]
+    small_loads = [
+        pltpu.make_async_copy(getattr(v, name), getattr(v, name + "_in"), v.ld.at[L - 1 + i])
+        for i, name in enumerate(d.small)
+    ]
+    for copy in small_loads + w_loads:
         copy.start()
+    base = L - 1 + len(d.small)
     for j in range(CH):
-        pltpu.make_async_copy(adj_cols(j, k), v.adjb.at[0, j], v.ld.at[L + j]).start()
-    v.xown[:F, :] = v.feat[...]
+        pltpu.make_async_copy(adj_cols(j, k), v.adjb.at[0, j], v.ld.at[base + j]).start()
+    for copy in small_loads:
+        copy.wait()
+    v.xown[:F, :] = v.feat_in[...]
     v.xown[F:, :] = jnp.ones((FR - F, R), F32)
-    v.wt0[rows(c, HC), :] = jnp.zeros((HC, 2 * FR), F32)
-    v.wt0[rows(c, HC), :F] = v.w0[:, :F]
-    v.wt0[rows(c, HC), FR : FR + F] = v.w0[:, F:]
+    v.wt0[own_rows, :] = jnp.zeros((HC, 2 * FR), F32)
+    v.wt0[own_rows, :F] = v.w0_in[:, :F]
+    v.wt0[own_rows, FR : FR + F] = v.w0_in[:, F:]
     pl.semaphore_wait(barrier, NDEV - 1)
 
     def halves(ref):
@@ -148,16 +165,19 @@
             for dd in reversed(range(1, CH)):
                 send(src, buf.at[ch], s.at[dd], r.at[dd], peer(dd))
 
-    def ag_blocks(g, src, buf, add):
+    def ag_forward(g, buf):
         s, r = v.s_ag.at[g], v.r_ag.at[g]
-        for part in range(2):
-            add(ch, part, halves(src)[part])
         if CH == 4:
-            x, y, z = (halves(buf.at[flip(ch, dd)]) for dd in (1, 2, 3))
+            x, y = (halves(buf.at[flip(ch, dd)]) for dd in (1, 2))
             wait_bytes(x[0], r.at[0])
             send(x[0], x[0], s.at[4], r.at[4], peer(2))
             wait_bytes(y[1], r.at[3])
             send(y[1], y[1], s.at[5], r.at[5], peer(1))
+
+    def ag_blocks(g, buf, add):
+        r = v.r_ag.at[g]
+        if CH == 4:
+            x, y, z = (halves(buf.at[flip(ch, dd)]) for dd in (1, 2, 3))
             add(flip(ch, 1), 0, x[0])
             add(flip(ch, 2), 1, y[1])
             wait_bytes(x[1], r.at[1])
@@ -191,8 +211,8 @@
             for i in range(vec.shape[1] // LANES):
                 v.arb[a, me, at : at + 1, :] = vec[:, i * LANES : (i + 1) * LANES]
                 at += 1
-        if at < 8:
-            v.arb[a, me, at:, :] = jnp.zeros((8 - at, LANES), F32)
+        if at < 4:
+            v.arb[a, me, at:, :] = jnp.zeros((4 - at, LANES), F32)
 
     def ar_wait(a):
         wait_bytes(v.arb.at[a, pl.ds(0, NDEV - 1)], v.r_ar.at[a])
@@ -203,44 +223,74 @@
 
     for part in range(2):
         ag_send(0, v.xown, v.xg, part)
+
+    def w_ref(l):
+        return v.wt0 if l == 0 else v.wtr.at[l - 1]
+
+    def w_half(l, dd, core):
+        at = lax.rem(c + dd, NC) * HC + core * (HC // 2)
+        return w_ref(l).at[pl.ds(pl.multiple_of(at, HC // 2), HC // 2), :]
+
+    def w_send(l):
+        block = w_half(l, 0, k)
+        for dd in range(1, NC):
+            send(block, block, v.s_w.at[l, dd], v.r_w.at[l, dd], (n, lax.rem(c + dd, NC)))
+
+    def w_pass(l):
+        for dd in range(1, NC):
+            block = w_half(l, NC - dd, k)
+            wait_bytes(block, v.r_w.at[l, dd])
+            send(block, block, v.s_wp.at[l, dd], v.r_wp.at[l, dd], sib)
+
+    def w_wait(l):
+        for dd in range(1, NC):
+            wait_bytes(w_half(l, NC - dd, 1 - k), v.r_wp.at[l, dd])
+
+    w_send(0)
     for j in range(CH):
         send(adj_cols(j, 1 - k), v.adjb.at[1, j], v.s_adj.at[j], v.r_adj.at[j], sib)
-    for l in range(L):
-        if l:
-            loads[l - 1].wait()
-        ref = v.wt0 if l == 0 else v.wtr.at[l - 1]
-        for dd in range(1, NC):
-            block = ref.at[rows(c, HC), :]
-            remote(block, block, v.s_w.at[l], v.r_w.at[l], (n, lax.rem(c + dd, NC))).start()
-        drains.append(lambda ref=ref, l=l: wait_bytes(ref.at[pl.ds(0, (NC - 1) * HC)], v.s_w.at[l]))
+    w_loads[0].wait()
+    w_send(1)
+    for copy in w_loads[1:]:
+        copy.wait()
 
     def column(row):
         return jnp.broadcast_to(row.astype(F32), (LANES, R)).T
 
-    v.valid[...] = column(v.nm[...])
-    v.counted[...] = column(v.lm[...] * v.nm[...])
-    v.label[...] = column(v.lb[...])
+    v.valid[...] = column(v.nm_in[...])
+    v.counted[...] = column(v.lm_in[...] * v.nm_in[...])
+    v.label[...] = column(v.lb_in[...])
     v.whp[...] = jnp.zeros(v.whp.shape, F32)
-    v.whp[: d.C, :] = v.whd[...]
+    v.whp[: d.C, :] = v.whd_in[...]
     v.biasp[...] = jnp.zeros(v.biasp.shape, F32)
-    v.biasp[:, : d.C] = v.bias[...]
-
-    def adj_block(j, side):
-        block = v.adjb[side, j].astype(F32)
-        v.abf[j, side * R : (side + 1) * R, :] = block.astype(BF16)
-        v.at[side, j] = block.T.astype(BF16)
+    v.biasp[:, : d.C] = v.bias_in[...]
+    ar_put(
+        8,
+        [
+            jnp.sum(v.valid[...], axis=0, keepdims=True),
+            jnp.sum(v.counted[...], axis=0, keepdims=True),
+        ],
+    )
+    ar_send(8)
 
     def adj_own(j, carry):
-        pltpu.make_async_copy(adj_cols(j, k), v.adjb.at[0, j], v.ld.at[L + j]).wait()
-        adj_block(j, 0)
+        pltpu.make_async_copy(adj_cols(j, k), v.adjb.at[0, j], v.ld.at[base + j]).wait()
+        v.abf[j, :R, :] = v.adjb[0, j].astype(F32).astype(BF16)
         return carry
 
     def adj_sib(j, carry):
         wait_bytes(v.adjb.at[1, j], v.r_adj.at[j])
-        adj_block(j, 1)
+        v.abf[j, R:, :] = v.adjb[1, j].astype(F32).astype(BF16)
         return carry
 
+    def adj_turn(j, carry):
+        for side in range(2):
+            v.at[side, j] = v.adjb[side, j].astype(F32).T.astype(BF16)
+        return carry
+
     lax.fori_loop(0, CH, adj_own, 0)
+    first_rows = len(drains)
+    ag_forward(0, v.xg)
     lax.fori_loop(0, CH, adj_sib, 0)
 
     def wide(value):
@@ -279,7 +329,7 @@
         mean = vec(total, 0) / count
         var = vec(total, 1) / count - mean * mean
         inverse = lax.rsqrt(var + NORM_EPS)
-        gain, shift = v.npar[l, 0:1, :], v.npar[l, 1:2, :]
+        gain, shift = v.npar_in[l, 0:1, :], v.npar_in[l, 1:2, :]
         v.vecs[l, 0:1, :] = mean
         v.vecs[l, 1:2, :] = inverse
         v.vecs[l, 2:3, :] = gain * inverse
@@ -292,13 +342,9 @@
             sums.append(activate(l, part))
             if l < L - 1:
                 ag_send(l + 1, v.acts.at[l], v.ag.at[l], part)
-        message = [over_rows(sums[0][i] + sums[1][i]) for i in range(2)]
-        if l == 0:
-            message += [over_rows(v.valid[...]), over_rows(v.counted[...])]
-        ar_put(l, message)
+        ar_put(l, [over_rows(sums[0][i] + sums[1][i]) for i in range(2)])
         ar_send(l)
 
-    first_rows = len(drains)
     def add_first(chip, part, ref):
         high, low = split(ref[...])
         a = v.abf[chip]
@@ -309,14 +355,17 @@
         v.aggt[r, :] = seen + got
 
     v.aggt[...] = jnp.zeros((FR, 2 * R), F32)
-    ag_blocks(0, v.xown, v.xg, add_first)
+    for part in range(2):
+        add_first(ch, part, halves(v.xown)[part])
+    w_pass(0)
+    ag_blocks(0, v.xg, add_first)
     v.part0[...] = v.aggt[:, R:]
-    send(v.part0, v.part0r, v.s_sib.at[0], v.r_sib.at[0], sib)
-    wait_bytes(v.wt0.at[pl.ds(0, (NC - 1) * HC)], v.r_w.at[0])
+    send(v.part0, v.part0r, v.s_sib.at[0, 0], v.r_sib.at[0, 0], sib)
+    w_wait(0)
     v.w0h[...], v.w0l[...] = split(v.wt0[...])
     feature = lax.broadcasted_iota(jnp.int32, (FR, R), 0) < F
     v.in0h[:FR, :], v.in0l[:FR, :] = split(jnp.where(feature, v.xown[...], 0.0))
-    wait_bytes(v.part0r, v.r_sib.at[0])
+    wait_bytes(v.part0r, v.r_sib.at[0, 0])
     total = v.aggt[:, :R] + v.part0r[...]
     degree = total[F : F + 1, :]
     v.in0h[FR:, :], v.in0l[FR:, :] = split(
@@ -328,34 +377,43 @@
     v.degree[...] = degree
     v.linked[...] = jnp.minimum(degree, 1.0)
     v.invdeg[...] = 1.0 / jnp.maximum(degree, 1.0)
+    v.count[...] = ar_wait(8)[0:2]
 
     for l in range(1, L):
-        wait_bytes(v.wtr.at[l - 1, pl.ds(0, (NC - 1) * HC)], v.r_w.at[l])
+        if l == 1:
+            lax.fori_loop(0, CH, adj_turn, 0)
+        w_pass(l)
+        ag_forward(l, v.ag.at[l - 1])
+        w_wait(l)
         v.wh[l - 1], v.wl[l - 1] = split(v.wtr[l - 1])
         total = ar_wait(l - 1)
-        if l == 1:
-            v.count[...] = total[2 * HV : 2 * HV + 2]
+        if l < L - 1:
+            w_send(l + 1)
         keep_stats(l - 1, total)
         scale, shift = v.vecs[l - 1, 2:3, :], v.vecs[l - 1, 3:4, :]
         v.inh[l - 1, :, :H], v.inl[l - 1, :, :H] = split(v.acts[l - 1] * scale + shift)
         v.lin[...] = dot3_t(
             (v.inh[l - 1, :, :H], v.inl[l - 1, :, :H]), (v.wh[l - 1, :, :H], v.wl[l - 1, :, :H])
         )
-        v.agg[...] = jnp.zeros((2 * R, H), F32)
 
         def add(chip, part, ref):
             high, low = split(ref[...])
             a = v.abf[chip, :, part * HALF : (part + 1) * HALF]
             v.agg[...] += dot(cat([a, a], 1), cat([high, low], 0))
 
-        ag_blocks(l, v.acts.at[l - 1], v.ag.at[l - 1], add)
-        v.parts[l - 1] = v.agg[R:, :]
-        send(v.parts.at[l - 1], v.partr.at[l - 1], v.s_sib.at[l], v.r_sib.at[l], sib)
-        wait_bytes(v.partr.at[l - 1], v.r_sib.at[l])
+        high, low = split(v.acts[l - 1])
+        a = v.abf[ch]
+        v.agg[...] = dot(cat([a, a], 1), cat([high, low], 0))
+        ag_blocks(l, v.ag.at[l - 1], add)
+        parts, partr = halves(v.parts.at[l - 1]), halves(v.partr.at[l - 1])
+        for part in range(2):
+            parts[part][...] = v.agg[R + part * HALF : R + (part + 1) * HALF, :]
+            send(parts[part], partr[part], v.s_sib.at[l, part], v.r_sib.at[l, part], sib)
 
         def part_lin(part):
             r = slice(part * HALF, (part + 1) * HALF)
-            agg = v.agg[r, :] + v.partr[l - 1, r, :]
+            wait_bytes(partr[part], v.r_sib.at[l, part])
+            agg = v.agg[r, :] + partr[part][...]
             v.kept[l - 1, r, :] = agg
             v.inh[l - 1, r, H:], v.inl[l - 1, r, H:] = split(
                 agg * wide(v.invdeg[r, :]) * scale + wide(v.linked[r, :]) * shift
@@ -459,64 +517,75 @@
             )
         )
 
+    def sibling_send(i):
+        send(v.dwb.at[i, 1 - k], v.dwr.at[i], v.s_d.at[i], v.r_d.at[i], sib)
+
     def cols_send(i):
+        wait_bytes(v.dwr.at[i], v.r_d.at[i])
+        v.dwb[i, k] += v.dwr[i]
         for dd in range(1, NC):
             t = lax.rem(c + dd, NC)
-            remote(v.dwb.at[i, t], v.zrecv.at[i, c], v.s_z.at[i], v.r_z.at[i], (n, t)).start()
+            remote(v.dwb.at[i, k, t], v.zrecv.at[i, c], v.s_z.at[i], v.r_z.at[i], (n, t)).start()
         drains.append(lambda: wait_bytes(v.zrecv.at[i, pl.ds(0, NC - 1)], v.s_z.at[i]))
 
     def nodes_send(i):
         wait_bytes(v.zrecv.at[i, pl.ds(0, NC - 1)], v.r_z.at[i])
-        v.zs[i] = others(c, NC, lambda s: v.zrecv[i, s], v.dwb[i, c])
+        v.zs[i] = others(c, NC, lambda s: v.zrecv[i, s], v.dwb[i, k, c])
 
         def one(j, carry):
-            t = lax.rem(n + j, NN)
+            t = lax.rem(ch + j, CH)
             either(
-                PPC == NN,
-                t < PPC,
+                PH == CH,
+                t < PH,
                 lambda: remote(
-                    v.zs.at[i, rows(t, RPP), :], v.nrecv.at[i, n], v.s_n.at[i], v.r_n.at[i], (t, c)
+                    v.zs.at[i, rows(t, RPP), :], v.nrecv.at[i, ch], v.s_n.at[i], v.r_n.at[i],
+                    (t * 2 + k, c),
                 ).start(),
             )
             return carry
 
+        lax.fori_loop(1, CH, one, 0)
+        drains.append(
+            lambda: either(
+                PH == CH,
+                ch < PH,
+                lambda: wait_bytes(v.zs.at[i, pl.ds(0, (PH - 1) * RPP), :], v.s_n.at[i]),
+                lambda: wait_bytes(v.zs.at[i, pl.ds(0, PH * RPP), :], v.s_n.at[i]),
+            )
+        )
+
+    def pieces_out(i, fin, at, piece):
+        mine = pl.ds(pl.multiple_of(at, RPP), RPP)
+        fin[mine, :] = piece
+        square = jnp.sum((piece * piece).reshape(RPP // 8, 8, piece.shape[1]), axis=0)
+        v.sq[...] += jnp.sum(square, axis=1, keepdims=True)
+
+        def one(j, carry):
+            block = fin.at[mine, :]
+            remote(block, block, v.s_f.at[i], v.r_f.at[i], (lax.rem(n + j, NN), c)).start()
+            return carry
+
         lax.fori_loop(1, NN, one, 0)
+
+    def pieces_drain(i, fin):
         drains.append(
             lambda: either(
                 PPC == NN,
-                n < PPC,
-                lambda: wait_bytes(v.nrecv.at[i, pl.ds(0, PPC - 1)], v.s_n.at[i]),
-                lambda: wait_bytes(v.nrecv.at[i, pl.ds(0, PPC)], v.s_n.at[i]),
+                n < PPC if i == L - 1 else ch < PH,
+                lambda: lax.fori_loop(
+                    1, NN, lambda j, carry: (wait_bytes(fin.at[pl.ds(0, RPP), :], v.s_f.at[i]), carry)[1], 0
+                ),
             )
         )
 
-    def pieces_out(i, fin, piece):
-        fin[rows(n, RPP), :] = piece
-        square = jnp.sum((piece * piece).reshape(RPP // 8, 8, piece.shape[1]), axis=0)
-        v.sq[...] += jnp.sum(square, axis=1, keepdims=True)
-
-        def one(j, carry):
-            block = fin.at[rows(n, RPP), :]
-            remote(block, block, v.s_f.at[i], v.r_f.at[i], (lax.rem(n + j, NN), c)).start()
-            return carry
-
-        lax.fori_loop(1, NN, one, 0)
-
-    def pieces_drain(i, like):
-        drains.append(
-            lambda: either(
-                PPC == NN, n < PPC, lambda: wait_bytes(like.at[pl.ds(0, NN - 1)], v.s_f.at[i])
-            )
-        )
-
     def nodes_gather(i):
         def go():
-            wait_bytes(v.nrecv.at[i, pl.ds(0, NN - 1)], v.r_n.at[i])
-            piece = others(n, NN, lambda s: v.nrecv[i, s], v.zs[i, rows(n, RPP), :])
-            pieces_out(i, v.fin.at[i], piece)
-
-        either(PPC == NN, n < PPC, go)
-        pieces_drain(i, v.nrecv.at[i])
+            wait_bytes(v.nrecv.at[i, pl.ds(0, CH - 1)], v.r_n.at[i])
+            piece = others(ch, CH, lambda s: v.nrecv[i, s], v.zs[i, rows(ch, RPP), :])
+            pieces_out(i, v.fin.at[i], k * (HC // 2) + ch * RPP, piece)
+
+        either(PH == CH, ch < PH, go)
+        pieces_drain(i, v.fin.at[i])
 
     v.sq[...] = jnp.zeros((8, LANES), F32)
 
@@ -548,7 +617,7 @@
         back = v.ag.at[2 - l]
         v.spread[...] = dot3(gl, (v.wh[g, :, H:], v.wl[g, :, H:])) * wide(v.invdeg[...])
         v.spreads[g] = v.spread[...]
-        send(v.spreads.at[g], v.spreadr.at[g], v.s_sib.at[L + g], v.r_sib.at[L + g], sib)
+        send(v.spreads.at[g], v.spreadr.at[g], v.s_sib.at[L + g, 0], v.r_sib.at[L + g, 0], sib)
         if g == 0:
             for drain in scatter_drains:
                 drain()
@@ -556,7 +625,7 @@
         for dd in reversed(range(CH)):
             t = v.at[0, flip(ch, dd)]
             v.out[dd] = dot(cat([t, t], 1), own)
-        wait_bytes(v.spreadr.at[g], v.r_sib.at[L + g])
+        wait_bytes(v.spreadr.at[g], v.r_sib.at[L + g, 0])
         other = cat(list(split(v.spreadr[g])), 0)
 
         def complete(dd):
@@ -589,6 +658,8 @@
             complete(0)
         scatter_drains, drains = drains, kept_drains
 
+        if l == 1:
+            cols_send(1)
         v.gout[...] = dot3(gl, (v.wh[g, :, :H], v.wl[g, :, :H]))
         mean, inverse = v.vecs[g, 0:1, :], v.vecs[g, 1:2, :]
 
@@ -606,14 +677,16 @@
         zero = jnp.zeros((8, H), F32)
         ar_put(6 - l, [over_rows(s) for s in lax.fori_loop(0, R // RC, chunk, (zero, zero))])
         ar_send(6 - l)
+        grad = dot3(split(v.lin[...].T), (v.inh[g], v.inl[g]))
+        for t in range(NC):
+            for half in range(2):
+                at = t * HC + half * (HC // 2)
+                v.dwb[g, half, t] = grad[at : at + HC // 2, :]
+        sibling_send(g)
         if l == 1:
             nodes_send(1)
-        grad = dot3(split(v.lin[...].T), (v.inh[g], v.inl[g]))
-        for t in range(NC):
-            v.dwb[g, t] = grad[t * HC : (t + 1) * HC, :]
-        cols_send(g)
-        if l == 1:
             head_gather()
+            cols_send(0)
         if CH == 4:
             for half, i in ((from_x[0], 2), (from_y[1], 3), (from_y[0], 5), (from_x[1], 4)):
                 wait_bytes(half, r.at[i])
@@ -649,17 +722,17 @@
             lambda: wait_bytes(v.recv0.at[pl.ds(0, PPC * NC)], v.s_0.at[0]),
         )
     )
+    nodes_gather(1)
     nodes_send(0)
-    nodes_gather(1)
     nodes_gather(0)
 
     def first_gather():
         wait_bytes(v.recv0.at[pl.ds(0, NDEV - 1)], v.r_0.at[0])
         piece = others(me, NDEV, lambda s: v.recv0[s], v.d0[c, rows(n, RPP), :])
-        pieces_out(L - 1, v.fin0, piece)
+        pieces_out(L - 1, v.fin0, n * RPP, piece)
 
     either(PPC == NN, n < PPC, first_gather)
-    pieces_drain(L - 1, v.recv0)
+    pieces_drain(L - 1, v.fin0)
     ar_put(7, [over_rows(v.sq[...])])
     ar_send(7)
 
@@ -673,7 +746,7 @@
     def fin_wait(i, fin):
         either(
             PPC == NN,
-            n < PPC,
+            n < PPC if i == L - 1 else ch < PH,
             lambda: wait_bytes(fin.at[pl.ds(0, (PPC - 1) * RPP), :], v.r_f.at[i]),
             lambda: wait_bytes(fin.at[pl.ds(0, PPC * RPP), :], v.r_f.at[i]),
         )
@@ -724,10 +797,16 @@
     HV = H // LANES
     d = types.SimpleNamespace(
         NN=NN, NC=NC, R=R, F=F, H=H, C=C, HC=HC, CH=CH, NDEV=NDEV, FR=FR, CR=CR, RPP=RPP,
-        PPC=HC // RPP, HV=HV, HT=CR // 8 * HV,
+        PPC=HC // RPP, PH=HC // RPP // 2, HV=HV, HT=CR // 8 * HV,
     )
     dma = pltpu.SemaphoreType.DMA
     L = LAYERS
+    inputs = {
+        "feat": feat, "adj": adj, "nm": nm, "lb": lb, "lm": lm, "w0": w0, "wr": wr, "npar": npar,
+        "whd": whd, "bias": bias,
+    }
+    small = [name for name in inputs if name not in ("adj", "wr")]
+    d.small = small
     scratch = {
         "xown": pltpu.VMEM((FR, R), F32),
         "xg": pltpu.VMEM((CH, FR, R), F32),
@@ -773,11 +852,12 @@
         "count": pltpu.VMEM((2, LANES), F32),
         "vecs": pltpu.VMEM((L, 8, H), F32),
         "sq": pltpu.VMEM((8, LANES), F32),
-        "arb": pltpu.VMEM((8, NDEV, 8, LANES), F32),
-        "dwb": pltpu.VMEM((L - 1, NC, HC, 2 * H), F32),
-        "zrecv": pltpu.VMEM((L - 1, NC, HC, 2 * H), F32),
-        "zs": pltpu.VMEM((L - 1, HC, 2 * H), F32),
-        "nrecv": pltpu.VMEM((L - 1, NN, RPP, 2 * H), F32),
+        "arb": pltpu.VMEM((9, NDEV, 4, LANES), F32),
+        "dwb": pltpu.VMEM((L - 1, 2, NC, HC // 2, 2 * H), F32),
+        "dwr": pltpu.VMEM((L - 1, NC, HC // 2, 2 * H), F32),
+        "zrecv": pltpu.VMEM((L - 1, NC, HC // 2, 2 * H), F32),
+        "zs": pltpu.VMEM((L - 1, HC // 2, 2 * H), F32),
+        "nrecv": pltpu.VMEM((L - 1, CH, RPP, 2 * H), F32),
         "fin": pltpu.VMEM((L - 1, HC, 2 * H), F32),
         "d0": pltpu.VMEM((NC, HC, 2 * FR), F32),
         "recv0": pltpu.VMEM((NDEV, RPP, 2 * FR), F32),
@@ -785,17 +865,21 @@
         "hg": pltpu.VMEM((d.HT, 8, LANES), F32),
         "hrecv": pltpu.VMEM((NDEV, 8, LANES), F32),
         "hfin": pltpu.VMEM((d.HT, 8, LANES), F32),
-        "ld": dma((L + CH,)),
+        "ld": dma((L - 1 + len(small) + CH,)),
         "s_adj": dma((CH,)),
         "r_adj": dma((CH,)),
         "s_ag": dma((L, max(CH, 6))),
         "r_ag": dma((L, max(CH, 6))),
-        "s_sib": dma((2 * L - 1,)),
-        "r_sib": dma((2 * L - 1,)),
-        "s_w": dma((L,)),
-        "r_w": dma((L,)),
-        "s_ar": dma((8,)),
-        "r_ar": dma((8,)),
+        "s_sib": dma((2 * L - 1, 2)),
+        "r_sib": dma((2 * L - 1, 2)),
+        "s_w": dma((L, NC)),
+        "r_w": dma((L, NC)),
+        "s_wp": dma((L, NC)),
+        "r_wp": dma((L, NC)),
+        "s_d": dma((L - 1,)),
+        "r_d": dma((L - 1,)),
+        "s_ar": dma((9,)),
+        "r_ar": dma((9,)),
         "s_rs": dma((L - 1, max(CH, 6))),
         "r_rs": dma((L - 1, max(CH, 6))),
         "s_z": dma((L - 1,)),
@@ -809,13 +893,12 @@
         "s_h": dma((2,)),
         "r_h": dma((2,)),
     }
-    ins = ["feat", "adj", "nm", "lb", "lm", "w0", "wr", "npar", "whd", "bias"]
+    for name in small:
+        scratch[name + "_in"] = pltpu.VMEM(inputs[name].shape, inputs[name].dtype)
+    ins = list(inputs)
     outs = ["g0", "gr", "gn", "gh", "misc"]
     d.names = ins + outs + list(scratch)
     vmem = pl.BlockSpec(memory_space=pltpu.VMEM)
-    specs = [vmem] * len(ins)
-    for name in ("adj", "wr"):
-        specs[ins.index(name)] = pl.BlockSpec(memory_space=pl.ANY)
     return pl.pallas_call(
         functools.partial(step_kernel, d),
         out_shape=[
@@ -825,13 +908,13 @@
             jax.ShapeDtypeStruct((CR, H), F32),
             jax.ShapeDtypeStruct((8, LANES), F32),
         ],
-        in_specs=specs,
+        in_specs=[pl.BlockSpec(memory_space=pl.ANY)] * len(ins),
         out_specs=[vmem] * len(outs),
         scratch_shapes=list(scratch.values()),
         compiler_params=pltpu.CompilerParams(
             collective_id=0, has_side_effects=True, vmem_limit_bytes=60 * 2**20
         ),
-    )(feat, adj, nm, lb, lm, w0, wr, npar, whd, bias)
+    )(*inputs.values())
 
 
 def adamw(weight, first, second, average, grad, rate):

time: 143 us -> 112 us (0.78)
  Pallas kernels: 141 us -> 110 us
    pallas_call x1, Pallas kernels: 138 us -> 106 us  [gradients(): pl.pallas_call(functools.partial(step_kernel, d), out_shape=[jax.ShapeDty...]
where the time goes in v3:
time: 112 us
  Pallas kernels  110 us (98%)
  local copies, waits for them, and re-layouts  1.55 us (1%)
    pallas_call x1, Pallas kernels, gradients(): pl.pallas_call(functools.partial(step_kernel, d), out_shape=[jax.ShapeDty...  106 us
    pallas_call x1, Pallas kernels, local(): done = pl.pallas_call(update_kernel, out_shape=outs)(*grads, *state)  3.12 us

profile of v3, /device:TPU:0, one launch (start us, length us, event | category | flops | bytes accessed | tf_op | source)
XLA Modules:
  0.0 111.7 jit_solution(16270714895659012227)
XLA Ops:
  0.7 1.5 %copy.50 = f32[1,256,100]{1,2,0:T(8,128)} copy(f32[1,256,100]{1,0,2:T(1,128)} %param.25) | data formatting | bytes 204800
  2.2 106.4 %shard_map.416 = (f32[64,200]{1,0:T(8,128)}, f32[2,64,512]{2,1,0:T(8,128)}, f32[3,2,256]{2,1,0:T(2,128)}, f32[48,256]{1,0:T(8,128)}, f32[8,128]{1,0:T(8,128)}) custom-call(f32[100,256]{1,0:T(8,128)} %bitcast.52, s32[256,2048]{1,0:T(8,128)} %bitcast.49, s32[1,256]{1,0:T(1,128)} %refs_2_.1, s32[1,256]{1,0:T(1,128)} %refs_3_.1, s32[1,256]{1,0:T(1,128)} %refs_4_.1, ...), custom_call_target="tpu_custom_call" | custom-call | tf_op jit(solution)/shard_map/pallas_call | solution.py:902
  108.6 3.1 %shard_map.417 = (f32[1,1]{1,0:T(1,128)}, f32[1,1]{1,0:T(1,128)}, f32[1,1]{1,0:T(1,128)}, f32[64,200]{1,0:T(8,128)}, f32[64,200]{1,0:T(8,128)}, /*index=5*/f32[6...) custom-call(f32[64,200]{1,0:T(8,128)} %get-tuple-element.51.refs_0_,, ...), custom_call_target="tpu_custom_call" | custom-call | tf_op jit(solution)/shard_map/pallas_call | solution.py:969

commit v4 on v3

--- a/solution.py
+++ b/solution.py
@@ -130,7 +130,11 @@
         pltpu.make_async_copy(v.wr.at[i], v.wtr.at[i, own_rows, :], v.ld.at[i]) for i in range(L - 1)
     ]
     small_loads = [
-        pltpu.make_async_copy(getattr(v, name), getattr(v, name + "_in"), v.ld.at[L - 1 + i])
+        pltpu.make_async_copy(
+            v.feat.at[:, 0, :] if name == "feat" else getattr(v, name),
+            getattr(v, name + "_in"),
+            v.ld.at[L - 1 + i],
+        )
         for i, name in enumerate(d.small)
     ]
     for copy in small_loads + w_loads:
@@ -194,15 +198,29 @@
                 for part in range(2):
                     add(flip(ch, dd), part, halves(buf.at[flip(ch, dd)])[part])
 
-    def ar_send(a):
+    def to_others(start, at_once=False):
+        if at_once and NDEV <= 32:
+            for dc in [*reversed(range(1, NC)), 0]:
+                for dn in reversed(range(NN)):
+                    if dn or dc:
+                        tn, tc = lax.rem(n + dn, NN) if dn else n, lax.rem(c + dc, NC) if dc else c
+                        start((tn, tc), tn * NC + tc)
+            return
+
         def one(i, carry):
-            remote(
-                v.arb.at[a, me], v.arb.at[a, me], v.s_ar.at[a], v.r_ar.at[a],
-                device(lax.rem(me + i, NDEV)),
-            ).start()
+            t = lax.rem(me + i, NDEV)
+            start(device(t), t)
             return carry
 
         lax.fori_loop(1, NDEV, one, 0)
+
+    def ar_send(a, at_once=False):
+        to_others(
+            lambda dev, t: remote(
+                v.arb.at[a, me], v.arb.at[a, me], v.s_ar.at[a], v.r_ar.at[a], dev
+            ).start(),
+            at_once,
+        )
         drains.append(lambda: wait_bytes(v.arb.at[a, pl.ds(0, NDEV - 1)], v.s_ar.at[a]))
 
     def ar_put(a, vectors):
@@ -343,7 +361,7 @@
             if l < L - 1:
                 ag_send(l + 1, v.acts.at[l], v.ag.at[l], part)
         ar_put(l, [over_rows(sums[0][i] + sums[1][i]) for i in range(2)])
-        ar_send(l)
+        ar_send(l, l == L - 1)
 
     def add_first(chip, part, ref):
         high, low = split(ref[...])
@@ -461,7 +479,7 @@
         return [over_rows(s) for s in lax.fori_loop(0, R // RC, chunk, (zero, zero))]
 
     ar_put(3, last_sums())
-    ar_send(3)
+    ar_send(3, True)
     logp = moved - jnp.log(power_sum)
     rows_loss = jnp.sum(jnp.where(real, onehot * logp, 0.0), axis=1, keepdims=True) * counted
     ar_put(6, [-over_rows(rows_loss), over_rows(g_logits)])
@@ -589,11 +607,24 @@
 
     v.sq[...] = jnp.zeros((8, LANES), F32)
 
+    def fin_wait(i, fin):
+        either(
+            PPC == NN,
+            n < PPC if i == L - 1 else ch < PH,
+            lambda: wait_bytes(fin.at[pl.ds(0, (PPC - 1) * RPP), :], v.r_f.at[i]),
+            lambda: wait_bytes(fin.at[pl.ds(0, PPC * RPP), :], v.r_f.at[i]),
+        )
+
+    def give(i, src, dst):
+        copy = pltpu.make_async_copy(src, dst, v.s_out.at[i])
+        copy.start()
+        drains.append(copy.wait)
+
     def linear_grad(l, a):
         total = ar_wait(a)
         g_gain, g_shift = vec(total, 0), vec(total, 1)
-        v.gn[l, 0:1, :] = g_gain
-        v.gn[l, 1:2, :] = g_shift
+        v.gn_o[l, 0:1, :] = g_gain
+        v.gn_o[l, 1:2, :] = g_shift
         mean, inverse, scale = v.vecs[l, 0:1, :], v.vecs[l, 1:2, :], v.vecs[l, 2:3, :]
         count = jnp.max(v.count[0:1, :], axis=1, keepdims=True)
         by_one = scale * g_shift / count
@@ -658,8 +689,6 @@
             complete(0)
         scatter_drains, drains = drains, kept_drains
 
-        if l == 1:
-            cols_send(1)
         v.gout[...] = dot3(gl, (v.wh[g, :, :H], v.wl[g, :, :H]))
         mean, inverse = v.vecs[g, 0:1, :], v.vecs[g, 1:2, :]
 
@@ -683,10 +712,13 @@
                 at = t * HC + half * (HC // 2)
                 v.dwb[g, half, t] = grad[at : at + HC // 2, :]
         sibling_send(g)
+        if l == 2:
+            head_gather()
+        else:
+            nodes_send(1)
+        cols_send(g)
         if l == 1:
-            nodes_send(1)
-            head_gather()
-            cols_send(0)
+            nodes_gather(1)
         if CH == 4:
             for half, i in ((from_x[0], 2), (from_y[1], 3), (from_y[0], 5), (from_x[1], 4)):
                 wait_bytes(half, r.at[i])
@@ -702,18 +734,17 @@
     for t in range(NC):
         v.d0[t] = grad[t * HC : (t + 1) * HC, :]
 
-    def first_scatter(i, carry):
-        tn, tc = device(lax.rem(me + i, NDEV))
+    def first_scatter(dev, t):
+        tn, tc = dev
         either(
             PPC == NN,
             tn < PPC,
             lambda: remote(
-                v.d0.at[tc, rows(tn, RPP), :], v.recv0.at[me], v.s_0.at[0], v.r_0.at[0], (tn, tc)
+                v.d0.at[tc, rows(tn, RPP), :], v.recv0.at[me], v.s_0.at[0], v.r_0.at[0], dev
             ).start(),
         )
-        return carry
-
-    lax.fori_loop(1, NDEV, first_scatter, 0)
+
+    to_others(first_scatter, True)
     drains.append(
         lambda: either(
             PPC == NN,
@@ -722,7 +753,6 @@
             lambda: wait_bytes(v.recv0.at[pl.ds(0, PPC * NC)], v.s_0.at[0]),
         )
     )
-    nodes_gather(1)
     nodes_send(0)
     nodes_gather(0)
 
@@ -734,60 +764,49 @@
     either(PPC == NN, n < PPC, first_gather)
     pieces_drain(L - 1, v.fin0)
     ar_put(7, [over_rows(v.sq[...])])
-    ar_send(7)
+    ar_send(7, True)
 
     total = ar_wait(6)
     bias_grad = total[1:2]
-    v.misc[...] = jnp.zeros((8, LANES), F32)
-    v.misc[0:1, :] = total[0:1]
-    v.misc[1:2, :] = v.count[1:2, :]
-    v.misc[3:4, :] = bias_grad
-
-    def fin_wait(i, fin):
-        either(
-            PPC == NN,
-            n < PPC if i == L - 1 else ch < PH,
-            lambda: wait_bytes(fin.at[pl.ds(0, (PPC - 1) * RPP), :], v.r_f.at[i]),
-            lambda: wait_bytes(fin.at[pl.ds(0, PPC * RPP), :], v.r_f.at[i]),
-        )
-
+    v.misc_o[...] = jnp.zeros((8, LANES), F32)
+    v.misc_o[0:1, :] = total[0:1]
+    v.misc_o[1:2, :] = v.count[1:2, :]
+    v.misc_o[3:4, :] = bias_grad
     either(
         HT == NDEV,
         me < HT,
         lambda: wait_bytes(v.hfin.at[pl.ds(0, HT - 1)], v.r_h.at[1]),
         lambda: wait_bytes(v.hfin.at[pl.ds(0, HT)], v.r_h.at[1]),
     )
+    give(2, v.gn_o, v.gn)
+    give(3, v.hfin, v.gh)
     square = jnp.zeros((8, LANES), F32)
     for t in range(HT):
-        i, j = t // HV, t % HV
-        tile = v.hfin[t]
-        v.gh[8 * i : 8 * i + 8, j * LANES : (j + 1) * LANES] = tile
-        square += tile * tile
+        square += v.hfin[t] * v.hfin[t]
     replicated = over_rows(square) + bias_grad * bias_grad
     small = jnp.zeros((1, H), F32)
     for l in range(L):
-        small += over_rows(v.gn[l] * v.gn[l])
+        small += over_rows(v.gn_o[l] * v.gn_o[l])
     for j in range(HV):
         replicated += small[:, j * LANES : (j + 1) * LANES]
-
     for i in range(L - 1):
         fin_wait(i, v.fin.at[i])
-        v.gr[i] = v.fin[i]
+        give(5 + i, v.fin.at[i], v.gr.at[i])
     total = ar_wait(7)
     squares = total[0:1, 0:1] + jnp.sum(replicated, axis=1, keepdims=True)
     norm = jnp.sqrt(squares)
-    v.misc[2:3, :] = jnp.broadcast_to(norm, (1, LANES))
-    v.misc[4:5, :] = jnp.broadcast_to(CLIP / jnp.maximum(norm, CLIP), (1, LANES))
+    v.misc_o[2:3, :] = jnp.broadcast_to(norm, (1, LANES))
+    v.misc_o[4:5, :] = jnp.broadcast_to(CLIP / jnp.maximum(norm, CLIP), (1, LANES))
+    give(4, v.misc_o, v.misc)
     fin_wait(L - 1, v.fin0)
-    v.g0[:, :F] = v.fin0[:, :F]
-    v.g0[:, F:] = v.fin0[:, FR : FR + F]
+    give(0, v.fin0, v.g0)
 
     for drain in drains:
         drain()
 
 
 def gradients(NN, NC, feat, adj, nm, lb, lm, w0, wr, npar, whd, bias):
-    F, R = feat.shape
+    F, _, R = feat.shape
     C, H = whd.shape
     HC = w0.shape[0]
     CH, NDEV = NN // 2, NN * NC
@@ -892,24 +911,27 @@
         "r_0": dma((1,)),
         "s_h": dma((2,)),
         "r_h": dma((2,)),
+        "gn_o": pltpu.VMEM(npar.shape, F32),
+        "misc_o": pltpu.VMEM((8, LANES), F32),
+        "s_out": dma((L + 4,)),
     }
     for name in small:
-        scratch[name + "_in"] = pltpu.VMEM(inputs[name].shape, inputs[name].dtype)
+        shape = (F, R) if name == "feat" else inputs[name].shape
+        scratch[name + "_in"] = pltpu.VMEM(shape, inputs[name].dtype)
     ins = list(inputs)
     outs = ["g0", "gr", "gn", "gh", "misc"]
     d.names = ins + outs + list(scratch)
-    vmem = pl.BlockSpec(memory_space=pltpu.VMEM)
     return pl.pallas_call(
         functools.partial(step_kernel, d),
         out_shape=[
-            jax.ShapeDtypeStruct(w0.shape, F32),
+            jax.ShapeDtypeStruct((HC, 2 * FR), F32),
             jax.ShapeDtypeStruct(wr.shape, F32),
             jax.ShapeDtypeStruct(npar.shape, F32),
-            jax.ShapeDtypeStruct((CR, H), F32),
+            jax.ShapeDtypeStruct((d.HT, 8, LANES), F32),
             jax.ShapeDtypeStruct((8, LANES), F32),
         ],
         in_specs=[pl.BlockSpec(memory_space=pl.ANY)] * len(ins),
-        out_specs=[vmem] * len(outs),
+        out_specs=[pl.BlockSpec(memory_space=pl.ANY)] * len(outs),
         scratch_shapes=list(scratch.values()),
         compiler_params=pltpu.CompilerParams(
             collective_id=0, has_side_effects=True, vmem_limit_bytes=60 * 2**20
@@ -928,25 +950,48 @@
     return (first, second, weight, average)
 
 
+ORDER = (1, 0, 3, 2, 4)
+
+
 def update_kernel(*refs):
-    grads, state, scalars, results = refs[:5], refs[5:25], refs[25:28], refs[28:]
-    misc = grads[4]
+    far, scalars, far_out = refs[:25], refs[25:28], refs[28:48]
+    near, near_out, loaded, stored = refs[48:73], refs[73:93], refs[93], refs[94]
+    loads = [pltpu.make_async_copy(a, b, loaded.at[i]) for i, (a, b) in enumerate(zip(far, near, strict=True))]
+    stores = [pltpu.make_async_copy(a, b, stored.at[i]) for i, (a, b) in enumerate(zip(near_out, far_out, strict=True))]
+    loads[4].start()
+    for group in ORDER:
+        for i in ([] if group == 4 else [group]) + [5 + group + 5 * j for j in range(4)]:
+            loads[i].start()
+    loads[4].wait()
+    misc = near[4]
     scale = misc[4:5, 0:1]
     for i in range(3):
         scalars[i][...] = misc[i : i + 1, 0:1]
-    for group in range(5):
-        weight, first, second, average = (state[group + 5 * i] for i in (0, 1, 2, 3))
+    for group in ORDER:
+        for i in ([] if group == 4 else [group]) + [5 + group + 5 * j for j in range(4)]:
+            loads[i].wait()
+        weight, first, second, average = (near[5 + group + 5 * j] for j in range(4))
         rate = RATE_SMALL if group in (2, 4) else RATE_MATRIX
         shape = weight.shape
         if group == 4:
             grad = misc[3:4, : shape[1]]
         elif group == 3:
-            grad = grads[3][: shape[0], :]
+            wide = shape[1] // LANES
+            grad = cat(
+                [cat([near[3][wide * i + j] for j in range(wide)], 1) for i in range(near[3].shape[0] // wide)], 0
+            )[: shape[0]]
+        elif group == 0:
+            half = shape[1] // 2
+            at = near[0].shape[1] // 2
+            grad = cat([near[0][:, :half], near[0][:, at : at + half]], 1)
         else:
-            grad = grads[group][...]
+            grad = near[group][...]
         done = adamw(weight[...], first[...], second[...], average[...], grad * scale, rate)
-        for ref, value in zip(results[4 * group : 4 * group + 4], done, strict=True):
-            ref[...] = value
+        for i, value in enumerate(done):
+            near_out[4 * group + i][...] = value
+            stores[4 * group + i].start()
+    for store in stores:
+        store.wait()
 
 
 def local(
@@ -962,11 +1007,20 @@
     back = turn[:4] + (lambda a: a.reshape(-1),)
     state = [turn[i % 5](a) for i, a in enumerate(state)]
     grads = gradients(
-        nodes, cols, features[0].T, adjacency[0], node_mask, labels, label_mask, *state[:5]
+        nodes, cols, features.transpose(2, 0, 1), adjacency[0], node_mask, labels, label_mask, *state[:5]
     )
     outs = [jax.ShapeDtypeStruct((1, 1), F32)] * 3
     outs += [jax.ShapeDtypeStruct(a.shape, F32) for a in state[:5] for _ in range(4)]
-    done = pl.pallas_call(update_kernel, out_shape=outs)(*grads, *state)
+    far = pl.BlockSpec(memory_space=pl.ANY)
+    given = [*grads, *state]
+    done = pl.pallas_call(
+        update_kernel,
+        out_shape=outs,
+        in_specs=[far] * len(given),
+        out_specs=[pl.BlockSpec(memory_space=pltpu.VMEM)] * 3 + [far] * (len(outs) - 3),
+        scratch_shapes=[pltpu.VMEM(a.shape, F32) for a in [*given, *outs[3:]]]
+        + [pltpu.SemaphoreType.DMA((25,)), pltpu.SemaphoreType.DMA((20,))],
+    )(*given)
     return (
         *(a.reshape(()) for a in done[:3]),
         *(back[i // 4](a) for i, a in enumerate(done[3:])),

time: 112 us -> 103 us (0.920)
  Pallas kernels: 110 us -> 102 us
  local copies, waits for them, and re-layouts: 1.55 us -> 0 us
    pallas_call x1, Pallas kernels: 106 us -> 98.5 us  [gradients(): pl.pallas_call(functools.partial(step_kernel, d), out_shape=[jax.ShapeDty...]
    unnamed x1 -> x0, local copies, waits for them, and re-layouts: 1.55 us -> none
where the time goes in v4:
time: 103 us
  Pallas kernels  102 us (99%)
    pallas_call x1, Pallas kernels, gradients(): pl.pallas_call(functools.partial(step_kernel, d), out_shape=[jax.ShapeDty...  98.5 us
    pallas_call x1, Pallas kernels, local(): pl.pallas_call(update_kernel, out_shape=outs, in_specs=[far] * len(given)...  3.67 us

profile of v4, /device:TPU:0, one launch (start us, length us, event | category | flops | bytes accessed | tf_op | source)
XLA Modules:
  0.0 102.9 jit_solution(13818957634318756267)
XLA Ops:
  0.7 98.5 %shard_map.416 = (f32[64,208]{1,0:T(8,128)}, f32[2,64,512]{2,1,0:T(8,128)}, f32[3,2,256]{2,1,0:T(2,128)}, f32[12,8,128]{2,1,0:T(8,128)}, f32[8,128]{1,0:T(8,128)}) custom-call(f32[100,1,256]{2,1,0:T(1,128)} %bitcast.55, s32[256,2048]{1,0:T(8,128)} %bitcast.45, s32[1,256]{1,0:T(1,128)} %refs_2_.1, s32[1,256]{1,0:T(1,128)} %refs_3_.1, s32[1,256]{1,0:T(1,128)} %refs_4_.1, ...), custom_call_target="tpu_custom_call" | custom-call | tf_op jit(solution)/shard_map/pallas_call | solution.py:924
  99.2 3.7 %shard_map.417 = (f32[1,1]{1,0:T(1,128)}, f32[1,1]{1,0:T(1,128)}, f32[1,1]{1,0:T(1,128)}, f32[64,200]{1,0:T(8,128)}, f32[64,200]{1,0:T(8,128)}, /*index=5*/f32[6...) custom-call(f32[64,208]{1,0:T(8,128)} %get-tuple-element.51.refs_0_,, ...), custom_call_target="tpu_custom_call" | custom-call | tf_op jit(solution)/shard_map/pallas_call | solution.py:1016

commit v5 on v4

--- a/solution.py
+++ b/solution.py
@@ -113,14 +113,6 @@
                 other()
 
     barrier = pltpu.get_barrier_semaphore()
-
-    def greet(i, carry):
-        pl.semaphore_signal(
-            barrier, inc=1, device_id=device(lax.rem(me + i, NDEV)), device_id_type=MESH
-        )
-        return carry
-
-    lax.fori_loop(1, NDEV, greet, 0)
 
     def adj_cols(j, core):
         return v.adj.at[:, rows(j * 2 + core, R)]
@@ -142,13 +134,17 @@
     base = L - 1 + len(d.small)
     for j in range(CH):
         pltpu.make_async_copy(adj_cols(j, k), v.adjb.at[0, j], v.ld.at[base + j]).start()
-    for copy in small_loads:
-        copy.wait()
+    def greet(i, carry):
+        pl.semaphore_signal(
+            barrier, inc=1, device_id=device(lax.rem(me + i, NDEV)), device_id_type=MESH
+        )
+        return carry
+
+    lax.fori_loop(1, NDEV, greet, 0)
+
+    small_loads[0].wait()
     v.xown[:F, :] = v.feat_in[...]
     v.xown[F:, :] = jnp.ones((FR - F, R), F32)
-    v.wt0[own_rows, :] = jnp.zeros((HC, 2 * FR), F32)
-    v.wt0[own_rows, :F] = v.w0_in[:, :F]
-    v.wt0[own_rows, FR : FR + F] = v.w0_in[:, F:]
     pl.semaphore_wait(barrier, NDEV - 1)
 
     def halves(ref):
@@ -264,6 +260,11 @@
         for dd in range(1, NC):
             wait_bytes(w_half(l, NC - dd, 1 - k), v.r_wp.at[l, dd])
 
+    for copy in small_loads[1:]:
+        copy.wait()
+    v.wt0[own_rows, :] = jnp.zeros((HC, 2 * FR), F32)
+    v.wt0[own_rows, :F] = v.w0_in[:, :F]
+    v.wt0[own_rows, FR : FR + F] = v.w0_in[:, F:]
     w_send(0)
     for j in range(CH):
         send(adj_cols(j, 1 - k), v.adjb.at[1, j], v.s_adj.at[j], v.r_adj.at[j], sib)
@@ -676,19 +677,11 @@
             complete(2)
             send(y[1], from_y[1], s.at[3], r.at[3], peer(2))
             complete(0)
-            wait_bytes(via[0], r.at[0])
-            y[0][...] += via[0][...]
-            send(y[0], from_y[0], s.at[5], r.at[5], peer(2))
-            wait_bytes(via[1], r.at[1])
-            x[1][...] += via[1][...]
-            send(x[1], from_x[1], s.at[4], r.at[4], peer(1))
         else:
             for dd in reversed(range(1, CH)):
                 complete(dd)
                 send(v.out.at[dd], back.at[dd], s.at[dd], r.at[dd], peer(dd))
             complete(0)
-        scatter_drains, drains = drains, kept_drains
-
         v.gout[...] = dot3(gl, (v.wh[g, :, :H], v.wl[g, :, :H]))
         mean, inverse = v.vecs[g, 0:1, :], v.vecs[g, 1:2, :]
 
@@ -704,8 +697,16 @@
             )
 
         zero = jnp.zeros((8, H), F32)
-        ar_put(6 - l, [over_rows(s) for s in lax.fori_loop(0, R // RC, chunk, (zero, zero))])
-        ar_send(6 - l)
+        ar_put(6 - l, [over_rows(t) for t in lax.fori_loop(0, R // RC, chunk, (zero, zero))])
+        ar_send(6 - l, True)
+        if CH == 4:
+            wait_bytes(via[0], r.at[0])
+            y[0][...] += via[0][...]
+            send(y[0], from_y[0], s.at[5], r.at[5], peer(2))
+            wait_bytes(via[1], r.at[1])
+            x[1][...] += via[1][...]
+            send(x[1], from_x[1], s.at[4], r.at[4], peer(1))
+        scatter_drains, drains = drains, kept_drains
         grad = dot3(split(v.lin[...].T), (v.inh[g], v.inl[g]))
         for t in range(NC):
             for half in range(2):
@@ -950,27 +951,14 @@
     return (first, second, weight, average)
 
 
-ORDER = (1, 0, 3, 2, 4)
-
-
 def update_kernel(*refs):
-    far, scalars, far_out = refs[:25], refs[25:28], refs[28:48]
-    near, near_out, loaded, stored = refs[48:73], refs[73:93], refs[93], refs[94]
-    loads = [pltpu.make_async_copy(a, b, loaded.at[i]) for i, (a, b) in enumerate(zip(far, near, strict=True))]
-    stores = [pltpu.make_async_copy(a, b, stored.at[i]) for i, (a, b) in enumerate(zip(near_out, far_out, strict=True))]
-    loads[4].start()
-    for group in ORDER:
-        for i in ([] if group == 4 else [group]) + [5 + group + 5 * j for j in range(4)]:
-            loads[i].start()
-    loads[4].wait()
-    misc = near[4]
+    grads, state, scalars, results = refs[:5], refs[5:25], refs[25:28], refs[28:]
+    misc = grads[4]
     scale = misc[4:5, 0:1]
     for i in range(3):
         scalars[i][...] = misc[i : i + 1, 0:1]
-    for group in ORDER:
-        for i in ([] if group == 4 else [group]) + [5 + group + 5 * j for j in range(4)]:
-            loads[i].wait()
-        weight, first, second, average = (near[5 + group + 5 * j] for j in range(4))
+    for group in range(5):
+        weight, first, second, average = (state[group + 5 * j] for j in range(4))
         rate = RATE_SMALL if group in (2, 4) else RATE_MATRIX
         shape = weight.shape
         if group == 4:
@@ -978,20 +966,21 @@
         elif group == 3:
             wide = shape[1] // LANES
             grad = cat(
-                [cat([near[3][wide * i + j] for j in range(wide)], 1) for i in range(near[3].shape[0] // wide)], 0
+                [
+                    cat([grads[3][wide * i + j] for j in range(wide)], 1)
+                    for i in range(grads[3].shape[0] // wide)
+                ],
+                0,
             )[: shape[0]]
         elif group == 0:
             half = shape[1] // 2
-            at = near[0].shape[1] // 2
-            grad = cat([near[0][:, :half], near[0][:, at : at + half]], 1)
+            at = grads[0].shape[1] // 2
+            grad = cat([grads[0][:, :half], grads[0][:, at : at + half]], 1)
         else:
-            grad = near[group][...]
+            grad = grads[group][...]
         done = adamw(weight[...], first[...], second[...], average[...], grad * scale, rate)
-        for i, value in enumerate(done):
-            near_out[4 * group + i][...] = value
-            stores[4 * group + i].start()
-    for store in stores:
-        store.wait()
+        for ref, value in zip(results[4 * group : 4 * group + 4], done, strict=True):
+            ref[...] = value
 
 
 def local(
@@ -1011,16 +1000,7 @@
     )
     outs = [jax.ShapeDtypeStruct((1, 1), F32)] * 3
     outs += [jax.ShapeDtypeStruct(a.shape, F32) for a in state[:5] for _ in range(4)]
-    far = pl.BlockSpec(memory_space=pl.ANY)
-    given = [*grads, *state]
-    done = pl.pallas_call(
-        update_kernel,
-        out_shape=outs,
-        in_specs=[far] * len(given),
-        out_specs=[pl.BlockSpec(memory_space=pltpu.VMEM)] * 3 + [far] * (len(outs) - 3),
-        scratch_shapes=[pltpu.VMEM(a.shape, F32) for a in [*given, *outs[3:]]]
-        + [pltpu.SemaphoreType.DMA((25,)), pltpu.SemaphoreType.DMA((20,))],
-    )(*given)
+    done = pl.pallas_call(update_kernel, out_shape=outs)(*grads, *state)
     return (
         *(a.reshape(()) for a in done[:3]),
         *(back[i // 4](a) for i, a in enumerate(done[3:])),

time: 103 us -> 102 us (level)
  no operation moved by 1% of the time
where the time goes in v5:
time: 102 us
  Pallas kernels  101 us (99%)
    pallas_call x1, Pallas kernels, gradients(): pl.pallas_call(functools.partial(step_kernel, d), out_shape=[jax.ShapeDty...  97.9 us
    pallas_call x1, Pallas kernels, local(): done = pl.pallas_call(update_kernel, out_shape=outs)(*grads, *state)  3.1 us

profile of v5, /device:TPU:0, one launch (start us, length us, event | category | flops | bytes accessed | tf_op | source)
XLA Modules:
  0.0 101.6 jit_solution(14069201977111604589)
XLA Ops:
  0.7 97.9 %shard_map.416 = (f32[64,208]{1,0:T(8,128)}, f32[2,64,512]{2,1,0:T(8,128)}, f32[3,2,256]{2,1,0:T(2,128)}, f32[12,8,128]{2,1,0:T(8,128)}, f32[8,128]{1,0:T(8,128)}) custom-call(f32[100,1,256]{2,1,0:T(1,128)} %bitcast.55, s32[256,2048]{1,0:T(8,128)} %bitcast.45, s32[1,256]{1,0:T(1,128)} %refs_2_.1, s32[1,256]{1,0:T(1,128)} %refs_3_.1, s32[1,256]{1,0:T(1,128)} %refs_4_.1, ...), custom_call_target="tpu_custom_call" | custom-call | tf_op jit(solution)/shard_map/pallas_call | solution.py:925
  98.5 3.1 %shard_map.417 = (f32[1,1]{1,0:T(1,128)}, f32[1,1]{1,0:T(1,128)}, f32[1,1]{1,0:T(1,128)}, f32[64,200]{1,0:T(8,128)}, f32[64,200]{1,0:T(8,128)}, /*index=5*/f32[6...) custom-call(f32[64,208]{1,0:T(8,128)} %get-tuple-element.51.refs_0_,, ...), custom_call_target="tpu_custom_call" | custom-call | tf_op jit(solution)/shard_map/pallas_call | solution.py:1003

commit v6 on v5

--- a/solution.py
+++ b/solution.py
@@ -187,12 +187,12 @@
             wait_bytes(z[0], r.at[4])
             add(flip(ch, 3), 0, z[0])
             wait_bytes(z[1], r.at[5])
-            add(flip(ch, 3), 1, z[1])
+            add(flip(ch, 3), 1, z[1], True)
         else:
             for dd in range(1, CH):
                 wait_bytes(buf.at[flip(ch, dd)], r.at[dd])
                 for part in range(2):
-                    add(flip(ch, dd), part, halves(buf.at[flip(ch, dd)])[part])
+                    add(flip(ch, dd), part, halves(buf.at[flip(ch, dd)])[part], dd == CH - 1 and part == 1)
 
     def to_others(start, at_once=False):
         if at_once and NDEV <= 32:
@@ -364,7 +364,7 @@
         ar_put(l, [over_rows(sums[0][i] + sums[1][i]) for i in range(2)])
         ar_send(l, l == L - 1)
 
-    def add_first(chip, part, ref):
+    def add_first(chip, part, ref, last=False):
         high, low = split(ref[...])
         a = v.abf[chip]
         got = dot_t(cat([high, low], 1), cat([a, a], 1))
@@ -415,24 +415,32 @@
             (v.inh[l - 1, :, :H], v.inl[l - 1, :, :H]), (v.wh[l - 1, :, :H], v.wl[l - 1, :, :H])
         )
 
-        def add(chip, part, ref):
-            high, low = split(ref[...])
-            a = v.abf[chip, :, part * HALF : (part + 1) * HALF]
-            v.agg[...] += dot(cat([a, a], 1), cat([high, low], 0))
-
-        high, low = split(v.acts[l - 1])
-        a = v.abf[ch]
-        v.agg[...] = dot(cat([a, a], 1), cat([high, low], 0))
+        parts, partr = v.parts.at[l - 1], v.partr.at[l - 1]
+
+        def share(a, both, first=False):
+            for at, total in ((R, parts), (0, v.agg)):
+                got = dot(cat([a[at : at + R]] * 2, 1), both)
+                total[...] = got if first else total[...] + got
+                if at and a is v.last_columns:
+                    for part in range(2):
+                        send(
+                            halves(parts)[part], halves(partr)[part], v.s_sib.at[l, part],
+                            v.r_sib.at[l, part], sib,
+                        )
+
+        def add(chip, part, ref, last=False):
+            columns = v.abf[chip, :, part * HALF : (part + 1) * HALF]
+            v.last_columns = columns if last else None
+            share(columns, cat(list(split(ref[...])), 0))
+
+        v.last_columns = None
+        share(v.abf[ch], cat(list(split(v.acts[l - 1])), 0), True)
         ag_blocks(l, v.ag.at[l - 1], add)
-        parts, partr = halves(v.parts.at[l - 1]), halves(v.partr.at[l - 1])
-        for part in range(2):
-            parts[part][...] = v.agg[R + part * HALF : R + (part + 1) * HALF, :]
-            send(parts[part], partr[part], v.s_sib.at[l, part], v.r_sib.at[l, part], sib)
 
         def part_lin(part):
             r = slice(part * HALF, (part + 1) * HALF)
-            wait_bytes(partr[part], v.r_sib.at[l, part])
-            agg = v.agg[r, :] + partr[part][...]
+            wait_bytes(halves(partr)[part], v.r_sib.at[l, part])
+            agg = v.agg[r, :] + partr[r, :]
             v.kept[l - 1, r, :] = agg
             v.inh[l - 1, r, H:], v.inl[l - 1, r, H:] = split(
                 agg * wide(v.invdeg[r, :]) * scale + wide(v.linked[r, :]) * shift
@@ -647,17 +655,23 @@
         linear_grad(l, 5 - l)
         gl = (v.glh[...], v.gll[...])
         back = v.ag.at[2 - l]
-        v.spread[...] = dot3(gl, (v.wh[g, :, H:], v.wl[g, :, H:])) * wide(v.invdeg[...])
-        v.spreads[g] = v.spread[...]
-        send(v.spreads.at[g], v.spreadr.at[g], v.s_sib.at[L + g, 0], v.r_sib.at[L + g, 0], sib)
+        for part in range(2):
+            r = slice(part * HALF, (part + 1) * HALF)
+            spread = dot3((v.glh[r, :], v.gll[r, :]), (v.wh[g, :, H:], v.wl[g, :, H:]))
+            v.spreads[g, r, :] = spread * wide(v.invdeg[r, :])
+            send(
+                halves(v.spreads.at[g])[part], halves(v.spreadr.at[g])[part],
+                v.s_sib.at[L + g, part], v.r_sib.at[L + g, part], sib,
+            )
         if g == 0:
             for drain in scatter_drains:
                 drain()
-        own = cat(list(split(v.spread[...])), 0)
+        own = cat(list(split(v.spreads[g])), 0)
         for dd in reversed(range(CH)):
             t = v.at[0, flip(ch, dd)]
             v.out[dd] = dot(cat([t, t], 1), own)
-        wait_bytes(v.spreadr.at[g], v.r_sib.at[L + g, 0])
+        for part in range(2):
+            wait_bytes(halves(v.spreadr.at[g])[part], v.r_sib.at[L + g, part])
         other = cat(list(split(v.spreadr[g])), 0)
 
         def complete(dd):
@@ -687,7 +701,7 @@
 
         def chunk(i, carry):
             r = rows(i, RC)
-            self, spread, degree = v.gout[r, :], v.spread[r, :], wide(v.degree[r, :])
+            self, spread, degree = v.gout[r, :], v.spreads[g, r, :], wide(v.degree[r, :])
             normed = (v.acts[g, r, :] - mean) * inverse
             reached = (v.kept[g, r, :] - degree * mean) * inverse
             v.gout[r, :] = self + v.out[0, r, :]
@@ -851,7 +865,7 @@
         "aggt": pltpu.VMEM((FR, 2 * R), F32),
         "part0": pltpu.VMEM((FR, R), F32),
         "part0r": pltpu.VMEM((FR, R), F32),
-        "agg": pltpu.VMEM((2 * R, H), F32),
+        "agg": pltpu.VMEM((R, H), F32),
         "parts": pltpu.VMEM((L - 1, R, H), F32),
         "partr": pltpu.VMEM((L - 1, R, H), F32),
         "kept": pltpu.VMEM((L - 1, R, H), F32),
@@ -859,7 +873,6 @@
         "gout": pltpu.VMEM((R, H), F32),
         "glh": pltpu.VMEM((R, H), BF16),
         "gll": pltpu.VMEM((R, H), BF16),
-        "spread": pltpu.VMEM((R, H), F32),
         "spreads": pltpu.VMEM((L - 1, R, H), F32),
         "spreadr": pltpu.VMEM((L - 1, R, H), F32),
         "out": pltpu.VMEM((CH, R, H), F32),
@@ -920,6 +933,13 @@
         shape = (F, R) if name == "feat" else inputs[name].shape
         scratch[name + "_in"] = pltpu.VMEM(shape, inputs[name].dtype)
     ins = list(inputs)
+    room = 6 * 2**20
+    for ref in scratch.values():
+        if ref.memory_space == pltpu.VMEM:
+            size = jnp.dtype(ref.dtype).itemsize
+            for i, length in enumerate(reversed(ref.shape)):
+                size *= -(-length // LANES) * LANES if i == 0 else -(-length // 8) * 8 if i == 1 else length
+            room += size
     outs = ["g0", "gr", "gn", "gh", "misc"]
     d.names = ins + outs + list(scratch)
     return pl.pallas_call(
@@ -931,13 +951,13 @@
             jax.ShapeDtypeStruct((d.HT, 8, LANES), F32),
             jax.ShapeDtypeStruct((8, LANES), F32),
         ],
-        in_specs=[pl.BlockSpec(memory_space=pl.ANY)] * len(ins),
+        in_specs=[pl.BlockSpec(memory_space=pltpu.HBM)] * len(ins),
         out_specs=[pl.BlockSpec(memory_space=pl.ANY)] * len(outs),
         scratch_shapes=list(scratch.values()),
         compiler_params=pltpu.CompilerParams(
-            collective_id=0, has_side_effects=True, vmem_limit_bytes=60 * 2**20
+            collective_id=0, has_side_effects=True, vmem_limit_bytes=min(room, 60 * 2**20)
         ),
-    )(*inputs.values())
+    )(*(pltpu.with_memory_space_constraint(a, pltpu.HBM) for a in inputs.values()))
 
 
 def adamw(weight, first, second, average, grad, rate):
@@ -1000,6 +1020,8 @@
     )
     outs = [jax.ShapeDtypeStruct((1, 1), F32)] * 3
     outs += [jax.ShapeDtypeStruct(a.shape, F32) for a in state[:5] for _ in range(4)]
+    grads = [pltpu.with_memory_space_constraint(a, pltpu.VMEM) for a in grads]
+    state = [pltpu.with_memory_space_constraint(a, pltpu.HBM) for a in state]
     done = pl.pallas_call(update_kernel, out_shape=outs)(*grads, *state)
     return (
         *(a.reshape(()) for a in done[:3]),

time: 102 us -> 101 us (level)
  no operation moved by 1% of the time
where the time goes in v6:
time: 101 us
  Pallas kernels  100 us (99%)
    pallas_call x1, Pallas kernels, gradients(): pl.pallas_call(functools.partial(step_kernel, d), out_shape=[jax.ShapeDty...  97.3 us
    pallas_call x1, Pallas kernels, local(): done = pl.pallas_call(update_kernel, out_shape=outs)(*grads, *state)  3.01 us

profile of v6, /device:TPU:0, one launch (start us, length us, event | category | flops | bytes accessed | tf_op | source)
XLA Modules:
  0.0 100.9 jit_solution(5383820155144113734)
XLA Ops:
  0.7 97.3 %shard_map.416 = (f32[64,208]{1,0:T(8,128)S(1)}, f32[2,64,512]{2,1,0:T(8,128)S(1)}, f32[3,2,256]{2,1,0:T(2,128)S(1)}, f32[12,8,128]{2,1,0:T(8,128)S(1)}, f32[8,128]{1,0:T(8,128)S(1)}) custom-call(f32[100,1,256]{2,1,0:T(1,128)} %bitcast.55, s32[256,2048]{1,0:T(8,128)} %bitcast.45, s32[1,256]{1,0:T(1,128)} %refs_2_.1, s32[1,256]{1,0:T(1,128)} %refs_3_.1, ...), custom_call_target="tpu_custom_call" | custom-call | tf_op jit(solution)/shard_map/pallas_call | solution.py:945
  97.9 3.0 %shard_map.417 = (f32[1,1]{1,0:T(1,128)}, f32[1,1]{1,0:T(1,128)}, f32[1,1]{1,0:T(1,128)}, f32[64,200]{1,0:T(8,128)}, f32[64,200]{1,0:T(8,128)}, /*index=5*/f32[6...) custom-call(f32[64,208]{1,0:T(8,128)S(1)} %get-tuple-element.51.refs, ...), custom_call_target="tpu_custom_call" | custom-call | tf_op jit(solution)/shard_map/pallas_call | solution.py:1025

commit v7 on v6

--- a/solution.py
+++ b/solution.py
@@ -502,20 +502,22 @@
     def others(index, size, ref_of, init):
         return lax.fori_loop(1, size, lambda i, s: s + ref_of(lax.rem(index + i, size)), init)
 
-    def head_scatter(i, carry):
-        t = lax.rem(me + i, NDEV)
-
-        def go():
-            remote(v.hg.at[t], v.hrecv.at[me], v.s_h.at[0], v.r_h.at[0], device(t)).start()
-
-        either(HT == NDEV, t < HT, go)
-        return carry
-
-    lax.fori_loop(1, NDEV, head_scatter, 0)
+    owners = [t * NDEV // HT for t in range(HT)]
+    tile = lax.div(me * HT + NDEV - 1, NDEV)
+    adds_tile = jnp.logical_and(tile < HT, lax.div(tile * NDEV, HT) == me)
+    tile = jnp.minimum(tile, HT - 1)
+    for t, owner in enumerate(owners):
+
+        def go(t=t, owner=owner):
+            remote(
+                v.hg.at[t], v.hrecv.at[me], v.s_h.at[0], v.r_h.at[0], (owner // NC, owner % NC)
+            ).start()
+
+        either(False, me != owner, go)
     drains.append(
         lambda: either(
             HT == NDEV,
-            me < HT,
+            adds_tile,
             lambda: wait_bytes(v.hrecv.at[pl.ds(0, HT - 1)], v.s_h.at[0]),
             lambda: wait_bytes(v.hrecv.at[pl.ds(0, HT)], v.s_h.at[0]),
         )
@@ -524,22 +526,22 @@
     def head_gather():
         def go():
             wait_bytes(v.hrecv.at[pl.ds(0, NDEV - 1)], v.r_h.at[0])
-            v.hfin[me] = others(me, NDEV, lambda s: v.hrecv[s], v.hg[me])
+            v.hfin[tile] = others(me, NDEV, lambda s: v.hrecv[s], v.hg[tile])
 
             def one(i, carry):
                 remote(
-                    v.hfin.at[me], v.hfin.at[me], v.s_h.at[1], v.r_h.at[1],
+                    v.hfin.at[tile], v.hfin.at[tile], v.s_h.at[1], v.r_h.at[1],
                     device(lax.rem(me + i, NDEV)),
                 ).start()
                 return carry
 
             lax.fori_loop(1, NDEV, one, 0)
 
-        either(HT == NDEV, me < HT, go)
+        either(HT == NDEV, adds_tile, go)
         drains.append(
             lambda: either(
                 HT == NDEV,
-                me < HT,
+                adds_tile,
                 lambda: wait_bytes(v.hrecv.at[pl.ds(0, NDEV - 1)], v.s_h.at[1]),
             )
         )
@@ -713,6 +715,12 @@
         zero = jnp.zeros((8, H), F32)
         ar_put(6 - l, [over_rows(t) for t in lax.fori_loop(0, R // RC, chunk, (zero, zero))])
         ar_send(6 - l, True)
+        grad = dot3(split(v.lin[...].T), (v.inh[g], v.inl[g]))
+        for t in range(NC):
+            for half in range(2):
+                at = t * HC + half * (HC // 2)
+                v.dwb[g, half, t] = grad[at : at + HC // 2, :]
+        sibling_send(g)
         if CH == 4:
             wait_bytes(via[0], r.at[0])
             y[0][...] += via[0][...]
@@ -721,12 +729,6 @@
             x[1][...] += via[1][...]
             send(x[1], from_x[1], s.at[4], r.at[4], peer(1))
         scatter_drains, drains = drains, kept_drains
-        grad = dot3(split(v.lin[...].T), (v.inh[g], v.inl[g]))
-        for t in range(NC):
-            for half in range(2):
-                at = t * HC + half * (HC // 2)
-                v.dwb[g, half, t] = grad[at : at + HC // 2, :]
-        sibling_send(g)
         if l == 2:
             head_gather()
         else:
@@ -789,7 +791,7 @@
     v.misc_o[3:4, :] = bias_grad
     either(
         HT == NDEV,
-        me < HT,
+        adds_tile,
         lambda: wait_bytes(v.hfin.at[pl.ds(0, HT - 1)], v.r_h.at[1]),
         lambda: wait_bytes(v.hfin.at[pl.ds(0, HT)], v.r_h.at[1]),
     )

time: 101 us -> 99.9 us (0.989)
    pallas_call x1, Pallas kernels: 97.3 us -> 96.1 us  [gradients(): pl.pallas_call(functools.partial(step_kernel, d), out_shape=[jax.ShapeDty...]
where the time goes in v7:
time: 99.9 us; the launch traced here: 99.8 us
  Pallas kernels  99.1 us (99%)
    pallas_call x1, Pallas kernels, gradients(): pl.pallas_call(functools.partial(step_kernel, d), out_shape=[jax.ShapeDty...  96.1 us
    pallas_call x1, Pallas kernels, local(): done = pl.pallas_call(update_kernel, out_shape=outs)(*grads, *state)  3.01 us

profile of v7, /device:TPU:0, one launch (start us, length us, event | category | flops | bytes accessed | tf_op | source)
XLA Modules:
  0.0 99.8 jit_solution(3879004961574318973)
XLA Ops:
  0.7 96.1 %shard_map.416 = (f32[64,208]{1,0:T(8,128)S(1)}, f32[2,64,512]{2,1,0:T(8,128)S(1)}, f32[3,2,256]{2,1,0:T(2,128)S(1)}, f32[12,8,128]{2,1,0:T(8,128)S(1)}, f32[8,128]{1,0:T(8,128)S(1)}) custom-call(f32[100,1,256]{2,1,0:T(1,128)} %bitcast.55, s32[256,2048]{1,0:T(8,128)} %bitcast.45, s32[1,256]{1,0:T(1,128)} %refs_2_.1, s32[1,256]{1,0:T(1,128)} %refs_3_.1, ...), custom_call_target="tpu_custom_call" | custom-call | tf_op jit(solution)/shard_map/pallas_call | solution.py:947
  96.8 3.0 %shard_map.417 = (f32[1,1]{1,0:T(1,128)}, f32[1,1]{1,0:T(1,128)}, f32[1,1]{1,0:T(1,128)}, f32[64,200]{1,0:T(8,128)}, f32[64,200]{1,0:T(8,128)}, /*index=5*/f32[6...) custom-call(f32[64,208]{1,0:T(8,128)S(1)} %get-tuple-element.51.refs, ...), custom_call_target="tpu_custom_call" | custom-call | tf_op jit(solution)/shard_map/pallas_call | solution.py:1027

commit v8 on v7

--- a/solution.py
+++ b/solution.py
@@ -583,18 +583,27 @@
             )
         )
 
-    def pieces_out(i, fin, at, piece):
+    def pieces_out(i, fin, at, piece, away=True):
         mine = pl.ds(pl.multiple_of(at, RPP), RPP)
         fin[mine, :] = piece
         square = jnp.sum((piece * piece).reshape(RPP // 8, 8, piece.shape[1]), axis=0)
         v.sq[...] += jnp.sum(square, axis=1, keepdims=True)
 
+        if away:
+            pieces_away(i, fin, at)
+
+    def pieces_away(i, fin, at):
+        block = fin.at[pl.ds(pl.multiple_of(at, RPP), RPP), :]
+
         def one(j, carry):
-            block = fin.at[mine, :]
             remote(block, block, v.s_f.at[i], v.r_f.at[i], (lax.rem(n + j, NN), c)).start()
             return carry
 
-        lax.fori_loop(1, NN, one, 0)
+        if NN <= 8:
+            for j in range(1, NN):
+                one(j, 0)
+        else:
+            lax.fori_loop(1, NN, one, 0)
 
     def pieces_drain(i, fin):
         drains.append(
@@ -751,6 +760,9 @@
     for t in range(NC):
         v.d0[t] = grad[t * HC : (t + 1) * HC, :]
 
+    def own_piece():
+        v.recv0[me] = v.d0[c, rows(n, RPP), :]
+
     def first_scatter(dev, t):
         tn, tc = dev
         either(
@@ -762,6 +774,7 @@
         )
 
     to_others(first_scatter, True)
+    either(PPC == NN, n < PPC, own_piece)
     drains.append(
         lambda: either(
             PPC == NN,
@@ -775,13 +788,14 @@
 
     def first_gather():
         wait_bytes(v.recv0.at[pl.ds(0, NDEV - 1)], v.r_0.at[0])
-        piece = others(me, NDEV, lambda s: v.recv0[s], v.d0[c, rows(n, RPP), :])
-        pieces_out(L - 1, v.fin0, n * RPP, piece)
+        piece = jnp.sum(v.recv0[...], axis=0)
+        pieces_out(L - 1, v.fin0, n * RPP, piece, False)
 
     either(PPC == NN, n < PPC, first_gather)
     pieces_drain(L - 1, v.fin0)
     ar_put(7, [over_rows(v.sq[...])])
     ar_send(7, True)
+    either(PPC == NN, n < PPC, lambda: pieces_away(L - 1, v.fin0, n * RPP))
 
     total = ar_wait(6)
     bias_grad = total[1:2]

time: 99.9 us -> 99.7 us (level)
  no operation moved by 1% of the time
where the time goes in v8:
time: 99.7 us; the launch traced here: 99.5 us
  Pallas kernels  98.8 us (99%)
    pallas_call x1, Pallas kernels, gradients(): pl.pallas_call(functools.partial(step_kernel, d), out_shape=[jax.ShapeDty...  95.8 us
    pallas_call x1, Pallas kernels, local(): done = pl.pallas_call(update_kernel, out_shape=outs)(*grads, *state)  3.01 us

profile of v8, /device:TPU:0, one launch (start us, length us, event | category | flops | bytes accessed | tf_op | source)
XLA Modules:
  0.0 99.5 jit_solution(13589479571705966883)
XLA Ops:
  0.7 95.8 %shard_map.416 = (f32[64,208]{1,0:T(8,128)S(1)}, f32[2,64,512]{2,1,0:T(8,128)S(1)}, f32[3,2,256]{2,1,0:T(2,128)S(1)}, f32[12,8,128]{2,1,0:T(8,128)S(1)}, f32[8,128]{1,0:T(8,128)S(1)}) custom-call(f32[100,1,256]{2,1,0:T(1,128)} %bitcast.55, s32[256,2048]{1,0:T(8,128)} %bitcast.45, s32[1,256]{1,0:T(1,128)} %refs_2_.1, s32[1,256]{1,0:T(1,128)} %refs_3_.1, ...), custom_call_target="tpu_custom_call" | custom-call | tf_op jit(solution)/shard_map/pallas_call | solution.py:961
  96.5 3.0 %shard_map.417 = (f32[1,1]{1,0:T(1,128)}, f32[1,1]{1,0:T(1,128)}, f32[1,1]{1,0:T(1,128)}, f32[64,200]{1,0:T(8,128)}, f32[64,200]{1,0:T(8,128)}, /*index=5*/f32[6...) custom-call(f32[64,208]{1,0:T(8,128)S(1)} %get-tuple-element.51.refs, ...), custom_call_target="tpu_custom_call" | custom-call | tf_op jit(solution)/shard_map/pallas_call | solution.py:1041

commit v9 on v8

--- a/solution.py
+++ b/solution.py
@@ -500,6 +500,10 @@
         v.hg[t] = head_grad[8 * i : 8 * i + 8, j * LANES : (j + 1) * LANES]
 
     def others(index, size, ref_of, init):
+        if size <= 8:
+            for i in range(1, size):
+                init = init + ref_of(lax.rem(index + i, size))
+            return init
         return lax.fori_loop(1, size, lambda i, s: s + ref_of(lax.rem(index + i, size)), init)
 
     owners = [t * NDEV // HT for t in range(HT)]
@@ -573,7 +577,11 @@
             )
             return carry
 
-        lax.fori_loop(1, CH, one, 0)
+        if CH <= 8:
+            for j in range(1, CH):
+                one(j, 0)
+        else:
+            lax.fori_loop(1, CH, one, 0)
         drains.append(
             lambda: either(
                 PH == CH,

time: 99.7 us -> 99.6 us (level)
  no operation moved by 1% of the time
where the time goes in v9:
time: 99.6 us; the launch traced here: 99.5 us
  Pallas kernels  98.8 us (99%)
    pallas_call x1, Pallas kernels, gradients(): pl.pallas_call(functools.partial(step_kernel, d), out_shape=[jax.ShapeDty...  95.8 us
    pallas_call x1, Pallas kernels, local(): done = pl.pallas_call(update_kernel, out_shape=outs)(*grads, *state)  3.01 us

profile of v9, /device:TPU:0, one launch (start us, length us, event | category | flops | bytes accessed | tf_op | source)
XLA Modules:
  0.0 99.5 jit_solution(6394458297547216595)
XLA Ops:
  0.7 95.8 %shard_map.416 = (f32[64,208]{1,0:T(8,128)S(1)}, f32[2,64,512]{2,1,0:T(8,128)S(1)}, f32[3,2,256]{2,1,0:T(2,128)S(1)}, f32[12,8,128]{2,1,0:T(8,128)S(1)}, f32[8,128]{1,0:T(8,128)S(1)}) custom-call(f32[100,1,256]{2,1,0:T(1,128)} %bitcast.55, s32[256,2048]{1,0:T(8,128)} %bitcast.45, s32[1,256]{1,0:T(1,128)} %refs_2_.1, s32[1,256]{1,0:T(1,128)} %refs_3_.1, ...), custom_call_target="tpu_custom_call" | custom-call | tf_op jit(solution)/shard_map/pallas_call | solution.py:969
  96.5 3.0 %shard_map.417 = (f32[1,1]{1,0:T(1,128)}, f32[1,1]{1,0:T(1,128)}, f32[1,1]{1,0:T(1,128)}, f32[64,200]{1,0:T(8,128)}, f32[64,200]{1,0:T(8,128)}, /*index=5*/f32[6...) custom-call(f32[64,208]{1,0:T(8,128)S(1)} %get-tuple-element.51.refs, ...), custom_call_target="tpu_custom_call" | custom-call | tf_op jit(solution)/shard_map/pallas_call | solution.py:1049
